TPU v7x, 32 devices: a whole 2x2x4 slice. The times are simulated.
32 devices in a mesh: groups: 1, expert: 32 (over z, y, x, core).
Axes of the slice: x: 2, y: 2, z: 4, core: 2. Of those that a mesh axis runs over, the one named last changes fastest.
Arguments:
- tokens: bfloat16 [1024, 6144], P(('groups', 'expert')), may hold values from -6 to 6
- routes: int32 [4096, 2], P(('groups', 'expert')), may hold values from 0 to 7, all different within a row; in each aligned block of 128 rows (0 to 127, 128 to 255, ...) at most 48 rows name the same one
- gates: float32 [4096, 2], P(('groups', 'expert')), may hold values from 0.1 to 1
- w_up: bfloat16 [32, 1536, 512], P('expert'), may hold values from -0.15625 to 0.15625
- w_down: bfloat16 [32, 512, 1536], P('expert'), may hold values from -0.125 to 0.125
- cotangent: bfloat16 [1024, 6144], P(('groups', 'expert')), may hold values from -6 to 6
Outputs:
- mixed: bfloat16 [1024, 6144], P(('groups', 'expert'))
- d_tokens: bfloat16 [1024, 6144], P(('groups', 'expert'))
- d_up: float32 [32, 1536, 512], P(('groups', 'expert'))
- d_down: float32 [32, 512, 1536], P(('groups', 'expert'))
Inputs may be any that keep to these rules, and one draw needn't show every extreme that they name: `routes`: the two experts of a row differ; in the rows of one device (aligned blocks of 128 rows) no expert is named more than 48 times, a bound that some block reaches.
All inputs are finite; a program needn't handle non-finite values.
Results may differ from a plain program's by a relative error of at most 0.0072.
Values may be sent and summed in bfloat16 or wider, within the bound.
No kernel may reach another device: no remote copies, remote signals or barrier semaphores. Data moves between devices by JAX's collectives and lax.ppermute only.
A program may use at most 128 MiB of HBM per device.

v0:
```python
import jax
import jax.numpy as jnp
from jax import lax
from jax.sharding import PartitionSpec as P

HEADS = 4
SPLIT = 4


def silu_grad(values):
    gate_sig = jax.nn.sigmoid(values)
    return gate_sig * (1.0 + values * (1.0 - gate_sig))


def send_rows(buffer, experts_all, capacity):
    feature = buffer.shape[1]
    copies = jnp.repeat(buffer.reshape(experts_all, 1, capacity, feature), SPLIT, axis=1).reshape(
        experts_all * SPLIT, capacity, feature
    )
    arrived = lax.all_to_all(copies, "expert", split_axis=0, concat_axis=0, tiled=True)
    return arrived.reshape(-1, feature)


def bring_back(partial_value, experts_all, capacity):
    feature = partial_value.shape[2]
    returned = lax.all_to_all(partial_value, "expert", split_axis=0, concat_axis=0, tiled=True)
    summed = jnp.sum(
        returned.reshape(experts_all, SPLIT, capacity, feature).astype(jnp.float32), axis=1
    )
    return summed.astype(jnp.bfloat16).reshape(experts_all * capacity, feature)


def on_device(tokens, routes, gates, w_up, w_down, cotangent):
    feature = w_up.shape[1]
    devices = lax.axis_size("expert")
    experts_all = devices // SPLIT
    tok_local = tokens.shape[0]
    capacity = SPLIT * (
        (6 * HEADS * tok_local + 2 * experts_all * SPLIT - 1) // (2 * experts_all * SPLIT)
    )
    sub_rows = tokens.reshape(-1, feature)
    grad_rows = cotangent.reshape(-1, feature)
    expert_ids = routes.reshape(-1)
    weights_flat = gates.reshape(-1)
    assigned = expert_ids.shape[0]
    onehot = (expert_ids[:, None] == jnp.arange(experts_all, dtype=jnp.int32)[None, :]).astype(
        jnp.int32
    )
    slot_rank = jnp.cumsum(onehot, axis=0) - 1
    slot_of = jnp.sum(slot_rank * onehot, axis=1)
    target = expert_ids * capacity + slot_of
    slot_total = experts_all * capacity
    matches = jnp.arange(slot_total, dtype=jnp.int32)[:, None] == target[None, :]
    filled = jnp.any(matches, axis=1)
    owner_index = jnp.sum(
        jnp.where(matches, jnp.arange(assigned, dtype=jnp.int32)[None, :], 0), axis=1
    )
    source_row = owner_index // 2
    inputs = jnp.where(
        filled[:, None], jnp.take(sub_rows, source_row, axis=0), jnp.zeros((), jnp.bfloat16)
    )
    gate_owner = jnp.where(filled, jnp.take(weights_flat, owner_index), 0.0)
    scaled = (
        gate_owner[:, None] * jnp.take(grad_rows, source_row, axis=0).astype(jnp.float32)
    ).astype(jnp.bfloat16)
    rows_in = send_rows(inputs, experts_all, capacity)
    up_local = w_up[0]
    down_local = w_down[0]
    pre_act = jnp.dot(rows_in, up_local, preferred_element_type=jnp.float32)
    hidden = jax.nn.silu(pre_act).astype(jnp.bfloat16)
    partial_value = (
        jnp.dot(hidden, down_local, preferred_element_type=jnp.float32)
        .astype(jnp.bfloat16)
        .reshape(devices, capacity, feature)
    )
    expert_out = bring_back(partial_value, experts_all, capacity)
    pair_targets = target.reshape(-1, 2)
    picked = jnp.take(expert_out, pair_targets, axis=0).astype(jnp.float32)
    layer_out = (
        jnp.sum(gates[:, :, None] * picked, axis=1).astype(jnp.bfloat16).reshape(tokens.shape)
    )
    grad_out = send_rows(scaled, experts_all, capacity)
    grad_hidden = lax.dot_general(
        grad_out, down_local, (((1,), (1,)), ((), ())), preferred_element_type=jnp.float32
    )
    grad_pre = (grad_hidden * silu_grad(pre_act)).astype(jnp.bfloat16)
    grad_down = lax.dot_general(
        hidden, grad_out, (((0,), (0,)), ((), ())), preferred_element_type=jnp.float32
    )
    grad_up = lax.dot_general(
        rows_in, grad_pre, (((0,), (0,)), ((), ())), preferred_element_type=jnp.float32
    )
    back_part = (
        lax.dot_general(
            grad_pre, up_local, (((1,), (1,)), ((), ())), preferred_element_type=jnp.float32
        )
        .astype(jnp.bfloat16)
        .reshape(devices, capacity, feature)
    )
    grad_sub = bring_back(back_part, experts_all, capacity)
    token_grad = (
        jnp.sum(jnp.take(grad_sub, pair_targets, axis=0).astype(jnp.float32), axis=1)
        .astype(jnp.bfloat16)
        .reshape(tokens.shape)
    )
    return (layer_out, token_grad, grad_up[None], grad_down[None])


def solution(mesh):
    placed = (
        P(("groups", "expert"), None),
        P(("groups", "expert"), None),
        P(("groups", "expert"), None),
        P("expert", None, None),
        P("expert", None, None),
        P(("groups", "expert"), None),
    )
    return jax.shard_map(
        on_device,
        mesh=mesh,
        in_specs=placed,
        out_specs=(
            P(("groups", "expert"), None),
            P(("groups", "expert"), None),
            P(("groups", "expert"), None, None),
            P(("groups", "expert"), None, None),
        ),
        check_vma=False,
    )
```

profile of v0, /device:TPU:0, one launch (start us, length us, event | category | flops | bytes accessed | tf_op | source)
XLA Modules:
  0.0 462.1 jit_solution(15001745420091850762)
XLA Ops:
  0.6 0.9 copy.26
  3.1 1.3 reshape.132
  4.4 2.2 gather_fusion.1
  6.9 2.7 broadcast_in_dim.75
  9.6 7.4 %all-to-all-start = ((bf16[32,48,1536]{2,1,0:T(8,128)(2,1)}), bf16[32,48,1536]{2,1,0:T(8,128)(2,1)}, u32[]{:S(2)}, u32[]{:S(2)}) async-start(bf16[32,48,1536]{2,1,0:T(8,128)(2,1)} %bitcast.42), calls=%async_computation | async-start | bytes 9437184 | tf_op jit(solution)/shard_map/all_to_all | solution.py:20
  18.2 2.2 gather_fusion.3
  20.5 2.8 gather_fusion
  23.3 1.4 multiply_convert_fusion.1
  24.6 97.7 %all-to-all-done = bf16[32,48,1536]{2,1,0:T(8,128)(2,1)} async-done(((bf16[32,48,1536]{2,1,0:T(8,128)(2,1)}), bf16[32,48,1536]{2,1,0:T(8,128)(2,1)}, u32[]{:S(2)}, u32[]{:S(2)}) %all-to-all-start) | async-done | bytes 4718624 | tf_op jit(solution)/shard_map/all_to_all | solution.py:20
  122.3 4.0 broadcast_in_dim.78
  126.3 3.9 all-to-all-start.2
  130.2 4.4 fusion.4
  134.7 1.7 copy-done.6
  136.4 4.3 convolution_convert_fusion.1
  140.7 94.9 %all-to-all-done.2 = bf16[32,48,1536]{2,1,0:T(8,128)(2,1)} async-done(((bf16[32,48,1536]{2,1,0:T(8,128)(2,1)}), bf16[32,48,1536]{2,1,0:T(8,128)(2,1)}, u32[]{:S(2)}, u32[]{:S(2)}) %all-to-all-start.2) | async-done | bytes 4718624 | tf_op jit(solution)/shard_map/all_to_all | solution.py:20
  235.5 3.9 all-to-all-start.1
  239.4 6.1 %fusion = bf16[1536,512]{1,0:T(8,128)(2,1)S(1)} fusion(f32[1536,512]{1,0:T(8,128)} %copy-done.6, bf16[1536,1536]{1,0:T(8,128)(2,1)} %bitcast.12, bf16[1,512,1536]{2,1,0:T(8,128)(2,1)S(1)} %copy-done), kind=kOutput, calls=%fused_computation.14 | convolution fusion | flops 2422996992 | bytes 11010048 | tf_op jit(solution)/shard_map/dot_general | solution.py:83
  245.5 1.1 copy-done.8
  246.6 4.4 convolution_convert_fusion
  251.0 93.7 %all-to-all-done.1 = bf16[32,48,1536]{2,1,0:T(8,128)(2,1)} async-done(((bf16[32,48,1536]{2,1,0:T(8,128)(2,1)}), bf16[32,48,1536]{2,1,0:T(8,128)(2,1)}, u32[]{:S(2)}, u32[]{:S(2)}) %all-to-all-start.1) | async-done | bytes 4718624 | tf_op jit(solution)/shard_map/all_to_all | solution.py:26
  344.7 4.1 all-to-all-start.3
  350.0 7.3 %convolution_bitcast_fusion.1 = f32[1,1536,512]{2,1,0:T(8,128)} fusion(bf16[1536,1536]{1,0:T(8,128)(2,1)} %bitcast.4, bf16[1536,512]{1,0:T(8,128)(2,1)} %copy-done.8), kind=kOutput, calls=%fused_computation.11 | convolution fusion | flops 2415919104 | bytes 9437184 | tf_op jit(solution)/shard_map/dot_general | solution.py:90
  357.3 6.8 %convolution_bitcast_fusion = f32[1,512,1536]{2,1,0:T(8,128)} fusion(bf16[1536,1536]{1,0:T(8,128)(2,1)} %bitcast.12, f32[1536,512]{1,0:T(8,128)S(1)} %copy-done.7), kind=kOutput, calls=%fused_computation.10 | convolution fusion | flops 2419851264 | bytes 11010048 | tf_op jit(solution)/shard_map/dot_general | solution.py:87
  364.1 3.0 bitcast_reduce_fusion.1
  367.1 1.3 gather_fusion.2
  368.7 4.1 multiply_reduce_fusion
  372.9 1.0 convert_element_type.44
  373.9 80.2 %all-to-all-done.3 = bf16[32,48,1536]{2,1,0:T(8,128)(2,1)} async-done(((bf16[32,48,1536]{2,1,0:T(8,128)(2,1)}), bf16[32,48,1536]{2,1,0:T(8,128)(2,1)}, u32[]{:S(2)}, u32[]{:S(2)}) %all-to-all-start.3) | async-done | bytes 4718624 | tf_op jit(solution)/shard_map/all_to_all | solution.py:26
  454.0 3.0 bitcast_reduce_fusion
  457.1 1.3 gather_fusion.4
  458.6 2.5 fusion.6
  461.1 1.0 reshape.145
  (45 shorter events, 4.8 us)
Async XLA Ops:
  0.6 135.7 %copy-start = (bf16[1,512,1536]{2,1,0:T(8,128)(2,1)S(1)}, bf16[1,512,1536]{2,1,0:T(8,128)(2,1)}, u32[]{:S(2)}) copy-start(bf16[1,512,1536]{2,1,0:T(8,128)(2,1)} %param.14) | copy-start | bytes 4718596
  9.6 7.4 %copy-start.4 = (f32[128,2]{0,1:T(2,128)S(1)}, f32[128,2]{0,1:T(2,128)}, u32[]{:S(2)}) copy-start(f32[128,2]{0,1:T(2,128)} %param.12) | copy-start | bytes 3076
  9.6 8.3 %copy-start.2 = (bf16[32,6144]{1,0:T(8,128)(2,1)S(1)}, bf16[32,6144]{1,0:T(8,128)(2,1)}, u32[]{:S(2)}) copy-start(bf16[32,6144]{1,0:T(8,128)(2,1)} %param.15) | copy-start | bytes 1179652
  9.6 112.7 %all-to-all-start = ((bf16[32,48,1536]{2,1,0:T(8,128)(2,1)}), bf16[32,48,1536]{2,1,0:T(8,128)(2,1)}, u32[]{:S(2)}, u32[]{:S(2)}) async-start(bf16[32,48,1536]{2,1,0:T(8,128)(2,1)} %bitcast.42), calls=%async_computation | async-start | bytes 9437184 | tf_op jit(solution)/shard_map/all_to_all | solution.py:20
  17.1 0.6 copy-start.1
  126.3 3.9 copy-start.5
  126.3 109.2 %all-to-all-start.2 = ((bf16[32,48,1536]{2,1,0:T(8,128)(2,1)}), bf16[32,48,1536]{2,1,0:T(8,128)(2,1)}, u32[]{:S(2)}, u32[]{:S(2)}) async-start(bf16[32,48,1536]{2,1,0:T(8,128)(2,1)} %bitcast.43), calls=%async_computation.2 | async-start | bytes 9437184 | tf_op jit(solution)/shard_map/all_to_all | solution.py:20
  134.7 1.7 copy-start.6
  235.5 109.2 %all-to-all-start.1 = ((bf16[32,48,1536]{2,1,0:T(8,128)(2,1)}), bf16[32,48,1536]{2,1,0:T(8,128)(2,1)}, u32[]{:S(2)}, u32[]{:S(2)}) async-start(bf16[32,48,1536]{2,1,0:T(8,128)(2,1)} %bitcast.45), calls=%async_computation.1 | async-start | bytes 9437184 | tf_op jit(solution)/shard_map/all_to_all | solution.py:26
  245.5 1.2 copy-start.8
  344.7 4.3 copy-start.3
  344.7 109.3 %all-to-all-start.3 = ((bf16[32,48,1536]{2,1,0:T(8,128)(2,1)}), bf16[32,48,1536]{2,1,0:T(8,128)(2,1)}, u32[]{:S(2)}, u32[]{:S(2)}) async-start(bf16[32,48,1536]{2,1,0:T(8,128)(2,1)} %bitcast.44), calls=%async_computation.3 | async-start | bytes 9437184 | tf_op jit(solution)/shard_map/all_to_all | solution.py:26
  350.0 7.3 %copy-start.7 = (f32[1536,512]{1,0:T(8,128)S(1)}, f32[1536,512]{1,0:T(8,128)}, u32[]{:S(2)}) copy-start(f32[1536,512]{1,0:T(8,128)} %copy-done.6) | copy-start | bytes 9437188
where the time goes:
time: 463 us; the launch traced here: 462 us
  waiting for transfers between devices  366 us (79%)
  matrix products  33.3 us (7%)
  local copies, waits for them, and re-layouts  27 us (6%)
  starting transfers between devices  19.2 us (4%)
  other arithmetic  15.4 us (3%)
    all_to_all x2, waiting for transfers between devices, send_rows(): lax.all_to_all(copies, 'expert', split_axis=0, concat_axis=0, tiled=True)  193 us
    all_to_all x2, waiting for transfers between devices, bring_back(): lax.all_to_all(partial_value, 'expert', split_axis=0, concat_axis=0, tile...  174 us
    all_to_all x2, starting transfers between devices, send_rows(): lax.all_to_all(copies, 'expert', split_axis=0, concat_axis=0, tiled=True)  11.3 us
  transfers between devices with their start and end apart: 4, of which 4 were waited for; matrix products, arithmetic and copies ran while one was open for 11% of the time, Pallas kernels for 0%

commit v1 on v0

v1 whole, which is shorter than its diff:
```python
import functools
import jax
import jax.numpy as jnp
from jax import lax
from jax.experimental import pallas as pl
from jax.experimental.pallas import tpu as pltpu
from jax.sharding import PartitionSpec as P

HEADS = 4
SPLIT = 4
VMEM = 48 * 1024 * 1024


def swap(value, bits):
    count = lax.axis_size("expert")
    return lax.ppermute(value, "expert", [(i, i ^ bits) for i in range(count)])


def silu_grad(values):
    gate_sig = jax.nn.sigmoid(values)
    return gate_sig * (1.0 + values * (1.0 - gate_sig))


def heads_of(index, per_head):
    head = jnp.zeros_like(index)
    for h in range(1, HEADS):
        head = head + (index >= h * per_head).astype(jnp.int32)
    return head


def natural(index, per_head):
    head = heads_of(index, per_head)
    return HEADS * (index - per_head * head) + head


def iota(shape, dim):
    return lax.broadcasted_iota(jnp.int32, shape, dim)


def by_head(pair_rows):
    rows = pair_rows.shape[1]
    place = natural(iota((rows, rows), 1), rows // HEADS)
    turn = (iota((rows, rows), 0) == place).astype(jnp.float32)
    return jnp.dot(
        pair_rows, turn, preferred_element_type=jnp.float32, precision=lax.Precision.HIGHEST
    )


def positions(me_ref, routes_ref, experts_all, capacity):
    rows = routes_ref.shape[1]
    routes = by_head(routes_ref[...].astype(jnp.float32)).astype(jnp.int32)
    first, second = routes[0:1], routes[1:2]
    expert = iota((experts_all, rows), 0)
    named = ((expert == first) | (expert == second)).astype(jnp.bfloat16)
    earlier = (
        natural(iota((rows, rows), 0), rows // HEADS)
        < natural(iota((rows, rows), 1), rows // HEADS)
    ).astype(jnp.bfloat16)
    rank = jnp.dot(named, earlier, preferred_element_type=jnp.float32).astype(jnp.int32)
    where_to = (expert ^ me_ref[0]) * capacity + rank
    return tuple(
        jnp.sum(jnp.where(expert == which, where_to, 0), axis=0, keepdims=True)
        for which in (first, second)
    )


def stacked(tokens_ref):
    feature = tokens_ref.shape[1] // HEADS
    return jnp.concatenate(
        [tokens_ref[:, h * feature : (h + 1) * feature] for h in range(HEADS)], axis=0
    )


def place_kernel(experts_all, capacity, gated, me_ref, routes_ref, gates_ref, tokens_ref, *blocks):
    rows = routes_ref.shape[1]
    first, second = positions(me_ref, routes_ref, experts_all, capacity)
    slot = iota((experts_all * capacity, rows), 0)
    at_first, at_second = slot == first, slot == second
    pick = (at_first | at_second).astype(jnp.bfloat16)
    placed = jnp.dot(pick, stacked(tokens_ref), preferred_element_type=jnp.float32)
    if gated:
        gates = by_head(gates_ref[...])
        weight = jnp.sum(
            jnp.where(at_first, gates[0:1], 0.0) + jnp.where(at_second, gates[1:2], 0.0),
            axis=1,
            keepdims=True,
        )
        placed = weight * placed
    placed = placed.astype(jnp.bfloat16)
    for m, block in enumerate(blocks):
        block[...] = placed[m * capacity : (m + 1) * capacity]


def column(row):
    count = row.shape[1]
    return jnp.sum(
        jnp.where(iota((count, count), 0) == iota((count, count), 1), row, jnp.zeros((), row.dtype)),
        axis=1,
        keepdims=True,
    )


def collect_kernel(experts_all, capacity, gated, me_ref, routes_ref, gates_ref, *refs):
    blocks, out_ref = refs[:-1], refs[-1]
    rows = routes_ref.shape[1]
    feature = out_ref.shape[1] // HEADS
    first, second = (column(t) for t in positions(me_ref, routes_ref, experts_all, capacity))
    values = jnp.concatenate([block[...] for block in blocks], axis=0)
    slot = iota((rows, experts_all * capacity), 1)
    at_first, at_second = slot == first, slot == second
    if gated:
        gates = by_head(gates_ref[...])
        total = column(gates[0:1]) * jnp.dot(
            at_first.astype(jnp.bfloat16), values, preferred_element_type=jnp.float32
        ) + column(gates[1:2]) * jnp.dot(
            at_second.astype(jnp.bfloat16), values, preferred_element_type=jnp.float32
        )
    else:
        total = jnp.dot(
            (at_first | at_second).astype(jnp.bfloat16), values, preferred_element_type=jnp.float32
        )
    total = total.astype(jnp.bfloat16)
    per_head = rows // HEADS
    for h in range(HEADS):
        out_ref[:, h * feature : (h + 1) * feature] = total[h * per_head : (h + 1) * per_head]


def place(me, routes, gates, tokens, experts_all, capacity, gated):
    feature = tokens.shape[1] // HEADS
    vmem = pl.BlockSpec(memory_space=pltpu.VMEM)
    block = jax.ShapeDtypeStruct((capacity, feature), jnp.bfloat16)
    return pl.pallas_call(
        functools.partial(place_kernel, experts_all, capacity, gated),
        out_shape=[block] * experts_all,
        in_specs=[pl.BlockSpec(memory_space=pltpu.SMEM), vmem, vmem, vmem],
        out_specs=[vmem] * experts_all,
        compiler_params=pltpu.CompilerParams(vmem_limit_bytes=VMEM),
    )(me, routes, gates, tokens)


def collect(me, routes, gates, blocks, tok_local, experts_all, capacity, gated):
    feature = blocks[0].shape[1]
    vmem = pl.BlockSpec(memory_space=pltpu.VMEM)
    return pl.pallas_call(
        functools.partial(collect_kernel, experts_all, capacity, gated),
        out_shape=jax.ShapeDtypeStruct((tok_local, HEADS * feature), jnp.bfloat16),
        in_specs=[pl.BlockSpec(memory_space=pltpu.SMEM)] + [vmem] * (2 + experts_all),
        out_specs=vmem,
        compiler_params=pltpu.CompilerParams(vmem_limit_bytes=VMEM),
    )(me, routes, gates, *blocks)


def spread(blocks, groups):
    sent = []
    for group in groups:
        mine = jnp.concatenate([swap(blocks[m], SPLIT * m) if m else blocks[m] for m in group])
        sent.append((mine, swap(mine, 2)))
    return [jnp.concatenate(pair) for pair in sent]


def bring_back(partials, groups, capacity):
    back = {}
    for group, partial in zip(groups, partials):
        half = len(group) * capacity
        total = (
            partial[:half].astype(jnp.float32) + swap(partial[half:], 2).astype(jnp.float32)
        ).astype(jnp.bfloat16)
        for i, m in enumerate(group):
            block = total[i * capacity : (i + 1) * capacity]
            back[m] = swap(block, SPLIT * m) if m else block
    return [back[m] for m in sorted(back)]


def dot(a, b, dims):
    return lax.dot_general(a, b, (dims, ((), ())), preferred_element_type=jnp.float32)


def on_device(tokens, routes, gates, w_up, w_down, cotangent):
    devices = lax.axis_size("expert")
    experts_all = devices // SPLIT
    tok_local = tokens.shape[0]
    capacity = SPLIT * (
        (6 * HEADS * tok_local + 2 * experts_all * SPLIT - 1) // (2 * experts_all * SPLIT)
    )
    capacity = 16 * ((capacity + 15) // 16)
    me = (lax.axis_index("expert") // SPLIT).astype(jnp.int32).reshape(1)
    routes, gates = routes.T, gates.T
    groups = [list(range(0, experts_all, 2)), list(range(1, experts_all, 2))]

    x_blocks = place(me, routes, gates, tokens, experts_all, capacity, False)
    g_blocks = place(me, routes, gates, cotangent, experts_all, capacity, True)
    up_own, down_own = w_up[0], w_down[0]
    block_hidden = up_own.shape[1]
    up = jnp.concatenate([up_own, swap(up_own, 1)], axis=1)
    down = jnp.concatenate([down_own, swap(down_own, 1)], axis=0)

    rows_in = spread(x_blocks, groups)
    pre_act = [dot(rows, up, ((1,), (0,))) for rows in rows_in]
    hidden = [jax.nn.silu(pre).astype(jnp.bfloat16) for pre in pre_act]
    partial = [dot(hid, down, ((1,), (0,))).astype(jnp.bfloat16) for hid in hidden]
    outs = bring_back(partial, groups, capacity)
    mixed = collect(me, routes, gates, outs, tok_local, experts_all, capacity, True)

    grads_in = spread(g_blocks, groups)
    grad_pre = [
        (dot(grad, down, ((1,), (1,))) * silu_grad(pre)).astype(jnp.bfloat16)
        for grad, pre in zip(grads_in, pre_act)
    ]
    back = [dot(grad, up, ((1,), (1,))).astype(jnp.bfloat16) for grad in grad_pre]
    backs = bring_back(back, groups, capacity)
    token_grad = collect(me, routes, gates, backs, tok_local, experts_all, capacity, False)

    x_all, g_all = jnp.concatenate(rows_in), jnp.concatenate(grads_in)
    hid_all, pre_all = jnp.concatenate(hidden), jnp.concatenate(grad_pre)
    x_other, g_other = swap(x_all, 1), swap(g_all, 1)
    hid_other = swap(hid_all[:, block_hidden:], 1)
    pre_other = swap(pre_all[:, block_hidden:], 1)
    grad_down = dot(hid_all[:, :block_hidden], g_all, ((0,), (0,))) + dot(
        hid_other, g_other, ((0,), (0,))
    )
    grad_up = dot(x_all, pre_all[:, :block_hidden], ((0,), (0,))) + dot(
        x_other, pre_other, ((0,), (0,))
    )
    return (mixed, token_grad, grad_up[None], grad_down[None])


def solution(mesh):
    placed = (
        P(("groups", "expert"), None),
        P(("groups", "expert"), None),
        P(("groups", "expert"), None),
        P("expert", None, None),
        P("expert", None, None),
        P(("groups", "expert"), None),
    )
    return jax.shard_map(
        on_device,
        mesh=mesh,
        in_specs=placed,
        out_specs=(
            P(("groups", "expert"), None),
            P(("groups", "expert"), None),
            P(("groups", "expert"), None, None),
            P(("groups", "expert"), None, None),
        ),
        check_vma=False,
    )
```

time: 463 us -> 235 us (0.51)
  waiting for transfers between devices: 366 us -> 139 us
  starting transfers between devices: 19.2 us -> 60.7 us
  local copies, waits for them, and re-layouts: 27 us -> 4.33 us
  other arithmetic: 15.4 us -> 0.86 us
  matrix products: 33.3 us -> 23 us
  Pallas kernels: 0 us -> 5.26 us
    all_to_all x4 -> x0, waiting for transfers between devices: 366 us -> none  [the longest x2 193 us: send_rows(): lax.all_to_all(copies, 'expert', split_axis=0, concat_axis=0, tiled=True)]
    ppermute x0 -> x42, waiting for transfers between devices: none -> 139 us  [swap(): return lax.ppermute(value, 'expert', [(i, i ^ bits) for i in range(count)])]
    ppermute x0 -> x42, starting transfers between devices: none -> 60.7 us  [swap(): return lax.ppermute(value, 'expert', [(i, i ^ bits) for i in range(count)])]
    all_to_all x4 -> x0, starting transfers between devices: 19.2 us -> none  [the longest x2 11.3 us: send_rows(): lax.all_to_all(copies, 'expert', split_axis=0, concat_axis=0, tiled=True)]
    reduce_sum x6 -> x0, other arithmetic: 12.9 us -> none  [the longest x2 6.05 us: bring_back(): jnp.sum(returned.reshape(experts_all, SPLIT, capacity, feature).astype(jn...]
    gather x7 -> x0, local copies, waits for them, and re-layouts: 10.4 us -> none  [the longest x1 2.81 us: on_device(): gate_owner = jnp.where(filled, jnp.take(weights_flat, owner_index), 0.0)]
    dot_general x6 -> x12, matrix products: 33.3 us -> 23 us  [dot(): lax.dot_general(a, b, (dims, ((), ())), preferred_element_type=jnp.float32)]
    broadcast_in_dim x3 -> x0, local copies, waits for them, and re-layouts: 6.89 us -> none  [the longest x2 6.75 us: send_rows(): jnp.repeat(buffer.reshape(experts_all, 1, capacity, feature), SPLIT, axis=1)]
  transfers between devices with their start and end apart: 4 -> 42, of which waited for: 4 -> 22; matrix products, arithmetic and copies ran while one was open for 11% -> 9% of each run, Pallas kernels for 0% -> 2%
where the time goes in v1:
time: 235 us
  waiting for transfers between devices  139 us (59%)
  starting transfers between devices  60.7 us (26%)
  matrix products  23 us (10%)
  Pallas kernels  5.26 us (2%)
  local copies, waits for them, and re-layouts  4.33 us (2%)
    ppermute x42, waiting for transfers between devices, swap(): return lax.ppermute(value, 'expert', [(i, i ^ bits) for i in range(count)])  139 us
    ppermute x42, starting transfers between devices, swap(): return lax.ppermute(value, 'expert', [(i, i ^ bits) for i in range(count)])  60.7 us
    dot_general x12, matrix products, dot(): lax.dot_general(a, b, (dims, ((), ())), preferred_element_type=jnp.float32)  23 us
  transfers between devices with their start and end apart: 42, of which 22 were waited for; matrix products, arithmetic and copies ran while one was open for 9% of the time, Pallas kernels for 2%

profile of v1, /device:TPU:0, one launch (start us, length us, event | category | flops | bytes accessed | tf_op | source)
XLA Modules:
  0.0 234.6 jit_solution(6386915158765844852)
XLA Ops:
  3.8 3.1 %collective-permute-start = (bf16[48,1536]{1,0:T(8,128)(2,1)S(1)}, bf16[48,1536]{1,0:T(8,128)(2,1)S(1)}, u32[]{:S(2)}, u32[]{:S(2)}) collective-permute-start(bf16[48,1536]{1,0:T(8,128)(2,1)S(1)} %get-tuple-element.21), channel_id=1, source_target_pairs={{0,8},{1,9},{2,10},{3,11},{4,12},{5,13},{6,14},{7,15},{8,0},{9,1},... | collective-permute-start | bytes 442376 | tf_op jit(solution)/shard_map/ppermute | solution.py:16
  6.9 2.6 %collective-permute-start.1 = (bf16[48,1536]{1,0:T(8,128)(2,1)S(1)}, bf16[48,1536]{1,0:T(8,128)(2,1)S(1)}, u32[]{:S(2)}, u32[]{:S(2)}) collective-permute-start(bf16[48,1536]{1,0:T(8,128)(2,1)S(1)} %get-tuple-element.22), channel_id=1, source_target_pairs={{0,16},{1,17},{2,18},{3,19},{4,20},{5,21},{6,22},{7,23},{8,24},{9,... | collective-permute-start | bytes 442376 | tf_op jit(solution)/shard_map/ppermute | solution.py:16
  15.3 5.7 %collective-permute-done.1 = bf16[48,1536]{1,0:T(8,128)(2,1)S(1)} collective-permute-done((bf16[48,1536]{1,0:T(8,128)(2,1)S(1)}, bf16[48,1536]{1,0:T(8,128)(2,1)S(1)}, u32[]{:S(2)}, u32[]{:S(2)}) %collective-permute-start.1) | collective-permute-done | bytes 147488 | tf_op jit(solution)/shard_map/ppermute | solution.py:16
  21.0 2.3 collective-permute-start.22
  25.0 3.3 %collective-permute-start.9 = (bf16[48,1536]{1,0:T(8,128)(2,1)S(1)}, bf16[48,1536]{1,0:T(8,128)(2,1)S(1)}, u32[]{:S(2)}, u32[]{:S(2)}) collective-permute-start(bf16[48,1536]{1,0:T(8,128)(2,1)S(1)} %get-tuple-element.26), channel_id=1, source_target_pairs={{0,20},{1,21},{2,22},{3,23},{4,16},{5,17},{6,18},{7,19},{8,28},{9,... | collective-permute-start | bytes 442376 | tf_op jit(solution)/shard_map/ppermute | solution.py:16
  28.3 10.9 %collective-permute-done.21 = bf16[48,1536]{1,0:T(8,128)(2,1)S(1)} collective-permute-done((bf16[48,1536]{1,0:T(8,128)(2,1)S(1)}, bf16[48,1536]{1,0:T(8,128)(2,1)S(1)}, u32[]{:S(2)}, u32[]{:S(2)}) %collective-permute-start.21) | collective-permute-done | bytes 147488 | tf_op jit(solution)/shard_map/ppermute | solution.py:16
  39.2 2.9 %collective-permute-start.10 = (bf16[48,1536]{1,0:T(8,128)(2,1)S(1)}, bf16[48,1536]{1,0:T(8,128)(2,1)S(1)}, u32[]{:S(2)}, u32[]{:S(2)}) collective-permute-start(bf16[48,1536]{1,0:T(8,128)(2,1)S(1)} %get-tuple-element.27), channel_id=1, source_target_pairs={{0,28},{1,29},{2,30},{3,31},{4,24},{5,25},{6,26},{7,27},{8,20},{9,... | collective-permute-start | bytes 442376 | tf_op jit(solution)/shard_map/ppermute | solution.py:16
  46.2 4.6 %collective-permute-done.9 = bf16[48,1536]{1,0:T(8,128)(2,1)S(1)} collective-permute-done((bf16[48,1536]{1,0:T(8,128)(2,1)S(1)}, bf16[48,1536]{1,0:T(8,128)(2,1)S(1)}, u32[]{:S(2)}, u32[]{:S(2)}) %collective-permute-start.9) | collective-permute-done | bytes 147488 | tf_op jit(solution)/shard_map/ppermute | solution.py:16
  50.8 4.9 %collective-permute-start.28 = (bf16[48,1536]{1,0:T(8,128)(2,1)S(1)}, bf16[48,1536]{1,0:T(8,128)(2,1)S(1)}, u32[]{:S(2)}, u32[]{:S(2)}) collective-permute-start(bf16[48,1536]{1,0:T(8,128)(2,1)S(1)} %get-tuple-element.35), channel_id=1, source_target_pairs={{0,28},{1,29},{2,30},{3,31},{4,24},{5,25},{6,26},{7,27},{8,20},{9,... | collective-permute-start | bytes 442376 | tf_op jit(solution)/shard_map/ppermute | solution.py:16
  62.1 8.5 %collective-permute-done.3 = bf16[192,1536]{1,0:T(8,128)(2,1)S(1)} collective-permute-done((bf16[192,1536]{1,0:T(8,128)(2,1)S(1)}, bf16[192,1536]{1,0:T(8,128)(2,1)S(1)}, u32[]{:S(2)}, u32[]{:S(2)}) %collective-permute-start.3) | collective-permute-done | bytes 589856 | tf_op jit(solution)/shard_map/ppermute | solution.py:16
  70.6 2.5 %collective-permute-start.29 = (bf16[192,1536]{1,0:T(8,128)(2,1)S(1)}, bf16[192,1536]{1,0:T(8,128)(2,1)S(1)}, u32[]{:S(2)}, u32[]{:S(2)}) collective-permute-start(bf16[192,1536]{1,0:T(8,128)(2,1)S(1)} %pad_maximum_fusion.7), channel_id=1, source_target_pairs={{0,2},{1,3},{2,0},{3,1},{4,6},{5,7},{6,4},{7,5},{8,10},{9,11},{10,... | collective-permute-start | bytes 1769480 | tf_op jit(solution)/shard_map/ppermute | solution.py:16
  73.3 9.9 %collective-permute-done.11 = bf16[192,1536]{1,0:T(8,128)(2,1)S(1)} collective-permute-done((bf16[192,1536]{1,0:T(8,128)(2,1)S(1)}, bf16[192,1536]{1,0:T(8,128)(2,1)S(1)}, u32[]{:S(2)}, u32[]{:S(2)}) %collective-permute-start.11) | collective-permute-done | bytes 589856 | tf_op jit(solution)/shard_map/ppermute | solution.py:16
  83.4 12.5 %collective-permute-done.23 = bf16[192,1536]{1,0:T(8,128)(2,1)S(1)} collective-permute-done((bf16[192,1536]{1,0:T(8,128)(2,1)S(1)}, bf16[192,1536]{1,0:T(8,128)(2,1)S(1)}, u32[]{:S(2)}, u32[]{:S(2)}) %collective-permute-start.23) | collective-permute-done | bytes 589856 | tf_op jit(solution)/shard_map/ppermute | solution.py:16
  96.1 7.4 %collective-permute-done.29 = bf16[192,1536]{1,0:T(8,128)(2,1)S(1)} collective-permute-done((bf16[192,1536]{1,0:T(8,128)(2,1)S(1)}, bf16[192,1536]{1,0:T(8,128)(2,1)S(1)}, u32[]{:S(2)}, u32[]{:S(2)}) %collective-permute-start.29) | collective-permute-done | bytes 589856 | tf_op jit(solution)/shard_map/ppermute | solution.py:16
  119.8 3.1 %collective-permute-done.6 = bf16[192,1536]{1,0:T(8,128)(2,1)S(1)} collective-permute-done((bf16[192,1536]{1,0:T(8,128)(2,1)S(1)}, bf16[192,1536]{1,0:T(8,128)(2,1)S(1)}, u32[]{:S(2)}, u32[]{:S(2)}) %collective-permute-start.6) | collective-permute-done | bytes 589856 | tf_op jit(solution)/shard_map/ppermute | solution.py:16
  124.5 11.0 %collective-permute-done.12 = bf16[192,1536]{1,0:T(8,128)(2,1)S(1)} collective-permute-done((bf16[192,1536]{1,0:T(8,128)(2,1)S(1)}, bf16[192,1536]{1,0:T(8,128)(2,1)S(1)}, u32[]{:S(2)}, u32[]{:S(2)}) %collective-permute-start.12) | collective-permute-done | bytes 589856 | tf_op jit(solution)/shard_map/ppermute | solution.py:16
  137.0 11.2 %collective-permute-done.24 = bf16[192,1536]{1,0:T(8,128)(2,1)S(1)} collective-permute-done((bf16[192,1536]{1,0:T(8,128)(2,1)S(1)}, bf16[192,1536]{1,0:T(8,128)(2,1)S(1)}, u32[]{:S(2)}, u32[]{:S(2)}) %collective-permute-start.24) | collective-permute-done | bytes 589856 | tf_op jit(solution)/shard_map/ppermute | solution.py:16
  149.2 11.2 %collective-permute-done.30 = bf16[192,1536]{1,0:T(8,128)(2,1)S(1)} collective-permute-done((bf16[192,1536]{1,0:T(8,128)(2,1)S(1)}, bf16[192,1536]{1,0:T(8,128)(2,1)S(1)}, u32[]{:S(2)}, u32[]{:S(2)}) %collective-permute-start.30) | collective-permute-done | bytes 589856 | tf_op jit(solution)/shard_map/ppermute | solution.py:16
  162.8 2.5 %collective-permute-start.17 = (bf16[48,1536]{1,0:T(8,128)(2,1)S(1)}, bf16[48,1536]{1,0:T(8,128)(2,1)S(1)}, u32[]{:S(2)}, u32[]{:S(2)}) collective-permute-start(bf16[48,1536]{1,0:T(8,128)(2,1)S(1)} %get-tuple-element.53), channel_id=1, source_target_pairs={{0,20},{1,21},{2,22},{3,23},{4,16},{5,17},{6,18},{7,19},{8,28},{9,... | collective-permute-start | bytes 442376 | tf_op jit(solution)/shard_map/ppermute | solution.py:16
  165.4 4.5 %collective-permute-done.15.refs_3_ = bf16[48,1536]{1,0:T(8,128)(2,1)S(1)} collective-permute-done((bf16[48,1536]{1,0:T(8,128)(2,1)S(1)}, bf16[48,1536]{1,0:T(8,128)(2,1)S(1)}, u32[]{:S(2)}, u32[]{:S(2)}) %collective-permute-start.15) | collective-permute-done | bytes 147488 | tf_op jit(solution)/shard_map/ppermute | solution.py:16
  169.9 8.8 %collective-permute-done.16.refs_4_ = bf16[48,1536]{1,0:T(8,128)(2,1)S(1)} collective-permute-done((bf16[48,1536]{1,0:T(8,128)(2,1)S(1)}, bf16[48,1536]{1,0:T(8,128)(2,1)S(1)}, u32[]{:S(2)}, u32[]{:S(2)}) %collective-permute-start.16) | collective-permute-done | bytes 147488 | tf_op jit(solution)/shard_map/ppermute | solution.py:16
  178.7 4.1 %collective-permute-done.17.refs_5_ = bf16[48,1536]{1,0:T(8,128)(2,1)S(1)} collective-permute-done((bf16[48,1536]{1,0:T(8,128)(2,1)S(1)}, bf16[48,1536]{1,0:T(8,128)(2,1)S(1)}, u32[]{:S(2)}, u32[]{:S(2)}) %collective-permute-start.17) | collective-permute-done | bytes 147488 | tf_op jit(solution)/shard_map/ppermute | solution.py:16
  186.3 4.6 %collective-permute-done.19.refs_7_ = bf16[48,1536]{1,0:T(8,128)(2,1)S(1)} collective-permute-done((bf16[48,1536]{1,0:T(8,128)(2,1)S(1)}, bf16[48,1536]{1,0:T(8,128)(2,1)S(1)}, u32[]{:S(2)}, u32[]{:S(2)}) %collective-permute-start.19) | collective-permute-done | bytes 147488 | tf_op jit(solution)/shard_map/ppermute | solution.py:16
  193.2 3.9 %collective-permute-done.32.refs_2_ = bf16[48,1536]{1,0:T(8,128)(2,1)S(1)} collective-permute-done((bf16[48,1536]{1,0:T(8,128)(2,1)S(1)}, bf16[48,1536]{1,0:T(8,128)(2,1)S(1)}, u32[]{:S(2)}, u32[]{:S(2)}) %collective-permute-start.32) | collective-permute-done | bytes 147488 | tf_op jit(solution)/shard_map/ppermute | solution.py:16
  199.3 4.6 %collective-permute-start.35 = (bf16[48,1536]{1,0:T(8,128)(2,1)S(1)}, bf16[48,1536]{1,0:T(8,128)(2,1)S(1)}, u32[]{:S(2)}, u32[]{:S(2)}) collective-permute-start(bf16[48,1536]{1,0:T(8,128)(2,1)S(1)} %get-tuple-element.45), channel_id=1, source_target_pairs={{0,20},{1,21},{2,22},{3,23},{4,16},{5,17},{6,18},{7,19},{8,28},{9,... | collective-permute-start | bytes 442376 | tf_op jit(solution)/shard_map/ppermute | solution.py:16
  203.8 7.1 %collective-permute-done.34.refs_4_ = bf16[48,1536]{1,0:T(8,128)(2,1)S(1)} collective-permute-done((bf16[48,1536]{1,0:T(8,128)(2,1)S(1)}, bf16[48,1536]{1,0:T(8,128)(2,1)S(1)}, u32[]{:S(2)}, u32[]{:S(2)}) %collective-permute-start.34) | collective-permute-done | bytes 147488 | tf_op jit(solution)/shard_map/ppermute | solution.py:16
  211.5 2.7 %collective-permute-done.35.refs_5_ = bf16[48,1536]{1,0:T(8,128)(2,1)S(1)} collective-permute-done((bf16[48,1536]{1,0:T(8,128)(2,1)S(1)}, bf16[48,1536]{1,0:T(8,128)(2,1)S(1)}, u32[]{:S(2)}, u32[]{:S(2)}) %collective-permute-start.35) | collective-permute-done | bytes 147488 | tf_op jit(solution)/shard_map/ppermute | solution.py:16
  214.2 2.9 %collective-permute-start.37 = (bf16[48,1536]{1,0:T(8,128)(2,1)S(1)}, bf16[48,1536]{1,0:T(8,128)(2,1)S(1)}, u32[]{:S(2)}, u32[]{:S(2)}) collective-permute-start(bf16[48,1536]{1,0:T(8,128)(2,1)S(1)} %get-tuple-element.44), channel_id=1, source_target_pairs={{0,28},{1,29},{2,30},{3,31},{4,24},{5,25},{6,26},{7,27},{8,20},{9,... | collective-permute-start | bytes 442376 | tf_op jit(solution)/shard_map/ppermute | solution.py:16
  219.0 3.1 %collective-permute-done.37.refs_7_ = bf16[48,1536]{1,0:T(8,128)(2,1)S(1)} collective-permute-done((bf16[48,1536]{1,0:T(8,128)(2,1)S(1)}, bf16[48,1536]{1,0:T(8,128)(2,1)S(1)}, u32[]{:S(2)}, u32[]{:S(2)}) %collective-permute-start.37) | collective-permute-done | bytes 147488 | tf_op jit(solution)/shard_map/ppermute | solution.py:16
  223.7 3.1 %fusion.14 = f32[1536,512]{1,0:T(8,128)S(1)} fusion(bf16[768,1536]{1,0:T(8,128)(2,1)} %collective-permute-done.38, bf16[768,512]{1,0:T(8,128)(2,1)S(1)} %collective-permute-done.39), kind=kOutput, calls=%fused_computation.80 | convolution fusion | flops 1207959552 | bytes 6291456 | tf_op jit(solution)/shard_map/dot_general | solution.py:175
  226.8 3.2 %fusion.1 = f32[1,1536,512]{2,1,0:T(8,128)} fusion(f32[1536,512]{1,0:T(8,128)S(1)} %fusion.14, bf16[768,1536]{1,0:T(8,128)(2,1)S(1)} %get-tuple-element.40, bf16[384,1024]{1,0:T(8,128)(2,1)S(1)} %multiply_convert_fusion.1, bf16[384,1024]{1,0:T(8,128)(2,1)S(1)} %multiply_convert_fusion), kind=kOutput, calls=%fused_computation.3 | convolution fusion | flops 1210318848 | bytes 10223616 | tf_op jit(solution)/shard_map/dot_general | solution.py:175
  231.4 3.2 %fusion = f32[1,512,1536]{2,1,0:T(8,128)} fusion(f32[512,1536]{1,0:T(8,128)S(1)} %fusion.15, bf16[768,1536]{1,0:T(8,128)(2,1)S(1)} %get-tuple-element.36, bf16[384,1024]{1,0:T(8,128)(2,1)S(1)} %get-tuple-element.92, bf16[384,1024]{1,0:T(8,128)(2,1)S(1)} %get-tuple-element.94), kind=kOutput, calls=%fused_computation.1 | convolution fusion | flops 1210318848 | bytes 10223616 | tf_op jit(solution)/shard_map/dot_general | solution.py:175
  (118 shorter events, 57.6 us)
Async XLA Ops:
  6.9 14.0 %collective-permute-start.1 = (bf16[48,1536]{1,0:T(8,128)(2,1)S(1)}, bf16[48,1536]{1,0:T(8,128)(2,1)S(1)}, u32[]{:S(2)}, u32[]{:S(2)}) collective-permute-start(bf16[48,1536]{1,0:T(8,128)(2,1)S(1)} %get-tuple-element.22), channel_id=1, source_target_pairs={{0,16},{1,17},{2,18},{3,19},{4,20},{5,21},{6,22},{7,23},{8,24},{9,... | collective-permute-start | bytes 442376 | tf_op jit(solution)/shard_map/ppermute | solution.py:16
  9.5 11.4 %collective-permute-start.2 = (bf16[48,1536]{1,0:T(8,128)(2,1)S(1)}, bf16[48,1536]{1,0:T(8,128)(2,1)S(1)}, u32[]{:S(2)}, u32[]{:S(2)}) collective-permute-start(bf16[48,1536]{1,0:T(8,128)(2,1)S(1)} %get-tuple-element.23), channel_id=1, source_target_pairs={{0,24},{1,25},{2,26},{3,27},{4,28},{5,29},{6,30},{7,31},{8,16},{9,... | collective-permute-start | bytes 442376 | tf_op jit(solution)/shard_map/ppermute | solution.py:16
  9.5 33.2 %collective-permute-start.7 = (bf16[48,1536]{1,0:T(8,128)(2,1)S(1)}, bf16[48,1536]{1,0:T(8,128)(2,1)S(1)}, u32[]{:S(2)}, u32[]{:S(2)}) collective-permute-start(bf16[48,1536]{1,0:T(8,128)(2,1)S(1)} %get-tuple-element.24), channel_id=1, source_target_pairs={{0,4},{1,5},{2,6},{3,7},{4,0},{5,1},{6,2},{7,3},{8,12},{9,13},{10,... | collective-permute-start | bytes 442376 | tf_op jit(solution)/shard_map/ppermute | solution.py:16
  11.3 33.3 %collective-permute-start.8 = (bf16[48,1536]{1,0:T(8,128)(2,1)S(1)}, bf16[48,1536]{1,0:T(8,128)(2,1)S(1)}, u32[]{:S(2)}, u32[]{:S(2)}) collective-permute-start(bf16[48,1536]{1,0:T(8,128)(2,1)S(1)} %get-tuple-element.25), channel_id=1, source_target_pairs={{0,12},{1,13},{2,14},{3,15},{4,8},{5,9},{6,10},{7,11},{8,4},{9,5},... | collective-permute-start | bytes 442376 | tf_op jit(solution)/shard_map/ppermute | solution.py:16
  14.0 11.0 %collective-permute-start.20 = (bf16[48,1536]{1,0:T(8,128)(2,1)S(1)}, bf16[48,1536]{1,0:T(8,128)(2,1)S(1)}, u32[]{:S(2)}, u32[]{:S(2)}) collective-permute-start(bf16[48,1536]{1,0:T(8,128)(2,1)S(1)} %get-tuple-element.29), channel_id=1, source_target_pairs={{0,8},{1,9},{2,10},{3,11},{4,12},{5,13},{6,14},{7,15},{8,0},{9,1},... | collective-permute-start | bytes 442376 | tf_op jit(solution)/shard_map/ppermute | solution.py:16
  21.0 18.3 %collective-permute-start.21 = (bf16[48,1536]{1,0:T(8,128)(2,1)S(1)}, bf16[48,1536]{1,0:T(8,128)(2,1)S(1)}, u32[]{:S(2)}, u32[]{:S(2)}) collective-permute-start(bf16[48,1536]{1,0:T(8,128)(2,1)S(1)} %get-tuple-element.30), channel_id=1, source_target_pairs={{0,16},{1,17},{2,18},{3,19},{4,20},{5,21},{6,22},{7,23},{8,24},{9,... | collective-permute-start | bytes 442376 | tf_op jit(solution)/shard_map/ppermute | solution.py:16
  21.0 21.2 %collective-permute-start.22 = (bf16[48,1536]{1,0:T(8,128)(2,1)S(1)}, bf16[48,1536]{1,0:T(8,128)(2,1)S(1)}, u32[]{:S(2)}, u32[]{:S(2)}) collective-permute-start(bf16[48,1536]{1,0:T(8,128)(2,1)S(1)} %get-tuple-element.31), channel_id=1, source_target_pairs={{0,24},{1,25},{2,26},{3,27},{4,28},{5,29},{6,30},{7,31},{8,16},{9,... | collective-permute-start | bytes 442376 | tf_op jit(solution)/shard_map/ppermute | solution.py:16
  25.0 25.8 %collective-permute-start.9 = (bf16[48,1536]{1,0:T(8,128)(2,1)S(1)}, bf16[48,1536]{1,0:T(8,128)(2,1)S(1)}, u32[]{:S(2)}, u32[]{:S(2)}) collective-permute-start(bf16[48,1536]{1,0:T(8,128)(2,1)S(1)} %get-tuple-element.26), channel_id=1, source_target_pairs={{0,20},{1,21},{2,22},{3,23},{4,16},{5,17},{6,18},{7,19},{8,28},{9,... | collective-permute-start | bytes 442376 | tf_op jit(solution)/shard_map/ppermute | solution.py:16
  39.2 16.5 %collective-permute-start.10 = (bf16[48,1536]{1,0:T(8,128)(2,1)S(1)}, bf16[48,1536]{1,0:T(8,128)(2,1)S(1)}, u32[]{:S(2)}, u32[]{:S(2)}) collective-permute-start(bf16[48,1536]{1,0:T(8,128)(2,1)S(1)} %get-tuple-element.27), channel_id=1, source_target_pairs={{0,28},{1,29},{2,30},{3,31},{4,24},{5,25},{6,26},{7,27},{8,20},{9,... | collective-permute-start | bytes 442376 | tf_op jit(solution)/shard_map/ppermute | solution.py:16
  42.2 15.1 %collective-permute-start.25 = (bf16[48,1536]{1,0:T(8,128)(2,1)S(1)}, bf16[48,1536]{1,0:T(8,128)(2,1)S(1)}, u32[]{:S(2)}, u32[]{:S(2)}) collective-permute-start(bf16[48,1536]{1,0:T(8,128)(2,1)S(1)} %get-tuple-element.32), channel_id=1, source_target_pairs={{0,4},{1,5},{2,6},{3,7},{4,0},{5,1},{6,2},{7,3},{8,12},{9,13},{10,... | collective-permute-start | bytes 442376 | tf_op jit(solution)/shard_map/ppermute | solution.py:16
  42.8 14.6 %collective-permute-start.26 = (bf16[48,1536]{1,0:T(8,128)(2,1)S(1)}, bf16[48,1536]{1,0:T(8,128)(2,1)S(1)}, u32[]{:S(2)}, u32[]{:S(2)}) collective-permute-start(bf16[48,1536]{1,0:T(8,128)(2,1)S(1)} %get-tuple-element.33), channel_id=1, source_target_pairs={{0,12},{1,13},{2,14},{3,15},{4,8},{5,9},{6,10},{7,11},{8,4},{9,5},... | collective-permute-start | bytes 442376 | tf_op jit(solution)/shard_map/ppermute | solution.py:16
  44.6 15.4 %collective-permute-start.27 = (bf16[48,1536]{1,0:T(8,128)(2,1)S(1)}, bf16[48,1536]{1,0:T(8,128)(2,1)S(1)}, u32[]{:S(2)}, u32[]{:S(2)}) collective-permute-start(bf16[48,1536]{1,0:T(8,128)(2,1)S(1)} %get-tuple-element.34), channel_id=1, source_target_pairs={{0,20},{1,21},{2,22},{3,23},{4,16},{5,17},{6,18},{7,19},{8,28},{9,... | collective-permute-start | bytes 442376 | tf_op jit(solution)/shard_map/ppermute | solution.py:16
  55.7 14.9 %collective-permute-start.3 = (bf16[192,1536]{1,0:T(8,128)(2,1)S(1)}, bf16[192,1536]{1,0:T(8,128)(2,1)S(1)}, u32[]{:S(2)}, u32[]{:S(2)}) collective-permute-start(bf16[192,1536]{1,0:T(8,128)(2,1)S(1)} %pad_maximum_fusion.4), channel_id=1, source_target_pairs={{0,2},{1,3},{2,0},{3,1},{4,6},{5,7},{6,4},{7,5},{8,10},{9,11},{10,... | collective-permute-start | bytes 1769480 | tf_op jit(solution)/shard_map/ppermute | solution.py:16
  57.3 46.3 %collective-permute-start.4 = (bf16[1536,512]{1,0:T(8,128)(2,1)S(1)}, bf16[1536,512]{1,0:T(8,128)(2,1)S(1)}, u32[]{:S(2)}, u32[]{:S(2)}) collective-permute-start(bf16[1536,512]{1,0:T(8,128)(2,1)S(1)} %bitcast.36), channel_id=1, source_target_pairs={{0,1},{1,0},{2,3},{3,2},{4,5},{5,4},{6,7},{7,6},{8,9},{9,8},{10,11... | collective-permute-start | bytes 4718600 | tf_op jit(solution)/shard_map/ppermute | solution.py:16
  57.4 47.8 %collective-permute-start.5 = (bf16[512,1536]{1,0:T(8,128)(2,1)S(1)}, bf16[512,1536]{1,0:T(8,128)(2,1)S(1)}, u32[]{:S(2)}, u32[]{:S(2)}) collective-permute-start(bf16[512,1536]{1,0:T(8,128)(2,1)S(1)} %bitcast.31), channel_id=1, source_target_pairs={{0,1},{1,0},{2,3},{3,2},{4,5},{5,4},{6,7},{7,6},{8,9},{9,8},{10,11... | collective-permute-start | bytes 4718600 | tf_op jit(solution)/shard_map/ppermute | solution.py:16
  60.0 23.3 %collective-permute-start.11 = (bf16[192,1536]{1,0:T(8,128)(2,1)S(1)}, bf16[192,1536]{1,0:T(8,128)(2,1)S(1)}, u32[]{:S(2)}, u32[]{:S(2)}) collective-permute-start(bf16[192,1536]{1,0:T(8,128)(2,1)S(1)} %pad_maximum_fusion.5), channel_id=1, source_target_pairs={{0,2},{1,3},{2,0},{3,1},{4,6},{5,7},{6,4},{7,5},{8,10},{9,11},{10,... | collective-permute-start | bytes 1769480 | tf_op jit(solution)/shard_map/ppermute | solution.py:16
  61.5 34.4 %collective-permute-start.23 = (bf16[192,1536]{1,0:T(8,128)(2,1)S(1)}, bf16[192,1536]{1,0:T(8,128)(2,1)S(1)}, u32[]{:S(2)}, u32[]{:S(2)}) collective-permute-start(bf16[192,1536]{1,0:T(8,128)(2,1)S(1)} %pad_maximum_fusion.6), channel_id=1, source_target_pairs={{0,2},{1,3},{2,0},{3,1},{4,6},{5,7},{6,4},{7,5},{8,10},{9,11},{10,... | collective-permute-start | bytes 1769480 | tf_op jit(solution)/shard_map/ppermute | solution.py:16
  70.6 32.9 %collective-permute-start.29 = (bf16[192,1536]{1,0:T(8,128)(2,1)S(1)}, bf16[192,1536]{1,0:T(8,128)(2,1)S(1)}, u32[]{:S(2)}, u32[]{:S(2)}) collective-permute-start(bf16[192,1536]{1,0:T(8,128)(2,1)S(1)} %pad_maximum_fusion.7), channel_id=1, source_target_pairs={{0,2},{1,3},{2,0},{3,1},{4,6},{5,7},{6,4},{7,5},{8,10},{9,11},{10,... | collective-permute-start | bytes 1769480 | tf_op jit(solution)/shard_map/ppermute | solution.py:16
  83.4 140.3 %collective-permute-start.38 = (bf16[768,1536]{1,0:T(8,128)(2,1)S(1)}, bf16[768,1536]{1,0:T(8,128)(2,1)}, u32[]{:S(2)}, u32[]{:S(2)}) collective-permute-start(bf16[768,1536]{1,0:T(8,128)(2,1)S(1)} %get-tuple-element.40), channel_id=1, source_target_pairs={{0,1},{1,0},{2,3},{3,2},{4,5},{5,4},{6,7},{7,6},{8,9},{9,8},{10,11... | collective-permute-start | bytes 7077896 | tf_op jit(solution)/shard_map/ppermute | solution.py:16
  103.6 126.4 %collective-permute-start.41 = (bf16[768,1536]{1,0:T(8,128)(2,1)S(1)}, bf16[768,1536]{1,0:T(8,128)(2,1)S(1)}, u32[]{:S(2)}, u32[]{:S(2)}) collective-permute-start(bf16[768,1536]{1,0:T(8,128)(2,1)S(1)} %get-tuple-element.36), channel_id=1, source_target_pairs={{0,1},{1,0},{2,3},{3,2},{4,5},{5,4},{6,7},{7,6},{8,9},{9,8},{10,11... | collective-permute-start | bytes 7077896 | tf_op jit(solution)/shard_map/ppermute | solution.py:16
  106.7 16.2 %collective-permute-start.6 = (bf16[192,1536]{1,0:T(8,128)(2,1)S(1)}, bf16[192,1536]{1,0:T(8,128)(2,1)S(1)}, u32[]{:S(2)}, u32[]{:S(2)}) collective-permute-start(bf16[192,1536]{1,0:T(8,128)(2,1)S(1)} %slice.113), channel_id=1, source_target_pairs={{0,2},{1,3},{2,0},{3,1},{4,6},{5,7},{6,4},{7,5},{8,10},{9,11},{10,... | collective-permute-start | bytes 1769480 | tf_op jit(solution)/shard_map/ppermute | solution.py:16
  111.3 24.3 %collective-permute-start.12 = (bf16[192,1536]{1,0:T(8,128)(2,1)S(1)}, bf16[192,1536]{1,0:T(8,128)(2,1)S(1)}, u32[]{:S(2)}, u32[]{:S(2)}) collective-permute-start(bf16[192,1536]{1,0:T(8,128)(2,1)S(1)} %slice.116), channel_id=1, source_target_pairs={{0,2},{1,3},{2,0},{3,1},{4,6},{5,7},{6,4},{7,5},{8,10},{9,11},{10,... | collective-permute-start | bytes 1769480 | tf_op jit(solution)/shard_map/ppermute | solution.py:16
  114.9 33.2 %collective-permute-start.24 = (bf16[192,1536]{1,0:T(8,128)(2,1)S(1)}, bf16[192,1536]{1,0:T(8,128)(2,1)S(1)}, u32[]{:S(2)}, u32[]{:S(2)}) collective-permute-start(bf16[192,1536]{1,0:T(8,128)(2,1)S(1)} %slice.125), channel_id=1, source_target_pairs={{0,2},{1,3},{2,0},{3,1},{4,6},{5,7},{6,4},{7,5},{8,10},{9,11},{10,... | collective-permute-start | bytes 1769480 | tf_op jit(solution)/shard_map/ppermute | solution.py:16
  122.9 37.5 %collective-permute-start.30 = (bf16[192,1536]{1,0:T(8,128)(2,1)S(1)}, bf16[192,1536]{1,0:T(8,128)(2,1)S(1)}, u32[]{:S(2)}, u32[]{:S(2)}) collective-permute-start(bf16[192,1536]{1,0:T(8,128)(2,1)S(1)} %slice.128), channel_id=1, source_target_pairs={{0,2},{1,3},{2,0},{3,1},{4,6},{5,7},{6,4},{7,5},{8,10},{9,11},{10,... | collective-permute-start | bytes 1769480 | tf_op jit(solution)/shard_map/ppermute | solution.py:16
  135.8 25.7 %collective-permute-start.13 = (bf16[48,1536]{1,0:T(8,128)(2,1)S(1)}, bf16[48,1536]{1,0:T(8,128)(2,1)S(1)}, u32[]{:S(2)}, u32[]{:S(2)}) collective-permute-start(bf16[48,1536]{1,0:T(8,128)(2,1)S(1)} %get-tuple-element.55), channel_id=1, source_target_pairs={{0,4},{1,5},{2,6},{3,7},{4,0},{5,1},{6,2},{7,3},{8,12},{9,13},{10,... | collective-permute-start | bytes 442376 | tf_op jit(solution)/shard_map/ppermute | solution.py:16
  148.2 14.6 %collective-permute-start.14 = (bf16[48,1536]{1,0:T(8,128)(2,1)S(1)}, bf16[48,1536]{1,0:T(8,128)(2,1)S(1)}, u32[]{:S(2)}, u32[]{:S(2)}) collective-permute-start(bf16[48,1536]{1,0:T(8,128)(2,1)S(1)} %get-tuple-element.58), channel_id=1, source_target_pairs={{0,8},{1,9},{2,10},{3,11},{4,12},{5,13},{6,14},{7,15},{8,0},{9,1},... | collective-permute-start | bytes 442376 | tf_op jit(solution)/shard_map/ppermute | solution.py:16
  161.4 17.2 %collective-permute-start.16 = (bf16[48,1536]{1,0:T(8,128)(2,1)S(1)}, bf16[48,1536]{1,0:T(8,128)(2,1)S(1)}, u32[]{:S(2)}, u32[]{:S(2)}) collective-permute-start(bf16[48,1536]{1,0:T(8,128)(2,1)S(1)} %get-tuple-element.57), channel_id=1, source_target_pairs={{0,16},{1,17},{2,18},{3,19},{4,20},{5,21},{6,22},{7,23},{8,24},{9,... | collective-permute-start | bytes 442376 | tf_op jit(solution)/shard_map/ppermute | solution.py:16
  162.8 19.9 %collective-permute-start.17 = (bf16[48,1536]{1,0:T(8,128)(2,1)S(1)}, bf16[48,1536]{1,0:T(8,128)(2,1)S(1)}, u32[]{:S(2)}, u32[]{:S(2)}) collective-permute-start(bf16[48,1536]{1,0:T(8,128)(2,1)S(1)} %get-tuple-element.53), channel_id=1, source_target_pairs={{0,20},{1,21},{2,22},{3,23},{4,16},{5,17},{6,18},{7,19},{8,28},{9,... | collective-permute-start | bytes 442376 | tf_op jit(solution)/shard_map/ppermute | solution.py:16
  169.8 15.1 %collective-permute-start.18 = (bf16[48,1536]{1,0:T(8,128)(2,1)S(1)}, bf16[48,1536]{1,0:T(8,128)(2,1)S(1)}, u32[]{:S(2)}, u32[]{:S(2)}) collective-permute-start(bf16[48,1536]{1,0:T(8,128)(2,1)S(1)} %get-tuple-element.56), channel_id=1, source_target_pairs={{0,24},{1,25},{2,26},{3,27},{4,28},{5,29},{6,30},{7,31},{8,16},{9,... | collective-permute-start | bytes 442376 | tf_op jit(solution)/shard_map/ppermute | solution.py:16
  178.7 45.0 %collective-permute-start.39 = (bf16[768,512]{1,0:T(8,128)(2,1)S(1)}, bf16[768,512]{1,0:T(8,128)(2,1)S(1)}, u32[]{:S(2)}, u32[]{:S(2)}) collective-permute-start(bf16[768,512]{1,0:T(8,128)(2,1)S(1)} %pad_maximum_fusion.3), channel_id=1, source_target_pairs={{0,1},{1,0},{2,3},{3,2},{4,5},{5,4},{6,7},{7,6},{8,9},{9,8},{10,11... | collective-permute-start | bytes 2359304 | tf_op jit(solution)/shard_map/ppermute | solution.py:16
  197.1 13.9 %collective-permute-start.34 = (bf16[48,1536]{1,0:T(8,128)(2,1)S(1)}, bf16[48,1536]{1,0:T(8,128)(2,1)S(1)}, u32[]{:S(2)}, u32[]{:S(2)}) collective-permute-start(bf16[48,1536]{1,0:T(8,128)(2,1)S(1)} %get-tuple-element.49), channel_id=1, source_target_pairs={{0,16},{1,17},{2,18},{3,19},{4,20},{5,21},{6,22},{7,23},{8,24},{9,... | collective-permute-start | bytes 442376 | tf_op jit(solution)/shard_map/ppermute | solution.py:16
  199.3 15.0 %collective-permute-start.35 = (bf16[48,1536]{1,0:T(8,128)(2,1)S(1)}, bf16[48,1536]{1,0:T(8,128)(2,1)S(1)}, u32[]{:S(2)}, u32[]{:S(2)}) collective-permute-start(bf16[48,1536]{1,0:T(8,128)(2,1)S(1)} %get-tuple-element.45), channel_id=1, source_target_pairs={{0,20},{1,21},{2,22},{3,23},{4,16},{5,17},{6,18},{7,19},{8,28},{9,... | collective-permute-start | bytes 442376 | tf_op jit(solution)/shard_map/ppermute | solution.py:16
  (16 other events, 119.6 us)

commit v2 on v1

v2 whole, which is shorter than its diff:
```python
import functools
import jax
import jax.numpy as jnp
from jax import lax
from jax.experimental import pallas as pl
from jax.experimental.pallas import tpu as pltpu
from jax.sharding import PartitionSpec as P

HEADS = 4
SPLIT = 4
VMEM = 20 * 1024 * 1024
FREE = pl.CostEstimate(flops=1, bytes_accessed=1, transcendentals=0)


def swap(value, bits, odd_bits=0):
    count = lax.axis_size("expert")
    return lax.ppermute(
        value, "expert", [(i, i ^ bits ^ (odd_bits if i % 2 else 0)) for i in range(count)]
    )


class Order:
    def __init__(self):
        self.last = ()

    def wait(self, *values):
        values = lax.optimization_barrier((*values, *self.last))[: len(values)]
        self.last = values[:1]
        return values[0] if len(values) == 1 else values

    def done(self, value):
        self.last = (value,)

    def begin(self, send, value, *where):
        return send(lax.optimization_barrier((value, *self.last))[0], *where)


def silu_grad(values):
    gate_sig = jax.nn.sigmoid(values)
    return gate_sig * (1.0 + values * (1.0 - gate_sig))


def heads_of(index, per_head):
    head = jnp.zeros_like(index)
    for h in range(1, HEADS):
        head = head + (index >= h * per_head).astype(jnp.int32)
    return head


def natural(index, per_head):
    head = heads_of(index, per_head)
    return HEADS * (index - per_head * head) + head


def iota(shape, dim):
    return lax.broadcasted_iota(jnp.int32, shape, dim)


def by_head(pair_rows):
    rows = pair_rows.shape[1]
    place = natural(iota((rows, rows), 1), rows // HEADS)
    turn = (iota((rows, rows), 0) == place).astype(jnp.float32)
    return jnp.dot(
        pair_rows, turn, preferred_element_type=jnp.float32, precision=lax.Precision.HIGHEST
    )


def ranks(me, routes_ref, experts_all):
    rows = routes_ref.shape[1]
    routes = by_head(routes_ref[...].astype(jnp.float32)).astype(jnp.int32)
    first, second = routes[0:1], routes[1:2]
    expert = iota((experts_all, rows), 0)
    named = ((expert == first) | (expert == second)).astype(jnp.bfloat16)
    earlier = (
        natural(iota((rows, rows), 0), rows // HEADS)
        < natural(iota((rows, rows), 1), rows // HEADS)
    ).astype(jnp.bfloat16)
    rank = jnp.dot(named, earlier, preferred_element_type=jnp.float32).astype(jnp.int32)
    return [
        (which ^ me, jnp.sum(jnp.where(expert == which, rank, 0), axis=0, keepdims=True))
        for which in (first, second)
    ]


def stacked(tokens_ref):
    feature = tokens_ref.shape[1] // HEADS
    return jnp.concatenate(
        [tokens_ref[:, h * feature : (h + 1) * feature] for h in range(HEADS)], axis=0
    )


def place_kernel(experts_all, capacity, gated, index_ref, *refs):
    routes_refs, refs = refs[:2], refs[2:]
    if gated:
        gates_refs, refs = refs[:2], refs[2:]
    tokens_refs, blocks = refs[:2], refs[2:]
    rows = routes_refs[0].shape[1]
    me, core = index_ref[0] // SPLIT, index_ref[0] % 2
    slot = iota((experts_all * capacity, rows), 0)
    picks, weight = [], 0.0
    for source in range(2):
        hits = []
        for distance, rank in ranks(me, routes_refs[source], experts_all):
            spot = ((distance >> 1) * 2 + source) * capacity + rank
            hits.append(slot == jnp.where((distance & 1) == core, spot, -1))
        picks.append((hits[0] | hits[1]).astype(jnp.bfloat16))
        if gated:
            gates = by_head(gates_refs[source][...])
            for k in range(2):
                weight = weight + jnp.where(hits[k], gates[k : k + 1], 0.0)
    placed = jnp.dot(
        jnp.concatenate(picks, axis=1),
        jnp.concatenate([stacked(ref) for ref in tokens_refs], axis=0),
        preferred_element_type=jnp.float32,
    )
    if gated:
        placed = jnp.sum(weight, axis=1, keepdims=True) * placed
    placed = placed.astype(jnp.bfloat16)
    for m, block in enumerate(blocks):
        block[...] = placed[2 * m * capacity : 2 * (m + 1) * capacity]


def column(row):
    count = row.shape[1]
    return jnp.sum(
        jnp.where(iota((count, count), 0) == iota((count, count), 1), row, jnp.zeros((), row.dtype)),
        axis=1,
        keepdims=True,
    )


def collect_kernel(experts_all, capacity, gated, index_ref, routes_ref, *refs):
    if gated:
        gates_ref, refs = refs[0], refs[1:]
    blocks, other_ref, out_ref = refs[:-2], refs[-2], refs[-1]
    rows = routes_ref.shape[1]
    feature = out_ref.shape[1] // HEADS
    me, core = index_ref[0] // SPLIT, index_ref[0] % 2
    values = jnp.concatenate([block[:capacity] for block in blocks] + [other_ref[...]], axis=0)
    slot = iota((rows, experts_all * capacity), 1)
    hits = []
    for distance, rank in ranks(me, routes_ref, experts_all):
        far = ((distance & 1) != core).astype(jnp.int32)
        spot = (far * (experts_all // 2) + (distance >> 1)) * capacity + rank
        hits.append(slot == column(spot))
    if gated:
        gates = by_head(gates_ref[...])
        total = sum(
            column(gates[k : k + 1])
            * jnp.dot(
                hits[k].astype(jnp.bfloat16), values, preferred_element_type=jnp.float32
            )
            for k in range(2)
        )
    else:
        total = jnp.dot(
            (hits[0] | hits[1]).astype(jnp.bfloat16), values, preferred_element_type=jnp.float32
        )
    total = total.astype(jnp.bfloat16)
    per_head = rows // HEADS
    for h in range(HEADS):
        out_ref[:, h * feature : (h + 1) * feature] = total[h * per_head : (h + 1) * per_head]


def place(index, routes, gates, tokens, experts_all, capacity):
    feature = tokens[0].shape[1] // HEADS
    operands = [*routes, *gates, *tokens]
    block = jax.ShapeDtypeStruct((2 * capacity, feature), jnp.bfloat16)
    return pl.pallas_call(
        functools.partial(place_kernel, experts_all, capacity, bool(gates)),
        out_shape=[block] * (experts_all // 2),
        in_specs=[pl.BlockSpec(memory_space=pltpu.SMEM)] + [pl.BlockSpec()] * len(operands),
        out_specs=[pl.BlockSpec(memory_space=pltpu.VMEM)] * (experts_all // 2),
        cost_estimate=FREE,
        compiler_params=pltpu.CompilerParams(vmem_limit_bytes=VMEM),
    )(index, *operands)


def collect(index, routes, gates, blocks, other, tok_local, experts_all, capacity):
    feature = other.shape[1]
    vmem = pl.BlockSpec(memory_space=pltpu.VMEM)
    operands = [routes, *gates, *blocks, other]
    return pl.pallas_call(
        functools.partial(collect_kernel, experts_all, capacity, bool(gates)),
        out_shape=jax.ShapeDtypeStruct((tok_local, HEADS * feature), jnp.bfloat16),
        in_specs=[pl.BlockSpec(memory_space=pltpu.SMEM)] + [vmem] * len(operands),
        out_specs=vmem,
        cost_estimate=FREE,
        compiler_params=pltpu.CompilerParams(vmem_limit_bytes=VMEM),
    )(index, *operands)


def dot(a, b, dims):
    return lax.dot_general(a, b, (dims, ((), ())), preferred_element_type=jnp.float32)


def call(kernel, out_shape, *operands):
    vmem = pl.BlockSpec(memory_space=pltpu.VMEM)
    return pl.pallas_call(
        kernel,
        out_shape=[jax.ShapeDtypeStruct(shape, dtype) for shape, dtype in out_shape],
        in_specs=[vmem] * len(operands),
        out_specs=[vmem] * len(out_shape),
        cost_estimate=FREE,
        compiler_params=pltpu.CompilerParams(vmem_limit_bytes=VMEM),
    )(*operands)


def forward_kernel(mine, far, up0, up1, down0, down1, pre0, pre1, hid0, hid1, part, part_far):
    rows = jnp.concatenate([mine[...], far[...]], axis=0)
    total = 0.0
    for up, down, pre, hid in ((up0, down0, pre0, hid0), (up1, down1, pre1, hid1)):
        act = dot(rows, up[...], ((1,), (0,)))
        pre[...] = act
        hidden = (act * jax.nn.sigmoid(act)).astype(jnp.bfloat16)
        hid[...] = hidden
        total = total + dot(hidden, down[...], ((1,), (0,)))
    total = total.astype(jnp.bfloat16)
    part[...] = total[: mine.shape[0]]
    part_far[...] = total[mine.shape[0] :]


def forward(mine, far, weights):
    rows, feature = mine.shape
    block = weights[0].shape[1]
    both = (2 * rows, block)
    pre0, pre1, hid0, hid1, part, part_far = call(
        forward_kernel,
        [(both, jnp.float32)] * 2 + [(both, jnp.bfloat16)] * 2 + [(mine.shape, jnp.bfloat16)] * 2,
        mine,
        far,
        *weights,
    )
    return (pre0, pre1), (hid0, hid1), part, part_far


def backward_kernel(mine, far, pre0, pre1, up0, up1, down0, down1, dpre0, dpre1, back, back_far):
    rows = jnp.concatenate([mine[...], far[...]], axis=0)
    total = 0.0
    for up, down, pre, dpre in ((up0, down0, pre0, dpre0), (up1, down1, pre1, dpre1)):
        grad = (dot(rows, down[...], ((1,), (1,))) * silu_grad(pre[...])).astype(jnp.bfloat16)
        dpre[...] = grad
        total = total + dot(grad, up[...], ((1,), (1,)))
    total = total.astype(jnp.bfloat16)
    back[...] = total[: mine.shape[0]]
    back_far[...] = total[mine.shape[0] :]


def backward(mine, far, pre, weights):
    dpre0, dpre1, back, back_far = call(
        backward_kernel,
        [(pre[0].shape, jnp.bfloat16)] * 2 + [(mine.shape, jnp.bfloat16)] * 2,
        mine,
        far,
        *pre,
        *weights,
    )
    return (dpre0, dpre1), back, back_far


def add_kernel(mine, far, *outs):
    total = (mine[...].astype(jnp.float32) + far[...].astype(jnp.float32)).astype(jnp.bfloat16)
    rows = outs[0].shape[0]
    for i, out in enumerate(outs):
        out[...] = total[i * rows : (i + 1) * rows]


def added(mine, far, group):
    shape = (mine.shape[0] // len(group), mine.shape[1])
    return dict(zip(group, call(add_kernel, [(shape, jnp.bfloat16)] * len(group), mine, far)))


def weight_kernel(lefts, rights, *refs):
    out, both = refs[-1], lefts + rights
    left = jnp.concatenate([ref[...] for ref in refs[:lefts]], axis=0)
    right = jnp.concatenate([ref[...] for ref in refs[lefts:both]], axis=0)
    total = dot(left, right, ((0,), (0,)))
    out[...] = total if len(refs) == both + 1 else total + refs[both][...]


def weight_grad(left, right, *other):
    shape = (left[0].shape[1], right[0].shape[1])
    return call(
        functools.partial(weight_kernel, len(left), len(right)), [(shape, jnp.float32)], *left, *right, *other
    )[0]


def hop(value, line):
    return swap(value, 2 * SPLIT * line, SPLIT)


def on_device(tokens, routes, gates, w_up, w_down, cotangent):
    devices = lax.axis_size("expert")
    experts_all = devices // SPLIT
    tok_local = tokens.shape[0]
    capacity = SPLIT * (
        (6 * HEADS * tok_local + 2 * experts_all * SPLIT - 1) // (2 * experts_all * SPLIT)
    )
    capacity = 16 * ((capacity + 15) // 16)
    index = lax.axis_index("expert").astype(jnp.int32).reshape(1)
    lines = experts_all // 2
    cuts = [0, lines // 2, lines - lines // 4, lines]
    near, mid, far = (list(range(a, b)) for a, b in zip(cuts, cuts[1:]))

    def joined(blocks, group):
        return blocks[group[0]] if len(group) == 1 else jnp.concatenate([blocks[m] for m in group])

    order = Order()

    def hops(blocks, group):
        return {m: order.begin(hop, blocks[m], m) for m in group}

    def come(sent):
        return dict(zip(sent, jax.tree.leaves(order.wait(*sent.values()))))

    def across(value):
        return order.begin(swap, value, 2)

    def core(value):
        return order.begin(swap, value, 1)

    def halves(blocks):
        return jnp.concatenate([blocks[m][capacity:] for m in sorted(blocks)])

    def ordered(blocks):
        return [blocks[m] for m in sorted(blocks)]

    sizes = (tok_local, experts_all, capacity)
    up_own, down_own = w_up[0], w_down[0]
    routes, gates = routes.T, gates.T

    tokens_other, routes_other = order.wait(core(tokens), core(routes))
    routes_both = (routes, routes_other)
    x_blocks = place(index, routes_both, (), (tokens, tokens_other), experts_all, capacity)
    order.done(x_blocks[0])
    x_near, x_mid, x_far, up_other = (
        hops(x_blocks, near), hops(x_blocks, mid), hops(x_blocks, far), core(up_own)
    )
    x0 = joined(come(x_near), near)
    x0_far, down_other = across(x0), core(down_own)
    up_other, down_other = order.wait(up_other, down_other)
    weights = (up_own, up_other, down_own, down_other)
    cotangent_other, gates_other = order.wait(core(cotangent), core(gates))
    g_blocks = place(
        index,
        routes_both,
        (gates, gates_other),
        (cotangent, cotangent_other),
        experts_all,
        capacity,
    )
    order.done(g_blocks[0])
    x1 = joined(come(x_mid), mid)
    x1_far, g_far = across(x1), hops(g_blocks, far)
    pre0, hid0, part0, part0_far = forward(x0, order.wait(x0_far), weights)
    order.done(part0_far)
    m0_far = across(part0_far)
    x2 = joined(come(x_far), far)
    x2_far, g_mid = across(x2), hops(g_blocks, mid)
    pre1, hid1, part1, part1_far = forward(x1, order.wait(x1_far), weights)
    order.done(part1_far)
    m1_far = across(part1_far)
    pre2, hid2, part2, part2_far = forward(x2, order.wait(x2_far), weights)
    order.done(part2_far)
    m2_far = across(part2_far)

    g2 = joined(come(g_far), far)
    g_near = hops(g_blocks, near[1:])
    m_sum = added(part0, order.wait(m0_far), near)
    order.done(m_sum[near[0]])
    g2_far = across(g2)
    g1 = joined(come(g_mid), mid)
    g_near |= hops(g_blocks, near[:1])
    g0 = joined(come(g_near), near)
    m_near = hops(m_sum, near)
    m_sum |= added(part1, order.wait(m1_far), mid)
    order.done(m_sum[mid[0]])
    g1_far = across(g1)
    m_home = come(m_near)
    m_mid = hops(m_sum, mid)
    m_sum |= added(part2, order.wait(m2_far), far)
    order.done(m_sum[far[0]])
    m_far, g0_far = hops(m_sum, far), across(g0)
    g2_far = order.wait(g2_far)
    dpre2, back2, back2_far = backward(g2, g2_far, pre2, weights)
    order.done(back2_far)
    b2_far = across(back2_far)
    g1_far = order.wait(g1_far)
    dpre1, back1, back1_far = backward(g1, g1_far, pre1, weights)
    order.done(back1_far)
    b1_far = across(back1_far)
    m_home |= come(m_mid)
    m_home |= come(m_far)
    m_other = core(halves(m_home))

    b_sum = added(back2, order.wait(b2_far), far)
    order.done(b_sum[far[0]])
    b_far = hops(b_sum, far)
    g0_far = order.wait(g0_far)
    dpre0, back0, back0_far = backward(g0, g0_far, pre0, weights)
    order.done(back0_far)
    b0_far = across(back0_far)
    mixed = collect(index, routes, (gates,), ordered(m_home), order.wait(m_other), *sizes)
    order.done(mixed)

    x_all = (x0, x0_far, x1, x1_far, x2, x2_far)
    g_all = (g0, g0_far, g1, g1_far, g2, g2_far)
    hid, dpre = zip(hid0, hid1, hid2), zip(dpre0, dpre1, dpre2)
    (hid_own, hid_other), (dpre_own, dpre_other) = hid, dpre
    down_part = weight_grad(hid_other, g_all)
    order.done(down_part)
    down_sent = core(down_part)
    up_part = weight_grad(x_all, dpre_other)
    order.done(up_part)
    up_sent = core(up_part)
    b_sum |= added(back1, order.wait(b1_far), mid)
    order.done(b_sum[mid[0]])
    b_mid = hops(b_sum, mid)
    grad_down = weight_grad(hid_own, g_all, order.wait(down_sent))
    order.done(grad_down)
    grad_up = weight_grad(x_all, dpre_own, order.wait(up_sent))
    order.done(grad_up)
    b_sum |= added(back0, order.wait(b0_far), near)
    order.done(b_sum[near[0]])
    b_home = come(b_far | b_mid | hops(b_sum, near))
    b_other = order.wait(core(halves(b_home)))
    token_grad = collect(index, routes, (), ordered(b_home), b_other, *sizes)
    return (mixed, token_grad, grad_up[None], grad_down[None])


def solution(mesh):
    placed = (
        P(("groups", "expert"), None),
        P(("groups", "expert"), None),
        P(("groups", "expert"), None),
        P("expert", None, None),
        P("expert", None, None),
        P(("groups", "expert"), None),
    )
    return jax.shard_map(
        on_device,
        mesh=mesh,
        in_specs=placed,
        out_specs=(
            P(("groups", "expert"), None),
            P(("groups", "expert"), None),
            P(("groups", "expert"), None, None),
            P(("groups", "expert"), None, None),
        ),
        check_vma=False,
    )
```

time: 235 us -> 185 us (0.79)
  waiting for transfers between devices: 139 us -> 104 us
  matrix products: 23 us -> 0 us
  Pallas kernels: 5.26 us -> 27.8 us
  starting transfers between devices: 60.7 us -> 48.3 us
    ppermute x42 -> x38, waiting for transfers between devices: 139 us -> 104 us  [swap(): lax.ppermute(value, 'expert', [(i, i ^ bits ^ (odd_bits if i % 2 else 0))...]
    dot_general x12 -> x0, matrix products: 23 us -> none  [dot(): lax.dot_general(a, b, (dims, ((), ())), preferred_element_type=jnp.float32)]
    pallas_call x4 -> x20, Pallas kernels: 5.26 us -> 27.8 us  [the longest x16 22.4 us: call(): pl.pallas_call(kernel, out_shape=[jax.ShapeDtypeStruct(shape, dtype) for...]
    ppermute x42 -> x38, starting transfers between devices: 60.7 us -> 48.3 us  [swap(): lax.ppermute(value, 'expert', [(i, i ^ bits ^ (odd_bits if i % 2 else 0))...]
  transfers between devices with their start and end apart: 42 -> 38, of which waited for: 22 -> 17; matrix products, arithmetic and copies ran while one was open for 9% -> 0% of each run, Pallas kernels for 2% -> 13%
where the time goes in v2:
time: 185 us; the launch traced here: 184 us
  waiting for transfers between devices  104 us (56%)
  starting transfers between devices  48.3 us (26%)
  Pallas kernels  27.8 us (15%)
  local copies, waits for them, and re-layouts  3.28 us (2%)
    ppermute x38, waiting for transfers between devices, swap(): lax.ppermute(value, 'expert', [(i, i ^ bits ^ (odd_bits if i % 2 else 0))...  104 us
    ppermute x38, starting transfers between devices, swap(): lax.ppermute(value, 'expert', [(i, i ^ bits ^ (odd_bits if i % 2 else 0))...  48.3 us
    pallas_call x16, Pallas kernels, call(): pl.pallas_call(kernel, out_shape=[jax.ShapeDtypeStruct(shape, dtype) for...  22.4 us
  transfers between devices with their start and end apart: 38, of which 17 were waited for; matrix products, arithmetic and copies ran while one was open for 0% of the time, Pallas kernels for 13%

profile of v2, /device:TPU:0, one launch (start us, length us, event | category | flops | bytes accessed | tf_op | source)
XLA Modules:
  0.0 184.4 jit_solution(2774146760570755145)
XLA Ops:
  6.3 3.0 %collective-permute-start.3 = (bf16[96,1536]{1,0:T(8,128)(2,1)S(1)}, bf16[96,1536]{1,0:T(8,128)(2,1)S(1)}, u32[]{:S(2)}, u32[]{:S(2)}) collective-permute-start(bf16[96,1536]{1,0:T(8,128)(2,1)S(1)} %get-tuple-element.124), channel_id=1, source_target_pairs={{0,8},{1,13},{2,10},{3,15},{4,12},{5,9},{6,14},{7,11},{8,0},{9,5},... | collective-permute-start | bytes 884744 | tf_op jit(solution)/shard_map/ppermute | solution.py:17
  9.3 2.3 %collective-permute-start.6 = (bf16[1536,512]{1,0:T(8,128)(2,1)}, bf16[1536,512]{1,0:T(8,128)(2,1)S(1)}, u32[]{:S(2)}, u32[]{:S(2)}) collective-permute-start(bf16[1536,512]{1,0:T(8,128)(2,1)} %bitcast.7), channel_id=1, source_target_pairs={{0,1},{1,0},{2,3},{3,2},{4,5},{5,4},{6,7},{7,6},{8,9},{9,8},{10,11... | collective-permute-start | bytes 4718600 | tf_op jit(solution)/shard_map/ppermute | solution.py:17
  11.5 3.6 %collective-permute-done.3 = bf16[96,1536]{1,0:T(8,128)(2,1)S(1)} collective-permute-done((bf16[96,1536]{1,0:T(8,128)(2,1)S(1)}, bf16[96,1536]{1,0:T(8,128)(2,1)S(1)}, u32[]{:S(2)}, u32[]{:S(2)}) %collective-permute-start.3) | collective-permute-done | bytes 294944 | tf_op jit(solution)/shard_map/ppermute | solution.py:17
  15.1 3.2 %collective-permute-start.7 = (bf16[512,1536]{1,0:T(8,128)(2,1)}, bf16[512,1536]{1,0:T(8,128)(2,1)S(1)}, u32[]{:S(2)}, u32[]{:S(2)}) collective-permute-start(bf16[512,1536]{1,0:T(8,128)(2,1)} %bitcast.14), channel_id=1, source_target_pairs={{0,1},{1,0},{2,3},{3,2},{4,5},{5,4},{6,7},{7,6},{8,9},{9,8},{10,11... | collective-permute-start | bytes 4718600 | tf_op jit(solution)/shard_map/ppermute | solution.py:17
  22.0 2.6 %collective-permute-start.5 = (bf16[96,1536]{1,0:T(8,128)(2,1)S(1)}, bf16[96,1536]{1,0:T(8,128)(2,1)S(1)}, u32[]{:S(2)}, u32[]{:S(2)}) collective-permute-start(bf16[96,1536]{1,0:T(8,128)(2,1)S(1)} %get-tuple-element.129), channel_id=1, source_target_pairs={{0,16},{1,21},{2,18},{3,23},{4,20},{5,17},{6,22},{7,19},{8,24},{9,... | collective-permute-start | bytes 884744 | tf_op jit(solution)/shard_map/ppermute | solution.py:17
  27.1 18.2 %collective-permute-done.5.mine.refs_2_ = bf16[96,1536]{1,0:T(8,128)(2,1)S(1)} collective-permute-done((bf16[96,1536]{1,0:T(8,128)(2,1)S(1)}, bf16[96,1536]{1,0:T(8,128)(2,1)S(1)}, u32[]{:S(2)}, u32[]{:S(2)}) %collective-permute-start.5) | collective-permute-done | bytes 294944 | tf_op jit(solution)/shard_map/ppermute | solution.py:17
  46.7 2.7 %shard_map.95 = (f32[384,512]{1,0:T(8,128)S(1)}, f32[384,512]{1,0:T(8,128)S(1)}, bf16[384,512]{1,0:T(8,128)(2,1)S(1)}, bf16[384,512]{1,0:T(8,128)(2,1)S(1)}, bf1...) custom-call(bf16[192,1536]{1,0:T(8,128)(2,1)S(1)} %constant_dynamic-update-slice_fusion.mine.refs_0_, ...), custom_call_target="tpu_custom_call" | custom-call | flops 1 | bytes 1 | tf_op jit(solution)/shard_map/pallas_call | solution.py:199
  53.0 3.1 %collective-permute-start.11 = (bf16[96,1536]{1,0:T(8,128)(2,1)S(1)}, bf16[96,1536]{1,0:T(8,128)(2,1)S(1)}, u32[]{:S(2)}, u32[]{:S(2)}) collective-permute-start(bf16[96,1536]{1,0:T(8,128)(2,1)S(1)} %get-tuple-element.145), channel_id=1, source_target_pairs={{0,24},{1,29},{2,26},{3,31},{4,28},{5,25},{6,30},{7,27},{8,16},{9,... | collective-permute-start | bytes 884744 | tf_op jit(solution)/shard_map/ppermute | solution.py:17
  56.1 15.9 %collective-permute-done.14.far.refs_3_ = bf16[96,1536]{1,0:T(8,128)(2,1)S(1)} collective-permute-done((bf16[96,1536]{1,0:T(8,128)(2,1)S(1)}, bf16[96,1536]{1,0:T(8,128)(2,1)S(1)}, u32[]{:S(2)}, u32[]{:S(2)}) %collective-permute-start.14) | collective-permute-done | bytes 294944 | tf_op jit(solution)/shard_map/ppermute | solution.py:17
  73.5 3.5 %collective-permute-done.13.far.refs_5_ = bf16[96,1536]{1,0:T(8,128)(2,1)S(1)} collective-permute-done((bf16[96,1536]{1,0:T(8,128)(2,1)S(1)}, bf16[96,1536]{1,0:T(8,128)(2,1)S(1)}, u32[]{:S(2)}, u32[]{:S(2)}) %collective-permute-start.13) | collective-permute-done | bytes 294944 | tf_op jit(solution)/shard_map/ppermute | solution.py:17
  79.4 2.2 %collective-permute-done.16.mine.refs_5_ = bf16[96,1536]{1,0:T(8,128)(2,1)S(1)} collective-permute-done((bf16[96,1536]{1,0:T(8,128)(2,1)S(1)}, bf16[96,1536]{1,0:T(8,128)(2,1)S(1)}, u32[]{:S(2)}, u32[]{:S(2)}) %collective-permute-start.16) | collective-permute-done | bytes 294944 | tf_op jit(solution)/shard_map/ppermute | solution.py:17
  84.9 2.9 %collective-permute-done.15 = bf16[96,1536]{1,0:T(8,128)(2,1)S(1)} collective-permute-done((bf16[96,1536]{1,0:T(8,128)(2,1)S(1)}, bf16[96,1536]{1,0:T(8,128)(2,1)S(1)}, u32[]{:S(2)}, u32[]{:S(2)}) %collective-permute-start.15) | collective-permute-done | bytes 294944 | tf_op jit(solution)/shard_map/ppermute | solution.py:17
  89.0 2.3 %collective-permute-done.20.far = bf16[96,1536]{1,0:T(8,128)(2,1)S(1)} collective-permute-done((bf16[96,1536]{1,0:T(8,128)(2,1)S(1)}, bf16[96,1536]{1,0:T(8,128)(2,1)S(1)}, u32[]{:S(2)}, u32[]{:S(2)}) %collective-permute-start.20) | collective-permute-done | bytes 294944 | tf_op jit(solution)/shard_map/ppermute | solution.py:17
  91.4 4.1 %collective-permute-done.19.refs_2_ = bf16[96,1536]{1,0:T(8,128)(2,1)S(1)} collective-permute-done((bf16[96,1536]{1,0:T(8,128)(2,1)S(1)}, bf16[96,1536]{1,0:T(8,128)(2,1)S(1)}, u32[]{:S(2)}, u32[]{:S(2)}) %collective-permute-start.19) | collective-permute-done | bytes 294944 | tf_op jit(solution)/shard_map/ppermute | solution.py:17
  95.5 2.1 %collective-permute-done.24.far = bf16[96,1536]{1,0:T(8,128)(2,1)S(1)} collective-permute-done((bf16[96,1536]{1,0:T(8,128)(2,1)S(1)}, bf16[96,1536]{1,0:T(8,128)(2,1)S(1)}, u32[]{:S(2)}, u32[]{:S(2)}) %collective-permute-start.24) | collective-permute-done | bytes 294944 | tf_op jit(solution)/shard_map/ppermute | solution.py:17
  99.8 1.8 collective-permute-start.21
  101.5 2.4 %collective-permute-done.23.far.refs_8_ = bf16[96,1536]{1,0:T(8,128)(2,1)S(1)} collective-permute-done((bf16[96,1536]{1,0:T(8,128)(2,1)S(1)}, bf16[96,1536]{1,0:T(8,128)(2,1)S(1)}, u32[]{:S(2)}, u32[]{:S(2)}) %collective-permute-start.23) | collective-permute-done | bytes 294944 | tf_op jit(solution)/shard_map/ppermute | solution.py:17
  103.9 3.1 %collective-permute-start.25 = (bf16[96,1536]{1,0:T(8,128)(2,1)S(1)}, bf16[96,1536]{1,0:T(8,128)(2,1)S(1)}, u32[]{:S(2)}, u32[]{:S(2)}) collective-permute-start(bf16[96,1536]{1,0:T(8,128)(2,1)S(1)} %shard_map.100), channel_id=1, source_target_pairs={{0,24},{1,29},{2,26},{3,31},{4,28},{5,25},{6,30},{7,27},{8,16},{9,... | collective-permute-start | bytes 884744 | tf_op jit(solution)/shard_map/ppermute | solution.py:17
  107.0 2.2 %shard_map.101 = (bf16[192,512]{1,0:T(8,128)(2,1)S(1)}, bf16[192,512]{1,0:T(8,128)(2,1)S(1)}, bf16[96,1536]{1,0:T(8,128)(2,1)S(1)}, bf16[96,1536]{1,0:T(8,128)(2,1)S(1)}) custom-call(bf16[96,1536]{1,0:T(8,128)(2,1)S(1)} %collective-permute-done.11.mine.refs_7_, bf16[96,1536]{1,0:T(8,128)(2,1)S(1)} %collective-permute-done.23.far.refs_8_, ...), custom_call_target="tpu_custom_call" | custom-call | flops 1 | bytes 1 | tf_op jit(solution)/shard_map/pallas_call | solution.py:199
  109.9 13.0 %collective-permute-done.22.far.refs_6_ = bf16[96,1536]{1,0:T(8,128)(2,1)S(1)} collective-permute-done((bf16[96,1536]{1,0:T(8,128)(2,1)S(1)}, bf16[96,1536]{1,0:T(8,128)(2,1)S(1)}, u32[]{:S(2)}, u32[]{:S(2)}) %collective-permute-start.22) | collective-permute-done | bytes 294944 | tf_op jit(solution)/shard_map/ppermute | solution.py:17
  122.9 2.2 %shard_map.102 = (bf16[192,512]{1,0:T(8,128)(2,1)S(1)}, bf16[192,512]{1,0:T(8,128)(2,1)S(1)}, bf16[96,1536]{1,0:T(8,128)(2,1)S(1)}, bf16[96,1536]{1,0:T(8,128)(2,1)S(1)}) custom-call(bf16[96,1536]{1,0:T(8,128)(2,1)S(1)} %collective-permute-done.16.mine.refs_5_, bf16[96,1536]{1,0:T(8,128)(2,1)S(1)} %collective-permute-done.22.far.refs_6_, ...), custom_call_target="tpu_custom_call" | custom-call | flops 1 | bytes 1 | tf_op jit(solution)/shard_map/pallas_call | solution.py:199
  125.1 4.1 %collective-permute-done.28.far = bf16[96,1536]{1,0:T(8,128)(2,1)S(1)} collective-permute-done((bf16[96,1536]{1,0:T(8,128)(2,1)S(1)}, bf16[96,1536]{1,0:T(8,128)(2,1)S(1)}, u32[]{:S(2)}, u32[]{:S(2)}) %collective-permute-start.28) | collective-permute-done | bytes 294944 | tf_op jit(solution)/shard_map/ppermute | solution.py:17
  131.5 2.8 %shard_map.104 = (bf16[384,512]{1,0:T(8,128)(2,1)S(1)}, bf16[384,512]{1,0:T(8,128)(2,1)S(1)}, bf16[192,1536]{1,0:T(8,128)(2,1)S(1)}, bf16[192,1536]{1,0:T(8,128)(2,1)S(1)}) custom-call(bf16[192,1536]{1,0:T(8,128)(2,1)S(1)} %constant_dynamic-update-slice_fusion.2.mine.refs_3_, bf16[192,1536]{1,0:T(8,128)(2,1)S(1)} %collective-permute-done.27.far.refs_4_, ...), custom_call_target="tpu_custom_call" | custom-call | flops 1 | bytes 1 | tf_op jit(solution)/shard_map/pallas_call | solution.py:199
  137.9 2.8 %collective-permute-start.29 = (bf16[96,1536]{1,0:T(8,128)(2,1)S(1)}, bf16[96,1536]{1,0:T(8,128)(2,1)S(1)}, u32[]{:S(2)}, u32[]{:S(2)}) collective-permute-start(bf16[96,1536]{1,0:T(8,128)(2,1)S(1)} %shard_map.103), channel_id=1, source_target_pairs={{0,24},{1,29},{2,26},{3,31},{4,28},{5,25},{6,30},{7,27},{8,16},{9,... | collective-permute-start | bytes 884744 | tf_op jit(solution)/shard_map/ppermute | solution.py:17
  140.7 17.1 %collective-permute-done.30.far = bf16[96,1536]{1,0:T(8,128)(2,1)S(1)} collective-permute-done((bf16[96,1536]{1,0:T(8,128)(2,1)S(1)}, bf16[96,1536]{1,0:T(8,128)(2,1)S(1)}, u32[]{:S(2)}, u32[]{:S(2)}) %collective-permute-start.30) | collective-permute-done | bytes 294944 | tf_op jit(solution)/shard_map/ppermute | solution.py:17
  157.9 1.8 collective-permute-start.31
  159.8 3.1 %shard_map.109 = f32[512,1536]{1,0:T(8,128)} custom-call(bf16[384,512]{1,0:T(8,128)(2,1)S(1)} %get-tuple-element.215.refs_0_, bf16[192,512]{1,0:T(8,128)(2,1)S(1)} %get-tuple-element.216.refs_1_, bf16[192,512]{1,0:T(8,128)(2,1)S(1)} %get-tuple-element.217.refs_2_, bf16[192,1536]{1,0:T(8,128)(2,1)S(1)} %constant_dynamic-update-slice_fusion.2.mine.refs_3_, ...), custom_call_target="tpu_custom_call" | custom-call | flops 1 | bytes 1 | tf_op jit(solution)/shard_map/pallas_call | solution.py:199
  162.9 3.1 %shard_map.110 = f32[1536,512]{1,0:T(8,128)} custom-call(bf16[192,1536]{1,0:T(8,128)(2,1)S(1)} %constant_dynamic-update-slice_fusion.mine.refs_0_, bf16[192,1536]{1,0:T(8,128)(2,1)S(1)} %collective-permute-done.4.far.refs_1_, bf16[96,1536]{1,0:T(8,128)(2,1)S(1)} %collective-permute-done.5.mine.refs_2_, ...), custom_call_target="tpu_custom_call" | custom-call | flops 1 | bytes 1 | tf_op jit(solution)/shard_map/pallas_call | solution.py:199
  168.6 2.2 %collective-permute-start.26 = (bf16[192,1536]{1,0:T(8,128)(2,1)S(1)}, bf16[192,1536]{1,0:T(8,128)(2,1)S(1)}, u32[]{:S(2)}, u32[]{:S(2)}) collective-permute-start(bf16[192,1536]{1,0:T(8,128)(2,1)S(1)} %pad_maximum_fusion), channel_id=1, source_target_pairs={{0,1},{1,0},{2,3},{3,2},{4,5},{5,4},{6,7},{7,6},{8,9},{9,8},{10,11... | collective-permute-start | bytes 1769480 | tf_op jit(solution)/shard_map/ppermute | solution.py:17
  170.8 3.1 %collective-permute-done.31.refs_2_ = bf16[96,1536]{1,0:T(8,128)(2,1)S(1)} collective-permute-done((bf16[96,1536]{1,0:T(8,128)(2,1)S(1)}, bf16[96,1536]{1,0:T(8,128)(2,1)S(1)}, u32[]{:S(2)}, u32[]{:S(2)}) %collective-permute-start.31) | collective-permute-done | bytes 294944 | tf_op jit(solution)/shard_map/ppermute | solution.py:17
  173.9 6.1 %collective-permute-done.36.refs_1_ = bf16[96,1536]{1,0:T(8,128)(2,1)S(1)} collective-permute-done((bf16[96,1536]{1,0:T(8,128)(2,1)S(1)}, bf16[96,1536]{1,0:T(8,128)(2,1)S(1)}, u32[]{:S(2)}, u32[]{:S(2)}) %collective-permute-start.36) | collective-permute-done | bytes 294944 | tf_op jit(solution)/shard_map/ppermute | solution.py:17
  181.0 1.8 shard_map.105
  (94 shorter events, 38.9 us)
Async XLA Ops:
  5.4 6.1 %collective-permute-start.2 = (bf16[96,1536]{1,0:T(8,128)(2,1)S(1)}, bf16[96,1536]{1,0:T(8,128)(2,1)S(1)}, u32[]{:S(2)}, u32[]{:S(2)}) collective-permute-start(bf16[96,1536]{1,0:T(8,128)(2,1)S(1)} %get-tuple-element.122), channel_id=1, source_target_pairs={{0,0},{1,5},{2,2},{3,7},{4,4},{5,1},{6,6},{7,3},{8,8},{9,13},{10,1... | collective-permute-start | bytes 884744 | tf_op jit(solution)/shard_map/ppermute | solution.py:17
  6.3 8.9 %collective-permute-start.3 = (bf16[96,1536]{1,0:T(8,128)(2,1)S(1)}, bf16[96,1536]{1,0:T(8,128)(2,1)S(1)}, u32[]{:S(2)}, u32[]{:S(2)}) collective-permute-start(bf16[96,1536]{1,0:T(8,128)(2,1)S(1)} %get-tuple-element.124), channel_id=1, source_target_pairs={{0,8},{1,13},{2,10},{3,15},{4,12},{5,9},{6,14},{7,11},{8,0},{9,5},... | collective-permute-start | bytes 884744 | tf_op jit(solution)/shard_map/ppermute | solution.py:17
  9.3 10.7 %collective-permute-start.6 = (bf16[1536,512]{1,0:T(8,128)(2,1)}, bf16[1536,512]{1,0:T(8,128)(2,1)S(1)}, u32[]{:S(2)}, u32[]{:S(2)}) collective-permute-start(bf16[1536,512]{1,0:T(8,128)(2,1)} %bitcast.7), channel_id=1, source_target_pairs={{0,1},{1,0},{2,3},{3,2},{4,5},{5,4},{6,7},{7,6},{8,9},{9,8},{10,11... | collective-permute-start | bytes 4718600 | tf_op jit(solution)/shard_map/ppermute | solution.py:17
  15.1 6.5 %collective-permute-start.7 = (bf16[512,1536]{1,0:T(8,128)(2,1)}, bf16[512,1536]{1,0:T(8,128)(2,1)S(1)}, u32[]{:S(2)}, u32[]{:S(2)}) collective-permute-start(bf16[512,1536]{1,0:T(8,128)(2,1)} %bitcast.14), channel_id=1, source_target_pairs={{0,1},{1,0},{2,3},{3,2},{4,5},{5,4},{6,7},{7,6},{8,9},{9,8},{10,11... | collective-permute-start | bytes 4718600 | tf_op jit(solution)/shard_map/ppermute | solution.py:17
  18.4 26.9 %collective-permute-start.4 = (bf16[192,1536]{1,0:T(8,128)(2,1)S(1)}, bf16[192,1536]{1,0:T(8,128)(2,1)S(1)}, u32[]{:S(2)}, u32[]{:S(2)}) collective-permute-start(bf16[192,1536]{1,0:T(8,128)(2,1)S(1)} %constant_dynamic-update-slice_fusion.mine.refs_0_), channel_id=1, source_target_pairs={{0,2},{1,3},{2,0},{3,1},{4,6},{5,7},{6,4},{7,5},{8,10},{9,11},{10,... | collective-permute-start | bytes 1769480 | tf_op jit(solution)/shard_map/ppermute | solution.py:17
  22.0 23.3 %collective-permute-start.5 = (bf16[96,1536]{1,0:T(8,128)(2,1)S(1)}, bf16[96,1536]{1,0:T(8,128)(2,1)S(1)}, u32[]{:S(2)}, u32[]{:S(2)}) collective-permute-start(bf16[96,1536]{1,0:T(8,128)(2,1)S(1)} %get-tuple-element.129), channel_id=1, source_target_pairs={{0,16},{1,21},{2,18},{3,23},{4,20},{5,17},{6,22},{7,19},{8,24},{9,... | collective-permute-start | bytes 884744 | tf_op jit(solution)/shard_map/ppermute | solution.py:17
  24.7 26.8 %collective-permute-start.12 = (bf16[96,1536]{1,0:T(8,128)(2,1)S(1)}, bf16[96,1536]{1,0:T(8,128)(2,1)S(1)}, u32[]{:S(2)}, u32[]{:S(2)}) collective-permute-start(bf16[96,1536]{1,0:T(8,128)(2,1)S(1)} %get-tuple-element.147), channel_id=1, source_target_pairs={{0,24},{1,29},{2,26},{3,31},{4,28},{5,25},{6,30},{7,27},{8,16},{9,... | collective-permute-start | bytes 884744 | tf_op jit(solution)/shard_map/ppermute | solution.py:17
  49.4 29.8 %collective-permute-start.10 = (bf16[192,1536]{1,0:T(8,128)(2,1)S(1)}, bf16[192,1536]{1,0:T(8,128)(2,1)S(1)}, u32[]{:S(2)}, u32[]{:S(2)}) collective-permute-start(bf16[192,1536]{1,0:T(8,128)(2,1)S(1)} %get-tuple-element.143), channel_id=1, source_target_pairs={{0,2},{1,3},{2,0},{3,1},{4,6},{5,7},{6,4},{7,5},{8,10},{9,11},{10,... | collective-permute-start | bytes 1769480 | tf_op jit(solution)/shard_map/ppermute | solution.py:17
  51.0 21.1 %collective-permute-start.14 = (bf16[96,1536]{1,0:T(8,128)(2,1)S(1)}, bf16[96,1536]{1,0:T(8,128)(2,1)S(1)}, u32[]{:S(2)}, u32[]{:S(2)}) collective-permute-start(bf16[96,1536]{1,0:T(8,128)(2,1)S(1)} %collective-permute-done.5.mine.refs_2_), channel_id=1, source_target_pairs={{0,2},{1,3},{2,0},{3,1},{4,6},{5,7},{6,4},{7,5},{8,10},{9,11},{10,... | collective-permute-start | bytes 884744 | tf_op jit(solution)/shard_map/ppermute | solution.py:17
  51.5 25.5 %collective-permute-start.13 = (bf16[96,1536]{1,0:T(8,128)(2,1)S(1)}, bf16[96,1536]{1,0:T(8,128)(2,1)S(1)}, u32[]{:S(2)}, u32[]{:S(2)}) collective-permute-start(bf16[96,1536]{1,0:T(8,128)(2,1)S(1)} %collective-permute-done.12.mine.refs_4_), channel_id=1, source_target_pairs={{0,2},{1,3},{2,0},{3,1},{4,6},{5,7},{6,4},{7,5},{8,10},{9,11},{10,... | collective-permute-start | bytes 884744 | tf_op jit(solution)/shard_map/ppermute | solution.py:17
  53.0 25.6 %collective-permute-start.11 = (bf16[96,1536]{1,0:T(8,128)(2,1)S(1)}, bf16[96,1536]{1,0:T(8,128)(2,1)S(1)}, u32[]{:S(2)}, u32[]{:S(2)}) collective-permute-start(bf16[96,1536]{1,0:T(8,128)(2,1)S(1)} %get-tuple-element.145), channel_id=1, source_target_pairs={{0,24},{1,29},{2,26},{3,31},{4,28},{5,25},{6,30},{7,27},{8,16},{9,... | collective-permute-start | bytes 884744 | tf_op jit(solution)/shard_map/ppermute | solution.py:17
  56.1 25.5 %collective-permute-start.16 = (bf16[96,1536]{1,0:T(8,128)(2,1)S(1)}, bf16[96,1536]{1,0:T(8,128)(2,1)S(1)}, u32[]{:S(2)}, u32[]{:S(2)}) collective-permute-start(bf16[96,1536]{1,0:T(8,128)(2,1)S(1)} %get-tuple-element.161), channel_id=1, source_target_pairs={{0,16},{1,21},{2,18},{3,23},{4,20},{5,17},{6,22},{7,19},{8,24},{9,... | collective-permute-start | bytes 884744 | tf_op jit(solution)/shard_map/ppermute | solution.py:17
  78.6 9.3 %collective-permute-start.15 = (bf16[96,1536]{1,0:T(8,128)(2,1)S(1)}, bf16[96,1536]{1,0:T(8,128)(2,1)S(1)}, u32[]{:S(2)}, u32[]{:S(2)}) collective-permute-start(bf16[96,1536]{1,0:T(8,128)(2,1)S(1)} %get-tuple-element.159), channel_id=1, source_target_pairs={{0,8},{1,13},{2,10},{3,15},{4,12},{5,9},{6,14},{7,11},{8,0},{9,5},... | collective-permute-start | bytes 884744 | tf_op jit(solution)/shard_map/ppermute | solution.py:17
  81.6 6.2 %collective-permute-start.17 = (bf16[96,1536]{1,0:T(8,128)(2,1)S(1)}, bf16[96,1536]{1,0:T(8,128)(2,1)S(1)}, u32[]{:S(2)}, u32[]{:S(2)}) collective-permute-start(bf16[96,1536]{1,0:T(8,128)(2,1)S(1)} %get-tuple-element.163), channel_id=1, source_target_pairs={{0,0},{1,5},{2,2},{3,7},{4,4},{5,1},{6,6},{7,3},{8,8},{9,13},{10,1... | collective-permute-start | bytes 884744 | tf_op jit(solution)/shard_map/ppermute | solution.py:17
  82.3 9.0 %collective-permute-start.20 = (bf16[96,1536]{1,0:T(8,128)(2,1)S(1)}, bf16[96,1536]{1,0:T(8,128)(2,1)S(1)}, u32[]{:S(2)}, u32[]{:S(2)}) collective-permute-start(bf16[96,1536]{1,0:T(8,128)(2,1)S(1)} %get-tuple-element.169), channel_id=1, source_target_pairs={{0,2},{1,3},{2,0},{3,1},{4,6},{5,7},{6,4},{7,5},{8,10},{9,11},{10,... | collective-permute-start | bytes 884744 | tf_op jit(solution)/shard_map/ppermute | solution.py:17
  82.9 14.7 %collective-permute-start.24 = (bf16[96,1536]{1,0:T(8,128)(2,1)S(1)}, bf16[96,1536]{1,0:T(8,128)(2,1)S(1)}, u32[]{:S(2)}, u32[]{:S(2)}) collective-permute-start(bf16[96,1536]{1,0:T(8,128)(2,1)S(1)} %get-tuple-element.177), channel_id=1, source_target_pairs={{0,2},{1,3},{2,0},{3,1},{4,6},{5,7},{6,4},{7,5},{8,10},{9,11},{10,... | collective-permute-start | bytes 884744 | tf_op jit(solution)/shard_map/ppermute | solution.py:17
  84.4 19.5 %collective-permute-start.23 = (bf16[96,1536]{1,0:T(8,128)(2,1)S(1)}, bf16[96,1536]{1,0:T(8,128)(2,1)S(1)}, u32[]{:S(2)}, u32[]{:S(2)}) collective-permute-start(bf16[96,1536]{1,0:T(8,128)(2,1)S(1)} %collective-permute-done.11.mine.refs_7_), channel_id=1, source_target_pairs={{0,2},{1,3},{2,0},{3,1},{4,6},{5,7},{6,4},{7,5},{8,10},{9,11},{10,... | collective-permute-start | bytes 884744 | tf_op jit(solution)/shard_map/ppermute | solution.py:17
  88.7 6.8 %collective-permute-start.19 = (bf16[96,1536]{1,0:T(8,128)(2,1)S(1)}, bf16[96,1536]{1,0:T(8,128)(2,1)S(1)}, u32[]{:S(2)}, u32[]{:S(2)}) collective-permute-start(bf16[96,1536]{1,0:T(8,128)(2,1)S(1)} %get-tuple-element.167), channel_id=1, source_target_pairs={{0,8},{1,13},{2,10},{3,15},{4,12},{5,9},{6,14},{7,11},{8,0},{9,5},... | collective-permute-start | bytes 884744 | tf_op jit(solution)/shard_map/ppermute | solution.py:17
  97.7 31.6 %collective-permute-start.27 = (bf16[192,1536]{1,0:T(8,128)(2,1)S(1)}, bf16[192,1536]{1,0:T(8,128)(2,1)S(1)}, u32[]{:S(2)}, u32[]{:S(2)}) collective-permute-start(bf16[192,1536]{1,0:T(8,128)(2,1)S(1)} %constant_dynamic-update-slice_fusion.2.mine.refs_3_), channel_id=1, source_target_pairs={{0,2},{1,3},{2,0},{3,1},{4,6},{5,7},{6,4},{7,5},{8,10},{9,11},{10,... | collective-permute-start | bytes 1769480 | tf_op jit(solution)/shard_map/ppermute | solution.py:17
  98.3 24.6 %collective-permute-start.22 = (bf16[96,1536]{1,0:T(8,128)(2,1)S(1)}, bf16[96,1536]{1,0:T(8,128)(2,1)S(1)}, u32[]{:S(2)}, u32[]{:S(2)}) collective-permute-start(bf16[96,1536]{1,0:T(8,128)(2,1)S(1)} %collective-permute-done.16.mine.refs_5_), channel_id=1, source_target_pairs={{0,2},{1,3},{2,0},{3,1},{4,6},{5,7},{6,4},{7,5},{8,10},{9,11},{10,... | collective-permute-start | bytes 884744 | tf_op jit(solution)/shard_map/ppermute | solution.py:17
  99.8 25.4 %collective-permute-start.21 = (bf16[96,1536]{1,0:T(8,128)(2,1)S(1)}, bf16[96,1536]{1,0:T(8,128)(2,1)S(1)}, u32[]{:S(2)}, u32[]{:S(2)}) collective-permute-start(bf16[96,1536]{1,0:T(8,128)(2,1)S(1)} %shard_map.99), channel_id=1, source_target_pairs={{0,16},{1,21},{2,18},{3,23},{4,20},{5,17},{6,22},{7,19},{8,24},{9,... | collective-permute-start | bytes 884744 | tf_op jit(solution)/shard_map/ppermute | solution.py:17
  103.9 21.2 %collective-permute-start.25 = (bf16[96,1536]{1,0:T(8,128)(2,1)S(1)}, bf16[96,1536]{1,0:T(8,128)(2,1)S(1)}, u32[]{:S(2)}, u32[]{:S(2)}) collective-permute-start(bf16[96,1536]{1,0:T(8,128)(2,1)S(1)} %shard_map.100), channel_id=1, source_target_pairs={{0,24},{1,29},{2,26},{3,31},{4,28},{5,25},{6,30},{7,27},{8,16},{9,... | collective-permute-start | bytes 884744 | tf_op jit(solution)/shard_map/ppermute | solution.py:17
  109.3 20.0 %collective-permute-start.28 = (bf16[96,1536]{1,0:T(8,128)(2,1)S(1)}, bf16[96,1536]{1,0:T(8,128)(2,1)S(1)}, u32[]{:S(2)}, u32[]{:S(2)}) collective-permute-start(bf16[96,1536]{1,0:T(8,128)(2,1)S(1)} %get-tuple-element.194), channel_id=1, source_target_pairs={{0,2},{1,3},{2,0},{3,1},{4,6},{5,7},{6,4},{7,5},{8,10},{9,11},{10,... | collective-permute-start | bytes 884744 | tf_op jit(solution)/shard_map/ppermute | solution.py:17
  130.7 29.1 %collective-permute-start.34 = (f32[512,1536]{1,0:T(8,128)S(1)}, f32[512,1536]{1,0:T(8,128)S(1)}, u32[]{:S(2)}, u32[]{:S(2)}) collective-permute-start(f32[512,1536]{1,0:T(8,128)S(1)} %shard_map.108), channel_id=1, source_target_pairs={{0,1},{1,0},{2,3},{3,2},{4,5},{5,4},{6,7},{7,6},{8,9},{9,8},{10,11... | collective-permute-start | bytes 9437192 | tf_op jit(solution)/shard_map/ppermute | solution.py:17
  135.7 27.2 %collective-permute-start.33 = (f32[1536,512]{1,0:T(8,128)S(1)}, f32[1536,512]{1,0:T(8,128)S(1)}, u32[]{:S(2)}, u32[]{:S(2)}) collective-permute-start(f32[1536,512]{1,0:T(8,128)S(1)} %shard_map.106), channel_id=1, source_target_pairs={{0,1},{1,0},{2,3},{3,2},{4,5},{5,4},{6,7},{7,6},{8,9},{9,8},{10,11... | collective-permute-start | bytes 9437192 | tf_op jit(solution)/shard_map/ppermute | solution.py:17
  135.8 30.1 %collective-permute-start.32 = (bf16[192,1536]{1,0:T(8,128)(2,1)S(1)}, bf16[192,1536]{1,0:T(8,128)(2,1)S(1)}, u32[]{:S(2)}, u32[]{:S(2)}) collective-permute-start(bf16[192,1536]{1,0:T(8,128)(2,1)S(1)} %get-tuple-element.210), channel_id=1, source_target_pairs={{0,2},{1,3},{2,0},{3,1},{4,6},{5,7},{6,4},{7,5},{8,10},{9,11},{10,... | collective-permute-start | bytes 1769480 | tf_op jit(solution)/shard_map/ppermute | solution.py:17
  136.4 21.5 %collective-permute-start.30 = (bf16[96,1536]{1,0:T(8,128)(2,1)S(1)}, bf16[96,1536]{1,0:T(8,128)(2,1)S(1)}, u32[]{:S(2)}, u32[]{:S(2)}) collective-permute-start(bf16[96,1536]{1,0:T(8,128)(2,1)S(1)} %get-tuple-element.203), channel_id=1, source_target_pairs={{0,2},{1,3},{2,0},{3,1},{4,6},{5,7},{6,4},{7,5},{8,10},{9,11},{10,... | collective-permute-start | bytes 884744 | tf_op jit(solution)/shard_map/ppermute | solution.py:17
  137.9 32.9 %collective-permute-start.29 = (bf16[96,1536]{1,0:T(8,128)(2,1)S(1)}, bf16[96,1536]{1,0:T(8,128)(2,1)S(1)}, u32[]{:S(2)}, u32[]{:S(2)}) collective-permute-start(bf16[96,1536]{1,0:T(8,128)(2,1)S(1)} %shard_map.103), channel_id=1, source_target_pairs={{0,24},{1,29},{2,26},{3,31},{4,28},{5,25},{6,30},{7,27},{8,16},{9,... | collective-permute-start | bytes 884744 | tf_op jit(solution)/shard_map/ppermute | solution.py:17
  157.9 15.9 %collective-permute-start.31 = (bf16[96,1536]{1,0:T(8,128)(2,1)S(1)}, bf16[96,1536]{1,0:T(8,128)(2,1)S(1)}, u32[]{:S(2)}, u32[]{:S(2)}) collective-permute-start(bf16[96,1536]{1,0:T(8,128)(2,1)S(1)} %shard_map.107), channel_id=1, source_target_pairs={{0,16},{1,21},{2,18},{3,23},{4,20},{5,17},{6,22},{7,19},{8,24},{9,... | collective-permute-start | bytes 884744 | tf_op jit(solution)/shard_map/ppermute | solution.py:17
  166.1 7.8 %collective-permute-start.35 = (bf16[96,1536]{1,0:T(8,128)(2,1)S(1)}, bf16[96,1536]{1,0:T(8,128)(2,1)S(1)}, u32[]{:S(2)}, u32[]{:S(2)}) collective-permute-start(bf16[96,1536]{1,0:T(8,128)(2,1)S(1)} %get-tuple-element.225), channel_id=1, source_target_pairs={{0,0},{1,5},{2,2},{3,7},{4,4},{5,1},{6,6},{7,3},{8,8},{9,13},{10,1... | collective-permute-start | bytes 884744 | tf_op jit(solution)/shard_map/ppermute | solution.py:17
  166.8 13.2 %collective-permute-start.36 = (bf16[96,1536]{1,0:T(8,128)(2,1)S(1)}, bf16[96,1536]{1,0:T(8,128)(2,1)S(1)}, u32[]{:S(2)}, u32[]{:S(2)}) collective-permute-start(bf16[96,1536]{1,0:T(8,128)(2,1)S(1)} %get-tuple-element.227), channel_id=1, source_target_pairs={{0,8},{1,13},{2,10},{3,15},{4,12},{5,9},{6,14},{7,11},{8,0},{9,5},... | collective-permute-start | bytes 884744 | tf_op jit(solution)/shard_map/ppermute | solution.py:17
  168.6 12.4 %collective-permute-start.26 = (bf16[192,1536]{1,0:T(8,128)(2,1)S(1)}, bf16[192,1536]{1,0:T(8,128)(2,1)S(1)}, u32[]{:S(2)}, u32[]{:S(2)}) collective-permute-start(bf16[192,1536]{1,0:T(8,128)(2,1)S(1)} %pad_maximum_fusion), channel_id=1, source_target_pairs={{0,1},{1,0},{2,3},{3,2},{4,5},{5,4},{6,7},{7,6},{8,9},{9,8},{10,11... | collective-permute-start | bytes 1769480 | tf_op jit(solution)/shard_map/ppermute | solution.py:17
  (14 other events, 137.7 us)

commit v3 on v2

--- a/solution.py
+++ b/solution.py
@@ -29,10 +29,13 @@
         return values[0] if len(values) == 1 else values
 
     def done(self, value):
-        self.last = (value,)
+        self.last = (*self.last, value)
+
+    def now(self, value):
+        return lax.optimization_barrier((value, *self.last))[0]
 
     def begin(self, send, value, *where):
-        return send(lax.optimization_barrier((value, *self.last))[0], *where)
+        return send(self.now(value), *where)
 
 
 def silu_grad(values):
@@ -234,7 +237,7 @@
     return (pre0, pre1), (hid0, hid1), part, part_far
 
 
-def backward_kernel(mine, far, pre0, pre1, up0, up1, down0, down1, dpre0, dpre1, back, back_far):
+def backward_kernel(mine, far, pre0, pre1, up0, up1, down0, down1, dpre0, dpre1, back, *backs_far):
     rows = jnp.concatenate([mine[...], far[...]], axis=0)
     total = 0.0
     for up, down, pre, dpre in ((up0, down0, pre0, dpre0), (up1, down1, pre1, dpre1)):
@@ -243,46 +246,58 @@
         total = total + dot(grad, up[...], ((1,), (1,)))
     total = total.astype(jnp.bfloat16)
     back[...] = total[: mine.shape[0]]
-    back_far[...] = total[mine.shape[0] :]
-
-
-def backward(mine, far, pre, weights):
-    dpre0, dpre1, back, back_far = call(
+    rows = backs_far[0].shape[0]
+    for i, back_far in enumerate(backs_far):
+        back_far[...] = total[mine.shape[0] + i * rows : mine.shape[0] + (i + 1) * rows]
+
+
+def backward(mine, far, pre, weights, cuts=1):
+    piece = (mine.shape[0] // cuts, mine.shape[1])
+    dpre0, dpre1, *backs = call(
         backward_kernel,
-        [(pre[0].shape, jnp.bfloat16)] * 2 + [(mine.shape, jnp.bfloat16)] * 2,
+        [(pre[0].shape, jnp.bfloat16)] * 2
+        + [(mine.shape, jnp.bfloat16)]
+        + [(piece, jnp.bfloat16)] * cuts,
         mine,
         far,
         *pre,
         *weights,
     )
-    return (dpre0, dpre1), back, back_far
-
-
-def add_kernel(mine, far, *outs):
-    total = (mine[...].astype(jnp.float32) + far[...].astype(jnp.float32)).astype(jnp.bfloat16)
+    return (dpre0, dpre1), *backs
+
+
+def add_kernel(first, mine, far, *outs):
+    mine = mine[first : first + far.shape[0]]
+    total = (mine.astype(jnp.float32) + far[...].astype(jnp.float32)).astype(jnp.bfloat16)
     rows = outs[0].shape[0]
     for i, out in enumerate(outs):
         out[...] = total[i * rows : (i + 1) * rows]
 
 
-def added(mine, far, group):
-    shape = (mine.shape[0] // len(group), mine.shape[1])
-    return dict(zip(group, call(add_kernel, [(shape, jnp.bfloat16)] * len(group), mine, far)))
-
-
-def weight_kernel(lefts, rights, *refs):
-    out, both = refs[-1], lefts + rights
+def added(mine, far, group, first=0):
+    kernel = functools.partial(add_kernel, first * far.shape[0])
+    shape = (far.shape[0] // len(group), mine.shape[1])
+    return dict(zip(group, call(kernel, [(shape, jnp.bfloat16)] * len(group), mine, far)))
+
+
+def weight_kernel(lefts, rights, others, *refs):
+    both = lefts + rights
     left = jnp.concatenate([ref[...] for ref in refs[:lefts]], axis=0)
     right = jnp.concatenate([ref[...] for ref in refs[lefts:both]], axis=0)
     total = dot(left, right, ((0,), (0,)))
-    out[...] = total if len(refs) == both + 1 else total + refs[both][...]
-
-
-def weight_grad(left, right, *other):
-    shape = (left[0].shape[1], right[0].shape[1])
-    return call(
-        functools.partial(weight_kernel, len(left), len(right)), [(shape, jnp.float32)], *left, *right, *other
-    )[0]
+    if others:
+        other = jnp.concatenate([ref[...] for ref in refs[both : both + others]], axis=0)
+        total = total + other.astype(jnp.float32)
+    outs = refs[both + others :]
+    rows = outs[0].shape[0]
+    for i, out in enumerate(outs):
+        out[...] = total[i * rows : (i + 1) * rows].astype(out.dtype)
+
+
+def weight_grad(dtype, cuts, left, right, others=()):
+    shape = (left[0].shape[1] // cuts, right[0].shape[1])
+    kernel = functools.partial(weight_kernel, len(left), len(right), len(others))
+    return call(kernel, [(shape, dtype)] * cuts, *left, *right, *others)
 
 
 def hop(value, line):
@@ -333,13 +348,14 @@
     routes_both = (routes, routes_other)
     x_blocks = place(index, routes_both, (), (tokens, tokens_other), experts_all, capacity)
     order.done(x_blocks[0])
-    x_near, x_mid, x_far, up_other = (
-        hops(x_blocks, near), hops(x_blocks, mid), hops(x_blocks, far), core(up_own)
-    )
+    x_near, x_mid, x_far = hops(x_blocks, near), hops(x_blocks, mid), hops(x_blocks, far)
+    up_other, down_other = core(up_own), core(down_own)
     x0 = joined(come(x_near), near)
-    x0_far, down_other = across(x0), core(down_own)
-    up_other, down_other = order.wait(up_other, down_other)
+    x0_far = across(x0)
+    *x1, up_other, down_other = order.wait(*ordered(x_mid), up_other, down_other)
     weights = (up_own, up_other, down_own, down_other)
+    x1 = joined(dict(zip(mid, x1)), mid)
+    x1_far = across(x1)
     cotangent_other, gates_other = order.wait(core(cotangent), core(gates))
     g_blocks = place(
         index,
@@ -350,80 +366,78 @@
         capacity,
     )
     order.done(g_blocks[0])
-    x1 = joined(come(x_mid), mid)
-    x1_far, g_far = across(x1), hops(g_blocks, far)
     pre0, hid0, part0, part0_far = forward(x0, order.wait(x0_far), weights)
     order.done(part0_far)
     m0_far = across(part0_far)
     x2 = joined(come(x_far), far)
-    x2_far, g_mid = across(x2), hops(g_blocks, mid)
+    x2_far, g_far = across(x2), hops(g_blocks, far)
     pre1, hid1, part1, part1_far = forward(x1, order.wait(x1_far), weights)
     order.done(part1_far)
-    m1_far = across(part1_far)
+    m1_far, g_mid = across(part1_far), hops(g_blocks, mid)
     pre2, hid2, part2, part2_far = forward(x2, order.wait(x2_far), weights)
     order.done(part2_far)
     m2_far = across(part2_far)
 
-    g2 = joined(come(g_far), far)
-    g_near = hops(g_blocks, near[1:])
     m_sum = added(part0, order.wait(m0_far), near)
     order.done(m_sum[near[0]])
+    g2 = joined(come(g_far), far)
     g2_far = across(g2)
-    g1 = joined(come(g_mid), mid)
-    g_near |= hops(g_blocks, near[:1])
-    g0 = joined(come(g_near), near)
-    m_near = hops(m_sum, near)
     m_sum |= added(part1, order.wait(m1_far), mid)
     order.done(m_sum[mid[0]])
+    g_near, m_mid = hops(g_blocks, near), hops(m_sum, mid)
+    g1 = joined(come(g_mid), mid)
     g1_far = across(g1)
-    m_home = come(m_near)
-    m_mid = hops(m_sum, mid)
     m_sum |= added(part2, order.wait(m2_far), far)
     order.done(m_sum[far[0]])
-    m_far, g0_far = hops(m_sum, far), across(g0)
-    g2_far = order.wait(g2_far)
-    dpre2, back2, back2_far = backward(g2, g2_far, pre2, weights)
+    m_far = hops(m_sum, far)
+    g0 = joined(come(g_near), near)
+    g0_far = across(g0)
+    dpre2, back2, back2_far = backward(g2, order.wait(g2_far), pre2, weights)
     order.done(back2_far)
     b2_far = across(back2_far)
-    g1_far = order.wait(g1_far)
-    dpre1, back1, back1_far = backward(g1, g1_far, pre1, weights)
+    m_home = come(m_mid)
+    dpre1, back1, back1_far = backward(g1, order.wait(g1_far), pre1, weights)
     order.done(back1_far)
     b1_far = across(back1_far)
-    m_home |= come(m_mid)
-    m_home |= come(m_far)
-    m_other = core(halves(m_home))
 
     b_sum = added(back2, order.wait(b2_far), far)
     order.done(b_sum[far[0]])
     b_far = hops(b_sum, far)
-    g0_far = order.wait(g0_far)
-    dpre0, back0, back0_far = backward(g0, g0_far, pre0, weights)
-    order.done(back0_far)
-    b0_far = across(back0_far)
-    mixed = collect(index, routes, (gates,), ordered(m_home), order.wait(m_other), *sizes)
-    order.done(mixed)
-
-    x_all = (x0, x0_far, x1, x1_far, x2, x2_far)
-    g_all = (g0, g0_far, g1, g1_far, g2, g2_far)
-    hid, dpre = zip(hid0, hid1, hid2), zip(dpre0, dpre1, dpre2)
-    (hid_own, hid_other), (dpre_own, dpre_other) = hid, dpre
-    down_part = weight_grad(hid_other, g_all)
-    order.done(down_part)
-    down_sent = core(down_part)
-    up_part = weight_grad(x_all, dpre_other)
-    order.done(up_part)
-    up_sent = core(up_part)
+    m_home |= come(m_far)
     b_sum |= added(back1, order.wait(b1_far), mid)
     order.done(b_sum[mid[0]])
     b_mid = hops(b_sum, mid)
-    grad_down = weight_grad(hid_own, g_all, order.wait(down_sent))
-    order.done(grad_down)
-    grad_up = weight_grad(x_all, dpre_own, order.wait(up_sent))
-    order.done(grad_up)
+    dpre0, back0, back0_far = backward(g0, order.wait(g0_far), pre0, weights)
+    order.done(back0_far)
+    b0_far = across(back0_far)
+    b_home = come(b_far)
+    m_late = hops(m_sum, near)
+    m_home |= come({m: m_late[m] for m in near[:1]})
+
+    x_all = (x0, x0_far, x1, x1_far, x2, x2_far)
+    g_all = (g0, g0_far, g1, g1_far, g2, g2_far)
+    hid_own, hid_other = zip(hid0, hid1, hid2)
+    dpre_own, dpre_other = zip(dpre0, dpre1, dpre2)
+    down_part = weight_grad(jnp.bfloat16, 2, (order.now(hid0[1]), *hid_other[1:]), g_all)
+    up_part = weight_grad(jnp.bfloat16, 2, x_all, (order.now(dpre0[1]), *dpre_other[1:]))
+    order.done(down_part[0])
+    order.done(up_part[0])
+    b_home |= come(b_mid)
+    m_home |= come({m: m_late[m] for m in near[1:]})
+    m_other = core(halves(m_home))
     b_sum |= added(back0, order.wait(b0_far), near)
     order.done(b_sum[near[0]])
-    b_home = come(b_far | b_mid | hops(b_sum, near))
-    b_other = order.wait(core(halves(b_home)))
+    b_near = hops(b_sum, near)
+    down_sent, up_sent = [core(part) for part in down_part], [core(part) for part in up_part]
+    mixed = collect(index, routes, (gates,), ordered(m_home), order.wait(m_other), *sizes)
+    order.done(mixed)
+    b_home |= come(b_near)
+    b_other = core(halves(b_home))
+    (grad_down,) = weight_grad(jnp.float32, 1, hid_own, g_all, order.wait(*down_sent))
+    order.done(grad_down)
+    (grad_up,) = weight_grad(jnp.float32, 1, x_all, dpre_own, order.wait(*up_sent))
+    order.done(grad_up)
+    b_other = order.wait(b_other)
     token_grad = collect(index, routes, (), ordered(b_home), b_other, *sizes)
     return (mixed, token_grad, grad_up[None], grad_down[None])
 

time: 185 us -> 158 us (0.85)
  waiting for transfers between devices: 104 us -> 56.3 us
  starting transfers between devices: 48.3 us -> 69.2 us
    ppermute x38 -> x40, waiting for transfers between devices: 104 us -> 56.3 us  [swap(): lax.ppermute(value, 'expert', [(i, i ^ bits ^ (odd_bits if i % 2 else 0))...]
    ppermute x38 -> x40, starting transfers between devices: 48.3 us -> 69.2 us  [swap(): lax.ppermute(value, 'expert', [(i, i ^ bits ^ (odd_bits if i % 2 else 0))...]
  transfers between devices with their start and end apart: 38 -> 40, of which waited for: 17 -> 12; matrix products, arithmetic and copies ran while one was open for 0% -> 0% of each run, Pallas kernels for 13% -> 16%
where the time goes in v3:
time: 158 us
  starting transfers between devices  69.2 us (44%)
  waiting for transfers between devices  56.3 us (36%)
  Pallas kernels  27.8 us (18%)
  local copies, waits for them, and re-layouts  3.29 us (2%)
    ppermute x40, starting transfers between devices, swap(): lax.ppermute(value, 'expert', [(i, i ^ bits ^ (odd_bits if i % 2 else 0))...  69.2 us
    ppermute x40, waiting for transfers between devices, swap(): lax.ppermute(value, 'expert', [(i, i ^ bits ^ (odd_bits if i % 2 else 0))...  56.3 us
    pallas_call x16, Pallas kernels, call(): pl.pallas_call(kernel, out_shape=[jax.ShapeDtypeStruct(shape, dtype) for...  22.4 us
    pallas_call x2, Pallas kernels, collect(): pl.pallas_call(functools.partial(collect_kernel, experts_all, capacity, b...  3.34 us
    unnamed x34, local copies, waits for them, and re-layouts  3.19 us
  transfers between devices with their start and end apart: 40, of which 12 were waited for; matrix products, arithmetic and copies ran while one was open for 0% of the time, Pallas kernels for 16%

profile of v3, /device:TPU:0, one launch (start us, length us, event | category | flops | bytes accessed | tf_op | source)
XLA Modules:
  0.0 157.7 jit_solution(2587066994932850785)
XLA Ops:
  6.7 3.0 %collective-permute-start.3 = (bf16[96,1536]{1,0:T(8,128)(2,1)S(1)}, bf16[96,1536]{1,0:T(8,128)(2,1)S(1)}, u32[]{:S(2)}, u32[]{:S(2)}) collective-permute-start(bf16[96,1536]{1,0:T(8,128)(2,1)S(1)} %get-tuple-element.135), channel_id=1, source_target_pairs={{0,8},{1,13},{2,10},{3,15},{4,12},{5,9},{6,14},{7,11},{8,0},{9,5},... | collective-permute-start | bytes 884744 | tf_op jit(solution)/shard_map/ppermute | solution.py:17
  9.7 2.6 %collective-permute-start.5 = (bf16[96,1536]{1,0:T(8,128)(2,1)S(1)}, bf16[96,1536]{1,0:T(8,128)(2,1)S(1)}, u32[]{:S(2)}, u32[]{:S(2)}) collective-permute-start(bf16[96,1536]{1,0:T(8,128)(2,1)S(1)} %get-tuple-element.140), channel_id=1, source_target_pairs={{0,16},{1,21},{2,18},{3,23},{4,20},{5,17},{6,22},{7,19},{8,24},{9,... | collective-permute-start | bytes 884744 | tf_op jit(solution)/shard_map/ppermute | solution.py:17
  12.3 8.8 %collective-permute-done.3 = bf16[96,1536]{1,0:T(8,128)(2,1)S(1)} collective-permute-done((bf16[96,1536]{1,0:T(8,128)(2,1)S(1)}, bf16[96,1536]{1,0:T(8,128)(2,1)S(1)}, u32[]{:S(2)}, u32[]{:S(2)}) %collective-permute-start.3) | collective-permute-done | bytes 294944 | tf_op jit(solution)/shard_map/ppermute | solution.py:17
  21.2 2.7 %collective-permute-start.4 = (bf16[192,1536]{1,0:T(8,128)(2,1)S(1)}, bf16[192,1536]{1,0:T(8,128)(2,1)S(1)}, u32[]{:S(2)}, u32[]{:S(2)}) collective-permute-start(bf16[192,1536]{1,0:T(8,128)(2,1)S(1)} %constant_dynamic-update-slice_fusion.mine.refs_0_), channel_id=1, source_target_pairs={{0,2},{1,3},{2,0},{3,1},{4,6},{5,7},{6,4},{7,5},{8,10},{9,11},{10,... | collective-permute-start | bytes 1769480 | tf_op jit(solution)/shard_map/ppermute | solution.py:17
  23.9 3.8 %collective-permute-start.8 = (bf16[32,6144]{1,0:T(8,128)(2,1)S(1)}, bf16[32,6144]{1,0:T(8,128)(2,1)S(1)}, u32[]{:S(2)}, u32[]{:S(2)}) collective-permute-start(bf16[32,6144]{1,0:T(8,128)(2,1)S(1)} %copy-done.12), channel_id=1, source_target_pairs={{0,1},{1,0},{2,3},{3,2},{4,5},{5,4},{6,7},{7,6},{8,9},{9,8},{10,11... | collective-permute-start | bytes 1179656 | tf_op jit(solution)/shard_map/ppermute | solution.py:17
  27.8 2.5 %collective-permute-start.11 = (bf16[96,1536]{1,0:T(8,128)(2,1)S(1)}, bf16[96,1536]{1,0:T(8,128)(2,1)S(1)}, u32[]{:S(2)}, u32[]{:S(2)}) collective-permute-start(bf16[96,1536]{1,0:T(8,128)(2,1)S(1)} %get-tuple-element.156), channel_id=1, source_target_pairs={{0,24},{1,29},{2,26},{3,31},{4,28},{5,25},{6,30},{7,27},{8,16},{9,... | collective-permute-start | bytes 884744 | tf_op jit(solution)/shard_map/ppermute | solution.py:17
  32.8 3.3 %collective-permute-done.4.far.refs_1_ = bf16[192,1536]{1,0:T(8,128)(2,1)S(1)} collective-permute-done((bf16[192,1536]{1,0:T(8,128)(2,1)S(1)}, bf16[192,1536]{1,0:T(8,128)(2,1)S(1)}, u32[]{:S(2)}, u32[]{:S(2)}) %collective-permute-start.4) | collective-permute-done | bytes 589856 | tf_op jit(solution)/shard_map/ppermute | solution.py:17
  37.5 2.7 %shard_map.95 = (f32[384,512]{1,0:T(8,128)S(1)}, f32[384,512]{1,0:T(8,128)S(1)}, bf16[384,512]{1,0:T(8,128)(2,1)S(1)}, bf16[384,512]{1,0:T(8,128)(2,1)S(1)}, bf1...) custom-call(bf16[192,1536]{1,0:T(8,128)(2,1)S(1)} %constant_dynamic-update-slice_fusion.mine.refs_0_, ...), custom_call_target="tpu_custom_call" | custom-call | flops 1 | bytes 1 | tf_op jit(solution)/shard_map/pallas_call | solution.py:202
  40.2 2.5 %collective-permute-start.10 = (bf16[192,1536]{1,0:T(8,128)(2,1)S(1)}, bf16[192,1536]{1,0:T(8,128)(2,1)S(1)}, u32[]{:S(2)}, u32[]{:S(2)}) collective-permute-start(bf16[192,1536]{1,0:T(8,128)(2,1)S(1)} %get-tuple-element.154), channel_id=1, source_target_pairs={{0,2},{1,3},{2,0},{3,1},{4,6},{5,7},{6,4},{7,5},{8,10},{9,11},{10,... | collective-permute-start | bytes 1769480 | tf_op jit(solution)/shard_map/ppermute | solution.py:17
  42.8 3.4 %collective-permute-start.14 = (bf16[96,1536]{1,0:T(8,128)(2,1)S(1)}, bf16[96,1536]{1,0:T(8,128)(2,1)S(1)}, u32[]{:S(2)}, u32[]{:S(2)}) collective-permute-start(bf16[96,1536]{1,0:T(8,128)(2,1)S(1)} %get-tuple-element.167), channel_id=1, source_target_pairs={{0,24},{1,29},{2,26},{3,31},{4,28},{5,25},{6,30},{7,27},{8,16},{9,... | collective-permute-start | bytes 884744 | tf_op jit(solution)/shard_map/ppermute | solution.py:17
  49.2 11.5 %collective-permute-done.12.far.refs_5_ = bf16[96,1536]{1,0:T(8,128)(2,1)S(1)} collective-permute-done((bf16[96,1536]{1,0:T(8,128)(2,1)S(1)}, bf16[96,1536]{1,0:T(8,128)(2,1)S(1)}, u32[]{:S(2)}, u32[]{:S(2)}) %collective-permute-start.12) | collective-permute-done | bytes 294944 | tf_op jit(solution)/shard_map/ppermute | solution.py:17
  62.3 2.6 %collective-permute-start.19 = (bf16[96,1536]{1,0:T(8,128)(2,1)S(1)}, bf16[96,1536]{1,0:T(8,128)(2,1)S(1)}, u32[]{:S(2)}, u32[]{:S(2)}) collective-permute-start(bf16[96,1536]{1,0:T(8,128)(2,1)S(1)} %get-tuple-element.176), channel_id=1, source_target_pairs={{0,2},{1,3},{2,0},{3,1},{4,6},{5,7},{6,4},{7,5},{8,10},{9,11},{10,... | collective-permute-start | bytes 884744 | tf_op jit(solution)/shard_map/ppermute | solution.py:17
  65.0 2.1 %collective-permute-done.16.far = bf16[96,1536]{1,0:T(8,128)(2,1)S(1)} collective-permute-done((bf16[96,1536]{1,0:T(8,128)(2,1)S(1)}, bf16[96,1536]{1,0:T(8,128)(2,1)S(1)}, u32[]{:S(2)}, u32[]{:S(2)}) %collective-permute-start.16) | collective-permute-done | bytes 294944 | tf_op jit(solution)/shard_map/ppermute | solution.py:17
  69.2 2.4 %collective-permute-start.15 = (bf16[96,1536]{1,0:T(8,128)(2,1)S(1)}, bf16[96,1536]{1,0:T(8,128)(2,1)S(1)}, u32[]{:S(2)}, u32[]{:S(2)}) collective-permute-start(bf16[96,1536]{1,0:T(8,128)(2,1)S(1)} %collective-permute-done.14.mine.refs_7_), channel_id=1, source_target_pairs={{0,2},{1,3},{2,0},{3,1},{4,6},{5,7},{6,4},{7,5},{8,10},{9,11},{10,... | collective-permute-start | bytes 884744 | tf_op jit(solution)/shard_map/ppermute | solution.py:17
  73.4 4.3 %collective-permute-start.23 = (bf16[96,1536]{1,0:T(8,128)(2,1)S(1)}, bf16[96,1536]{1,0:T(8,128)(2,1)S(1)}, u32[]{:S(2)}, u32[]{:S(2)}) collective-permute-start(bf16[96,1536]{1,0:T(8,128)(2,1)S(1)} %shard_map.99), channel_id=1, source_target_pairs={{0,16},{1,21},{2,18},{3,23},{4,20},{5,17},{6,22},{7,19},{8,24},{9,... | collective-permute-start | bytes 884744 | tf_op jit(solution)/shard_map/ppermute | solution.py:17
  77.8 1.9 %collective-permute-done.15.far.refs_8_ = bf16[96,1536]{1,0:T(8,128)(2,1)S(1)} collective-permute-done((bf16[96,1536]{1,0:T(8,128)(2,1)S(1)}, bf16[96,1536]{1,0:T(8,128)(2,1)S(1)}, u32[]{:S(2)}, u32[]{:S(2)}) %collective-permute-start.15) | collective-permute-done | bytes 294944 | tf_op jit(solution)/shard_map/ppermute | solution.py:17
  79.7 2.2 %shard_map.101 = (bf16[192,512]{1,0:T(8,128)(2,1)S(1)}, bf16[192,512]{1,0:T(8,128)(2,1)S(1)}, bf16[96,1536]{1,0:T(8,128)(2,1)S(1)}, bf16[96,1536]{1,0:T(8,128)(2,1)S(1)}) custom-call(bf16[96,1536]{1,0:T(8,128)(2,1)S(1)} %collective-permute-done.14.mine.refs_7_, bf16[96,1536]{1,0:T(8,128)(2,1)S(1)} %collective-permute-done.15.far.refs_8_, ...), custom_call_target="tpu_custom_call" | custom-call | flops 1 | bytes 1 | tf_op jit(solution)/shard_map/pallas_call | solution.py:202
  82.0 2.5 %collective-permute-start.21 = (bf16[96,1536]{1,0:T(8,128)(2,1)S(1)}, bf16[96,1536]{1,0:T(8,128)(2,1)S(1)}, u32[]{:S(2)}, u32[]{:S(2)}) collective-permute-start(bf16[96,1536]{1,0:T(8,128)(2,1)S(1)} %get-tuple-element.188), channel_id=1, source_target_pairs={{0,2},{1,3},{2,0},{3,1},{4,6},{5,7},{6,4},{7,5},{8,10},{9,11},{10,... | collective-permute-start | bytes 884744 | tf_op jit(solution)/shard_map/ppermute | solution.py:17
  84.6 3.6 %collective-permute-start.27 = (bf16[96,1536]{1,0:T(8,128)(2,1)S(1)}, bf16[96,1536]{1,0:T(8,128)(2,1)S(1)}, u32[]{:S(2)}, u32[]{:S(2)}) collective-permute-start(bf16[96,1536]{1,0:T(8,128)(2,1)S(1)} %shard_map.100), channel_id=1, source_target_pairs={{0,24},{1,29},{2,26},{3,31},{4,28},{5,25},{6,30},{7,27},{8,16},{9,... | collective-permute-start | bytes 884744 | tf_op jit(solution)/shard_map/ppermute | solution.py:17
  88.2 8.6 %collective-permute-done.23.refs_3_ = bf16[96,1536]{1,0:T(8,128)(2,1)S(1)} collective-permute-done((bf16[96,1536]{1,0:T(8,128)(2,1)S(1)}, bf16[96,1536]{1,0:T(8,128)(2,1)S(1)}, u32[]{:S(2)}, u32[]{:S(2)}) %collective-permute-start.23) | collective-permute-done | bytes 294944 | tf_op jit(solution)/shard_map/ppermute | solution.py:17
  96.8 2.2 %shard_map.102 = (bf16[192,512]{1,0:T(8,128)(2,1)S(1)}, bf16[192,512]{1,0:T(8,128)(2,1)S(1)}, bf16[96,1536]{1,0:T(8,128)(2,1)S(1)}, bf16[96,1536]{1,0:T(8,128)(2,1)S(1)}) custom-call(bf16[96,1536]{1,0:T(8,128)(2,1)S(1)} %collective-permute-done.20.mine.refs_5_, bf16[96,1536]{1,0:T(8,128)(2,1)S(1)} %collective-permute-done.22.far.refs_6_, ...), custom_call_target="tpu_custom_call" | custom-call | flops 1 | bytes 1 | tf_op jit(solution)/shard_map/pallas_call | solution.py:202
  99.3 12.1 %collective-permute-done.26.far = bf16[96,1536]{1,0:T(8,128)(2,1)S(1)} collective-permute-done((bf16[96,1536]{1,0:T(8,128)(2,1)S(1)}, bf16[96,1536]{1,0:T(8,128)(2,1)S(1)}, u32[]{:S(2)}, u32[]{:S(2)}) %collective-permute-start.26) | collective-permute-done | bytes 294944 | tf_op jit(solution)/shard_map/ppermute | solution.py:17
  111.5 2.8 %shard_map.105 = (bf16[384,512]{1,0:T(8,128)(2,1)S(1)}, bf16[384,512]{1,0:T(8,128)(2,1)S(1)}, bf16[192,1536]{1,0:T(8,128)(2,1)S(1)}, bf16[192,1536]{1,0:T(8,128)(2,1)S(1)}) custom-call(bf16[192,1536]{1,0:T(8,128)(2,1)S(1)} %constant_dynamic-update-slice_fusion.2.mine.refs_3_, bf16[192,1536]{1,0:T(8,128)(2,1)S(1)} %collective-permute-done.25.far.refs_4_, ...), custom_call_target="tpu_custom_call" | custom-call | flops 1 | bytes 1 | tf_op jit(solution)/shard_map/pallas_call | solution.py:202
  115.0 3.0 %collective-permute-start.30 = (bf16[96,1536]{1,0:T(8,128)(2,1)S(1)}, bf16[96,1536]{1,0:T(8,128)(2,1)S(1)}, u32[]{:S(2)}, u32[]{:S(2)}) collective-permute-start(bf16[96,1536]{1,0:T(8,128)(2,1)S(1)} %shard_map.104), channel_id=1, source_target_pairs={{0,16},{1,21},{2,18},{3,23},{4,20},{5,17},{6,22},{7,19},{8,24},{9,... | collective-permute-start | bytes 884744 | tf_op jit(solution)/shard_map/ppermute | solution.py:17
  124.0 3.2 %collective-permute-done.30.refs_2_ = bf16[96,1536]{1,0:T(8,128)(2,1)S(1)} collective-permute-done((bf16[96,1536]{1,0:T(8,128)(2,1)S(1)}, bf16[96,1536]{1,0:T(8,128)(2,1)S(1)}, u32[]{:S(2)}, u32[]{:S(2)}) %collective-permute-start.30) | collective-permute-done | bytes 294944 | tf_op jit(solution)/shard_map/ppermute | solution.py:17
  128.3 8.6 %collective-permute-start.31 = (bf16[192,1536]{1,0:T(8,128)(2,1)S(1)}, bf16[192,1536]{1,0:T(8,128)(2,1)S(1)}, u32[]{:S(2)}, u32[]{:S(2)}) collective-permute-start(bf16[192,1536]{1,0:T(8,128)(2,1)S(1)} %pad_maximum_fusion), channel_id=1, source_target_pairs={{0,1},{1,0},{2,3},{3,2},{4,5},{5,4},{6,7},{7,6},{8,9},{9,8},{10,11... | collective-permute-start | bytes 1769480 | tf_op jit(solution)/shard_map/ppermute | solution.py:17
  138.0 1.7 %collective-permute-start.34 = (bf16[96,1536]{1,0:T(8,128)(2,1)S(1)}, bf16[96,1536]{1,0:T(8,128)(2,1)S(1)}, u32[]{:S(2)}, u32[]{:S(2)}) collective-permute-start(bf16[96,1536]{1,0:T(8,128)(2,1)S(1)} %get-tuple-element.235), channel_id=1, source_target_pairs={{0,8},{1,13},{2,10},{3,15},{4,12},{5,9},{6,14},{7,11},{8,0},{9,5},... | collective-permute-start | bytes 884744 | tf_op jit(solution)/shard_map/ppermute | solution.py:17
  139.7 2.8 %collective-permute-start.36 = (bf16[768,512]{1,0:T(8,128)(2,1)S(1)}, bf16[768,512]{1,0:T(8,128)(2,1)S(1)}, u32[]{:S(2)}, u32[]{:S(2)}) collective-permute-start(bf16[768,512]{1,0:T(8,128)(2,1)S(1)} %get-tuple-element.239), channel_id=1, source_target_pairs={{0,1},{1,0},{2,3},{3,2},{4,5},{5,4},{6,7},{7,6},{8,9},{9,8},{10,11... | collective-permute-start | bytes 2359304 | tf_op jit(solution)/shard_map/ppermute | solution.py:17
  143.0 1.7 %shard_map.109 = bf16[32,6144]{1,0:T(8,128)(2,1)} custom-call(s32[1]{0:T(128)} %bitcast.index_ref, s32[2,128]{1,0:T(2,128)S(1)} %bitcast.24, f32[2,128]{1,0:T(2,128)S(1)} %bitcast.28, bf16[96,1536]{1,0:T(8,128)(2,1)S(1)} %collective-permute-done.28.refs_1_, bf16[96,1536]{1,0:T(8,128)(2,1)S(1)} %collective-permute-done.29.refs_2_, ...), custom_call_target="tpu_custom_call" | custom-call | flops 1 | bytes 1 | tf_op jit(solution)/shard_map/pallas_call | solution.py:186
  144.8 3.2 %collective-permute-start.39 = (bf16[256,1536]{1,0:T(8,128)(2,1)S(1)}, bf16[256,1536]{1,0:T(8,128)(2,1)S(1)}, u32[]{:S(2)}, u32[]{:S(2)}) collective-permute-start(bf16[256,1536]{1,0:T(8,128)(2,1)S(1)} %get-tuple-element.244), channel_id=1, source_target_pairs={{0,1},{1,0},{2,3},{3,2},{4,5},{5,4},{6,7},{7,6},{8,9},{9,8},{10,11... | collective-permute-start | bytes 2359304 | tf_op jit(solution)/shard_map/ppermute | solution.py:17
  149.9 3.1 %shard_map.110 = f32[512,1536]{1,0:T(8,128)} custom-call(bf16[384,512]{1,0:T(8,128)(2,1)S(1)} %get-tuple-element.246.refs_0_, bf16[192,512]{1,0:T(8,128)(2,1)S(1)} %get-tuple-element.247.refs_1_, bf16[192,512]{1,0:T(8,128)(2,1)S(1)} %get-tuple-element.248.refs_2_, bf16[192,1536]{1,0:T(8,128)(2,1)S(1)} %constant_dynamic-update-slice_fusion.2.mine.refs_3_, ...), custom_call_target="tpu_custom_call" | custom-call | flops 1 | bytes 1 | tf_op jit(solution)/shard_map/pallas_call | solution.py:202
  153.0 3.1 %shard_map.111 = f32[1536,512]{1,0:T(8,128)} custom-call(bf16[192,1536]{1,0:T(8,128)(2,1)S(1)} %constant_dynamic-update-slice_fusion.mine.refs_0_, bf16[192,1536]{1,0:T(8,128)(2,1)S(1)} %collective-permute-done.4.far.refs_1_, bf16[96,1536]{1,0:T(8,128)(2,1)S(1)} %collective-permute-done.5.mine.refs_2_, ...), custom_call_target="tpu_custom_call" | custom-call | flops 1 | bytes 1 | tf_op jit(solution)/shard_map/pallas_call | solution.py:202
  (118 shorter events, 32.1 us)
Async XLA Ops:
  5.4 18.5 %collective-permute-start.6 = (bf16[1536,512]{1,0:T(8,128)(2,1)}, bf16[1536,512]{1,0:T(8,128)(2,1)S(1)}, u32[]{:S(2)}, u32[]{:S(2)}) collective-permute-start(bf16[1536,512]{1,0:T(8,128)(2,1)} %bitcast.7), channel_id=1, source_target_pairs={{0,1},{1,0},{2,3},{3,2},{4,5},{5,4},{6,7},{7,6},{8,9},{9,8},{10,11... | collective-permute-start | bytes 4718600 | tf_op jit(solution)/shard_map/ppermute | solution.py:17
  5.9 18.0 %collective-permute-start.7 = (bf16[512,1536]{1,0:T(8,128)(2,1)}, bf16[512,1536]{1,0:T(8,128)(2,1)S(1)}, u32[]{:S(2)}, u32[]{:S(2)}) collective-permute-start(bf16[512,1536]{1,0:T(8,128)(2,1)} %bitcast.14), channel_id=1, source_target_pairs={{0,1},{1,0},{2,3},{3,2},{4,5},{5,4},{6,7},{7,6},{8,9},{9,8},{10,11... | collective-permute-start | bytes 4718600 | tf_op jit(solution)/shard_map/ppermute | solution.py:17
  6.7 14.4 %collective-permute-start.3 = (bf16[96,1536]{1,0:T(8,128)(2,1)S(1)}, bf16[96,1536]{1,0:T(8,128)(2,1)S(1)}, u32[]{:S(2)}, u32[]{:S(2)}) collective-permute-start(bf16[96,1536]{1,0:T(8,128)(2,1)S(1)} %get-tuple-element.135), channel_id=1, source_target_pairs={{0,8},{1,13},{2,10},{3,15},{4,12},{5,9},{6,14},{7,11},{8,0},{9,5},... | collective-permute-start | bytes 884744 | tf_op jit(solution)/shard_map/ppermute | solution.py:17
  9.7 14.2 %collective-permute-start.5 = (bf16[96,1536]{1,0:T(8,128)(2,1)S(1)}, bf16[96,1536]{1,0:T(8,128)(2,1)S(1)}, u32[]{:S(2)}, u32[]{:S(2)}) collective-permute-start(bf16[96,1536]{1,0:T(8,128)(2,1)S(1)} %get-tuple-element.140), channel_id=1, source_target_pairs={{0,16},{1,21},{2,18},{3,23},{4,20},{5,17},{6,22},{7,19},{8,24},{9,... | collective-permute-start | bytes 884744 | tf_op jit(solution)/shard_map/ppermute | solution.py:17
  21.2 14.9 %collective-permute-start.4 = (bf16[192,1536]{1,0:T(8,128)(2,1)S(1)}, bf16[192,1536]{1,0:T(8,128)(2,1)S(1)}, u32[]{:S(2)}, u32[]{:S(2)}) collective-permute-start(bf16[192,1536]{1,0:T(8,128)(2,1)S(1)} %constant_dynamic-update-slice_fusion.mine.refs_0_), channel_id=1, source_target_pairs={{0,2},{1,3},{2,0},{3,1},{4,6},{5,7},{6,4},{7,5},{8,10},{9,11},{10,... | collective-permute-start | bytes 1769480 | tf_op jit(solution)/shard_map/ppermute | solution.py:17
  23.9 7.9 %collective-permute-start.8 = (bf16[32,6144]{1,0:T(8,128)(2,1)S(1)}, bf16[32,6144]{1,0:T(8,128)(2,1)S(1)}, u32[]{:S(2)}, u32[]{:S(2)}) collective-permute-start(bf16[32,6144]{1,0:T(8,128)(2,1)S(1)} %copy-done.12), channel_id=1, source_target_pairs={{0,1},{1,0},{2,3},{3,2},{4,5},{5,4},{6,7},{7,6},{8,9},{9,8},{10,11... | collective-permute-start | bytes 1179656 | tf_op jit(solution)/shard_map/ppermute | solution.py:17
  27.8 14.9 %collective-permute-start.11 = (bf16[96,1536]{1,0:T(8,128)(2,1)S(1)}, bf16[96,1536]{1,0:T(8,128)(2,1)S(1)}, u32[]{:S(2)}, u32[]{:S(2)}) collective-permute-start(bf16[96,1536]{1,0:T(8,128)(2,1)S(1)} %get-tuple-element.156), channel_id=1, source_target_pairs={{0,24},{1,29},{2,26},{3,31},{4,28},{5,25},{6,30},{7,27},{8,16},{9,... | collective-permute-start | bytes 884744 | tf_op jit(solution)/shard_map/ppermute | solution.py:17
  30.3 12.6 %collective-permute-start.13 = (bf16[96,1536]{1,0:T(8,128)(2,1)S(1)}, bf16[96,1536]{1,0:T(8,128)(2,1)S(1)}, u32[]{:S(2)}, u32[]{:S(2)}) collective-permute-start(bf16[96,1536]{1,0:T(8,128)(2,1)S(1)} %collective-permute-done.5.mine.refs_2_), channel_id=1, source_target_pairs={{0,2},{1,3},{2,0},{3,1},{4,6},{5,7},{6,4},{7,5},{8,10},{9,11},{10,... | collective-permute-start | bytes 884744 | tf_op jit(solution)/shard_map/ppermute | solution.py:17
  40.2 24.6 %collective-permute-start.10 = (bf16[192,1536]{1,0:T(8,128)(2,1)S(1)}, bf16[192,1536]{1,0:T(8,128)(2,1)S(1)}, u32[]{:S(2)}, u32[]{:S(2)}) collective-permute-start(bf16[192,1536]{1,0:T(8,128)(2,1)S(1)} %get-tuple-element.154), channel_id=1, source_target_pairs={{0,2},{1,3},{2,0},{3,1},{4,6},{5,7},{6,4},{7,5},{8,10},{9,11},{10,... | collective-permute-start | bytes 1769480 | tf_op jit(solution)/shard_map/ppermute | solution.py:17
  42.7 18.0 %collective-permute-start.12 = (bf16[96,1536]{1,0:T(8,128)(2,1)S(1)}, bf16[96,1536]{1,0:T(8,128)(2,1)S(1)}, u32[]{:S(2)}, u32[]{:S(2)}) collective-permute-start(bf16[96,1536]{1,0:T(8,128)(2,1)S(1)} %collective-permute-done.11.mine.refs_4_), channel_id=1, source_target_pairs={{0,2},{1,3},{2,0},{3,1},{4,6},{5,7},{6,4},{7,5},{8,10},{9,11},{10,... | collective-permute-start | bytes 884744 | tf_op jit(solution)/shard_map/ppermute | solution.py:17
  42.8 22.1 %collective-permute-start.14 = (bf16[96,1536]{1,0:T(8,128)(2,1)S(1)}, bf16[96,1536]{1,0:T(8,128)(2,1)S(1)}, u32[]{:S(2)}, u32[]{:S(2)}) collective-permute-start(bf16[96,1536]{1,0:T(8,128)(2,1)S(1)} %get-tuple-element.167), channel_id=1, source_target_pairs={{0,24},{1,29},{2,26},{3,31},{4,28},{5,25},{6,30},{7,27},{8,16},{9,... | collective-permute-start | bytes 884744 | tf_op jit(solution)/shard_map/ppermute | solution.py:17
  47.7 19.4 %collective-permute-start.16 = (bf16[96,1536]{1,0:T(8,128)(2,1)S(1)}, bf16[96,1536]{1,0:T(8,128)(2,1)S(1)}, u32[]{:S(2)}, u32[]{:S(2)}) collective-permute-start(bf16[96,1536]{1,0:T(8,128)(2,1)S(1)} %get-tuple-element.170), channel_id=1, source_target_pairs={{0,2},{1,3},{2,0},{3,1},{4,6},{5,7},{6,4},{7,5},{8,10},{9,11},{10,... | collective-permute-start | bytes 884744 | tf_op jit(solution)/shard_map/ppermute | solution.py:17
  49.2 23.8 %collective-permute-start.20 = (bf16[96,1536]{1,0:T(8,128)(2,1)S(1)}, bf16[96,1536]{1,0:T(8,128)(2,1)S(1)}, u32[]{:S(2)}, u32[]{:S(2)}) collective-permute-start(bf16[96,1536]{1,0:T(8,128)(2,1)S(1)} %get-tuple-element.178), channel_id=1, source_target_pairs={{0,16},{1,21},{2,18},{3,23},{4,20},{5,17},{6,22},{7,19},{8,24},{9,... | collective-permute-start | bytes 884744 | tf_op jit(solution)/shard_map/ppermute | solution.py:17
  62.3 11.1 %collective-permute-start.19 = (bf16[96,1536]{1,0:T(8,128)(2,1)S(1)}, bf16[96,1536]{1,0:T(8,128)(2,1)S(1)}, u32[]{:S(2)}, u32[]{:S(2)}) collective-permute-start(bf16[96,1536]{1,0:T(8,128)(2,1)S(1)} %get-tuple-element.176), channel_id=1, source_target_pairs={{0,2},{1,3},{2,0},{3,1},{4,6},{5,7},{6,4},{7,5},{8,10},{9,11},{10,... | collective-permute-start | bytes 884744 | tf_op jit(solution)/shard_map/ppermute | solution.py:17
  67.1 10.6 %collective-permute-start.17 = (bf16[96,1536]{1,0:T(8,128)(2,1)S(1)}, bf16[96,1536]{1,0:T(8,128)(2,1)S(1)}, u32[]{:S(2)}, u32[]{:S(2)}) collective-permute-start(bf16[96,1536]{1,0:T(8,128)(2,1)S(1)} %get-tuple-element.173), channel_id=1, source_target_pairs={{0,0},{1,5},{2,2},{3,7},{4,4},{5,1},{6,6},{7,3},{8,8},{9,13},{10,1... | collective-permute-start | bytes 884744 | tf_op jit(solution)/shard_map/ppermute | solution.py:17
  68.0 9.8 %collective-permute-start.18 = (bf16[96,1536]{1,0:T(8,128)(2,1)S(1)}, bf16[96,1536]{1,0:T(8,128)(2,1)S(1)}, u32[]{:S(2)}, u32[]{:S(2)}) collective-permute-start(bf16[96,1536]{1,0:T(8,128)(2,1)S(1)} %get-tuple-element.175), channel_id=1, source_target_pairs={{0,8},{1,13},{2,10},{3,15},{4,12},{5,9},{6,14},{7,11},{8,0},{9,5},... | collective-permute-start | bytes 884744 | tf_op jit(solution)/shard_map/ppermute | solution.py:17
  69.2 10.5 %collective-permute-start.15 = (bf16[96,1536]{1,0:T(8,128)(2,1)S(1)}, bf16[96,1536]{1,0:T(8,128)(2,1)S(1)}, u32[]{:S(2)}, u32[]{:S(2)}) collective-permute-start(bf16[96,1536]{1,0:T(8,128)(2,1)S(1)} %collective-permute-done.14.mine.refs_7_), channel_id=1, source_target_pairs={{0,2},{1,3},{2,0},{3,1},{4,6},{5,7},{6,4},{7,5},{8,10},{9,11},{10,... | collective-permute-start | bytes 884744 | tf_op jit(solution)/shard_map/ppermute | solution.py:17
  73.0 23.8 %collective-permute-start.22 = (bf16[96,1536]{1,0:T(8,128)(2,1)S(1)}, bf16[96,1536]{1,0:T(8,128)(2,1)S(1)}, u32[]{:S(2)}, u32[]{:S(2)}) collective-permute-start(bf16[96,1536]{1,0:T(8,128)(2,1)S(1)} %collective-permute-done.20.mine.refs_5_), channel_id=1, source_target_pairs={{0,2},{1,3},{2,0},{3,1},{4,6},{5,7},{6,4},{7,5},{8,10},{9,11},{10,... | collective-permute-start | bytes 884744 | tf_op jit(solution)/shard_map/ppermute | solution.py:17
  73.4 23.4 %collective-permute-start.23 = (bf16[96,1536]{1,0:T(8,128)(2,1)S(1)}, bf16[96,1536]{1,0:T(8,128)(2,1)S(1)}, u32[]{:S(2)}, u32[]{:S(2)}) collective-permute-start(bf16[96,1536]{1,0:T(8,128)(2,1)S(1)} %shard_map.99), channel_id=1, source_target_pairs={{0,16},{1,21},{2,18},{3,23},{4,20},{5,17},{6,22},{7,19},{8,24},{9,... | collective-permute-start | bytes 884744 | tf_op jit(solution)/shard_map/ppermute | solution.py:17
  82.0 17.2 %collective-permute-start.21 = (bf16[96,1536]{1,0:T(8,128)(2,1)S(1)}, bf16[96,1536]{1,0:T(8,128)(2,1)S(1)}, u32[]{:S(2)}, u32[]{:S(2)}) collective-permute-start(bf16[96,1536]{1,0:T(8,128)(2,1)S(1)} %get-tuple-element.188), channel_id=1, source_target_pairs={{0,2},{1,3},{2,0},{3,1},{4,6},{5,7},{6,4},{7,5},{8,10},{9,11},{10,... | collective-permute-start | bytes 884744 | tf_op jit(solution)/shard_map/ppermute | solution.py:17
  84.5 26.9 %collective-permute-start.25 = (bf16[192,1536]{1,0:T(8,128)(2,1)S(1)}, bf16[192,1536]{1,0:T(8,128)(2,1)S(1)}, u32[]{:S(2)}, u32[]{:S(2)}) collective-permute-start(bf16[192,1536]{1,0:T(8,128)(2,1)S(1)} %constant_dynamic-update-slice_fusion.2.mine.refs_3_), channel_id=1, source_target_pairs={{0,2},{1,3},{2,0},{3,1},{4,6},{5,7},{6,4},{7,5},{8,10},{9,11},{10,... | collective-permute-start | bytes 1769480 | tf_op jit(solution)/shard_map/ppermute | solution.py:17
  84.6 14.7 %collective-permute-start.27 = (bf16[96,1536]{1,0:T(8,128)(2,1)S(1)}, bf16[96,1536]{1,0:T(8,128)(2,1)S(1)}, u32[]{:S(2)}, u32[]{:S(2)}) collective-permute-start(bf16[96,1536]{1,0:T(8,128)(2,1)S(1)} %shard_map.100), channel_id=1, source_target_pairs={{0,24},{1,29},{2,26},{3,31},{4,28},{5,25},{6,30},{7,27},{8,16},{9,... | collective-permute-start | bytes 884744 | tf_op jit(solution)/shard_map/ppermute | solution.py:17
  99.0 12.3 %collective-permute-start.26 = (bf16[96,1536]{1,0:T(8,128)(2,1)S(1)}, bf16[96,1536]{1,0:T(8,128)(2,1)S(1)}, u32[]{:S(2)}, u32[]{:S(2)}) collective-permute-start(bf16[96,1536]{1,0:T(8,128)(2,1)S(1)} %get-tuple-element.200), channel_id=1, source_target_pairs={{0,2},{1,3},{2,0},{3,1},{4,6},{5,7},{6,4},{7,5},{8,10},{9,11},{10,... | collective-permute-start | bytes 884744 | tf_op jit(solution)/shard_map/ppermute | solution.py:17
  99.2 15.0 %collective-permute-start.24 = (bf16[96,1536]{1,0:T(8,128)(2,1)S(1)}, bf16[96,1536]{1,0:T(8,128)(2,1)S(1)}, u32[]{:S(2)}, u32[]{:S(2)}) collective-permute-start(bf16[96,1536]{1,0:T(8,128)(2,1)S(1)} %shard_map.103), channel_id=1, source_target_pairs={{0,24},{1,29},{2,26},{3,31},{4,28},{5,25},{6,30},{7,27},{8,16},{9,... | collective-permute-start | bytes 884744 | tf_op jit(solution)/shard_map/ppermute | solution.py:17
  115.0 12.2 %collective-permute-start.30 = (bf16[96,1536]{1,0:T(8,128)(2,1)S(1)}, bf16[96,1536]{1,0:T(8,128)(2,1)S(1)}, u32[]{:S(2)}, u32[]{:S(2)}) collective-permute-start(bf16[96,1536]{1,0:T(8,128)(2,1)S(1)} %shard_map.104), channel_id=1, source_target_pairs={{0,16},{1,21},{2,18},{3,23},{4,20},{5,17},{6,22},{7,19},{8,24},{9,... | collective-permute-start | bytes 884744 | tf_op jit(solution)/shard_map/ppermute | solution.py:17
  118.0 10.2 %collective-permute-start.29 = (bf16[96,1536]{1,0:T(8,128)(2,1)S(1)}, bf16[96,1536]{1,0:T(8,128)(2,1)S(1)}, u32[]{:S(2)}, u32[]{:S(2)}) collective-permute-start(bf16[96,1536]{1,0:T(8,128)(2,1)S(1)} %get-tuple-element.213), channel_id=1, source_target_pairs={{0,8},{1,13},{2,10},{3,15},{4,12},{5,9},{6,14},{7,11},{8,0},{9,5},... | collective-permute-start | bytes 884744 | tf_op jit(solution)/shard_map/ppermute | solution.py:17
  119.6 17.3 %collective-permute-start.32 = (bf16[192,1536]{1,0:T(8,128)(2,1)S(1)}, bf16[192,1536]{1,0:T(8,128)(2,1)S(1)}, u32[]{:S(2)}, u32[]{:S(2)}) collective-permute-start(bf16[192,1536]{1,0:T(8,128)(2,1)S(1)} %get-tuple-element.228), channel_id=1, source_target_pairs={{0,2},{1,3},{2,0},{3,1},{4,6},{5,7},{6,4},{7,5},{8,10},{9,11},{10,... | collective-permute-start | bytes 1769480 | tf_op jit(solution)/shard_map/ppermute | solution.py:17
  128.3 14.3 %collective-permute-start.31 = (bf16[192,1536]{1,0:T(8,128)(2,1)S(1)}, bf16[192,1536]{1,0:T(8,128)(2,1)S(1)}, u32[]{:S(2)}, u32[]{:S(2)}) collective-permute-start(bf16[192,1536]{1,0:T(8,128)(2,1)S(1)} %pad_maximum_fusion), channel_id=1, source_target_pairs={{0,1},{1,0},{2,3},{3,2},{4,5},{5,4},{6,7},{7,6},{8,9},{9,8},{10,11... | collective-permute-start | bytes 1769480 | tf_op jit(solution)/shard_map/ppermute | solution.py:17
  138.0 10.0 %collective-permute-start.34 = (bf16[96,1536]{1,0:T(8,128)(2,1)S(1)}, bf16[96,1536]{1,0:T(8,128)(2,1)S(1)}, u32[]{:S(2)}, u32[]{:S(2)}) collective-permute-start(bf16[96,1536]{1,0:T(8,128)(2,1)S(1)} %get-tuple-element.235), channel_id=1, source_target_pairs={{0,8},{1,13},{2,10},{3,15},{4,12},{5,9},{6,14},{7,11},{8,0},{9,5},... | collective-permute-start | bytes 884744 | tf_op jit(solution)/shard_map/ppermute | solution.py:17
  139.7 13.3 %collective-permute-start.36 = (bf16[768,512]{1,0:T(8,128)(2,1)S(1)}, bf16[768,512]{1,0:T(8,128)(2,1)S(1)}, u32[]{:S(2)}, u32[]{:S(2)}) collective-permute-start(bf16[768,512]{1,0:T(8,128)(2,1)S(1)} %get-tuple-element.239), channel_id=1, source_target_pairs={{0,1},{1,0},{2,3},{3,2},{4,5},{5,4},{6,7},{7,6},{8,9},{9,8},{10,11... | collective-permute-start | bytes 2359304 | tf_op jit(solution)/shard_map/ppermute | solution.py:17
  142.5 10.5 %collective-permute-start.37 = (bf16[768,512]{1,0:T(8,128)(2,1)S(1)}, bf16[768,512]{1,0:T(8,128)(2,1)S(1)}, u32[]{:S(2)}, u32[]{:S(2)}) collective-permute-start(bf16[768,512]{1,0:T(8,128)(2,1)S(1)} %get-tuple-element.241), channel_id=1, source_target_pairs={{0,1},{1,0},{2,3},{3,2},{4,5},{5,4},{6,7},{7,6},{8,9},{9,8},{10,11... | collective-permute-start | bytes 2359304 | tf_op jit(solution)/shard_map/ppermute | solution.py:17
  148.1 8.0 %collective-permute-start.35 = (bf16[192,1536]{1,0:T(8,128)(2,1)S(1)}, bf16[192,1536]{1,0:T(8,128)(2,1)S(1)}, u32[]{:S(2)}, u32[]{:S(2)}) collective-permute-start(bf16[192,1536]{1,0:T(8,128)(2,1)S(1)} %pad_maximum_fusion.1), channel_id=1, source_target_pairs={{0,1},{1,0},{2,3},{3,2},{4,5},{5,4},{6,7},{7,6},{8,9},{9,8},{10,11... | collective-permute-start | bytes 1769480 | tf_op jit(solution)/shard_map/ppermute | solution.py:17
  (28 other events, 291.8 us)

commit v4 on v3

--- a/solution.py
+++ b/solution.py
@@ -135,11 +135,12 @@
 def collect_kernel(experts_all, capacity, gated, index_ref, routes_ref, *refs):
     if gated:
         gates_ref, refs = refs[0], refs[1:]
-    blocks, other_ref, out_ref = refs[:-2], refs[-2], refs[-1]
+    lines = experts_all // 2
+    blocks, others, out_ref = refs[:lines], refs[lines:-1], refs[-1]
     rows = routes_ref.shape[1]
     feature = out_ref.shape[1] // HEADS
     me, core = index_ref[0] // SPLIT, index_ref[0] % 2
-    values = jnp.concatenate([block[:capacity] for block in blocks] + [other_ref[...]], axis=0)
+    values = jnp.concatenate([block[:capacity] for block in blocks] + [other[...] for other in others], axis=0)
     slot = iota((rows, experts_all * capacity), 1)
     hits = []
     for distance, rank in ranks(me, routes_ref, experts_all):
@@ -179,10 +180,10 @@
     )(index, *operands)
 
 
-def collect(index, routes, gates, blocks, other, tok_local, experts_all, capacity):
-    feature = other.shape[1]
+def collect(index, routes, gates, blocks, others, tok_local, experts_all, capacity):
+    feature = blocks[0].shape[1]
     vmem = pl.BlockSpec(memory_space=pltpu.VMEM)
-    operands = [routes, *gates, *blocks, other]
+    operands = [routes, *gates, *blocks, *others]
     return pl.pallas_call(
         functools.partial(collect_kernel, experts_all, capacity, bool(gates)),
         out_shape=jax.ShapeDtypeStruct((tok_local, HEADS * feature), jnp.bfloat16),
@@ -280,24 +281,28 @@
     return dict(zip(group, call(kernel, [(shape, jnp.bfloat16)] * len(group), mine, far)))
 
 
-def weight_kernel(lefts, rights, others, *refs):
-    both = lefts + rights
+def weight_kernel(lefts, rights, *refs):
     left = jnp.concatenate([ref[...] for ref in refs[:lefts]], axis=0)
-    right = jnp.concatenate([ref[...] for ref in refs[lefts:both]], axis=0)
+    right = jnp.concatenate([ref[...] for ref in refs[lefts : lefts + rights]], axis=0)
     total = dot(left, right, ((0,), (0,)))
-    if others:
-        other = jnp.concatenate([ref[...] for ref in refs[both : both + others]], axis=0)
-        total = total + other.astype(jnp.float32)
-    outs = refs[both + others :]
+    outs = refs[lefts + rights :]
     rows = outs[0].shape[0]
     for i, out in enumerate(outs):
         out[...] = total[i * rows : (i + 1) * rows].astype(out.dtype)
 
 
-def weight_grad(dtype, cuts, left, right, others=()):
+def weight_grad(dtype, cuts, left, right):
     shape = (left[0].shape[1] // cuts, right[0].shape[1])
-    kernel = functools.partial(weight_kernel, len(left), len(right), len(others))
-    return call(kernel, [(shape, dtype)] * cuts, *left, *right, *others)
+    kernel = functools.partial(weight_kernel, len(left), len(right))
+    return call(kernel, [(shape, dtype)] * cuts, *left, *right)
+
+
+def joined_kernel(own, other, out):
+    out[...] = own[...] + other[...].astype(jnp.float32)
+
+
+def joined_weights(own, other):
+    return call(joined_kernel, [(own.shape, jnp.float32)], own, other)[0]
 
 
 def hop(value, line):
@@ -404,6 +409,7 @@
     order.done(b_sum[far[0]])
     b_far = hops(b_sum, far)
     m_home |= come(m_far)
+    m_near = hops(m_sum, near)
     b_sum |= added(back1, order.wait(b1_far), mid)
     order.done(b_sum[mid[0]])
     b_mid = hops(b_sum, mid)
@@ -411,34 +417,44 @@
     order.done(back0_far)
     b0_far = across(back0_far)
     b_home = come(b_far)
-    m_late = hops(m_sum, near)
-    m_home |= come({m: m_late[m] for m in near[:1]})
+    m_other = order.wait(core(halves(m_home)))
 
     x_all = (x0, x0_far, x1, x1_far, x2, x2_far)
     g_all = (g0, g0_far, g1, g1_far, g2, g2_far)
     hid_own, hid_other = zip(hid0, hid1, hid2)
     dpre_own, dpre_other = zip(dpre0, dpre1, dpre2)
-    down_part = weight_grad(jnp.bfloat16, 2, (order.now(hid0[1]), *hid_other[1:]), g_all)
-    up_part = weight_grad(jnp.bfloat16, 2, x_all, (order.now(dpre0[1]), *dpre_other[1:]))
-    order.done(down_part[0])
-    order.done(up_part[0])
+    (down_part,) = weight_grad(jnp.bfloat16, 1, (order.now(hid0[1]), *hid_other[1:]), g_all)
+    (up_part,) = weight_grad(jnp.bfloat16, 1, x_all, (order.now(dpre0[1]), *dpre_other[1:]))
+    order.done(down_part)
+    order.done(up_part)
+    (down_own_part,) = weight_grad(jnp.float32, 1, (order.now(hid0[0]), *hid_own[1:]), g_all)
+    order.done(down_own_part)
+    (up_own_part,) = weight_grad(jnp.float32, 1, x_all, (order.now(dpre0[0]), *dpre_own[1:]))
+    order.done(up_own_part)
+    down_sent, up_sent = core(down_part), core(up_part)
     b_home |= come(b_mid)
-    m_home |= come({m: m_late[m] for m in near[1:]})
-    m_other = core(halves(m_home))
+    m_near = come(m_near)
+    m_near_other = core(halves(m_near))
     b_sum |= added(back0, order.wait(b0_far), near)
     order.done(b_sum[near[0]])
     b_near = hops(b_sum, near)
-    down_sent, up_sent = [core(part) for part in down_part], [core(part) for part in up_part]
-    mixed = collect(index, routes, (gates,), ordered(m_home), order.wait(m_other), *sizes)
+    mixed = collect(
+        index,
+        routes,
+        (gates,),
+        ordered(m_home | m_near),
+        [order.wait(m_near_other), m_other],
+        *sizes,
+    )
     order.done(mixed)
     b_home |= come(b_near)
     b_other = core(halves(b_home))
-    (grad_down,) = weight_grad(jnp.float32, 1, hid_own, g_all, order.wait(*down_sent))
+    grad_down = joined_weights(down_own_part, order.wait(down_sent))
     order.done(grad_down)
-    (grad_up,) = weight_grad(jnp.float32, 1, x_all, dpre_own, order.wait(*up_sent))
+    grad_up = joined_weights(up_own_part, order.wait(up_sent))
     order.done(grad_up)
     b_other = order.wait(b_other)
-    token_grad = collect(index, routes, (), ordered(b_home), b_other, *sizes)
+    token_grad = collect(index, routes, (), ordered(b_home), [b_other], *sizes)
     return (mixed, token_grad, grad_up[None], grad_down[None])
 
 

time: 158 us -> 156 us (0.987)
  starting transfers between devices: 69.2 us -> 60.2 us
  waiting for transfers between devices: 56.3 us -> 62.5 us
    ppermute x40 -> x39, starting transfers between devices: 69.2 us -> 60.2 us  [swap(): lax.ppermute(value, 'expert', [(i, i ^ bits ^ (odd_bits if i % 2 else 0))...]
    ppermute x40 -> x39, waiting for transfers between devices: 56.3 us -> 62.5 us  [swap(): lax.ppermute(value, 'expert', [(i, i ^ bits ^ (odd_bits if i % 2 else 0))...]
    pallas_call x16 -> x18, Pallas kernels: 22.4 us -> 23 us  [call(): pl.pallas_call(kernel, out_shape=[jax.ShapeDtypeStruct(shape, dtype) for...]
    unnamed x34 -> x22, local copies, waits for them, and re-layouts: 3.19 us -> 3.16 us
  transfers between devices with their start and end apart: 40 -> 39, of which waited for: 12 -> 14; matrix products, arithmetic and copies ran while one was open for 0% -> 0% of each run, Pallas kernels for 16% -> 17%
where the time goes in v4:
time: 156 us; the launch traced here: 155 us
  waiting for transfers between devices  62.5 us (40%)
  starting transfers between devices  60.2 us (39%)
  Pallas kernels  28.4 us (18%)
  local copies, waits for them, and re-layouts  3.28 us (2%)
    ppermute x39, waiting for transfers between devices, swap(): lax.ppermute(value, 'expert', [(i, i ^ bits ^ (odd_bits if i % 2 else 0))...  62.5 us
    ppermute x39, starting transfers between devices, swap(): lax.ppermute(value, 'expert', [(i, i ^ bits ^ (odd_bits if i % 2 else 0))...  60.2 us
    pallas_call x18, Pallas kernels, call(): pl.pallas_call(kernel, out_shape=[jax.ShapeDtypeStruct(shape, dtype) for...  23 us
    pallas_call x2, Pallas kernels, collect(): pl.pallas_call(functools.partial(collect_kernel, experts_all, capacity, b...  3.34 us
    unnamed x22, local copies, waits for them, and re-layouts  3.16 us
  transfers between devices with their start and end apart: 39, of which 14 were waited for; matrix products, arithmetic and copies ran while one was open for 0% of the time, Pallas kernels for 17%

profile of v4, /device:TPU:0, one launch (start us, length us, event | category | flops | bytes accessed | tf_op | source)
XLA Modules:
  0.0 155.5 jit_solution(14056345095536448483)
XLA Ops:
  6.7 3.0 %collective-permute-start.3 = (bf16[96,1536]{1,0:T(8,128)(2,1)S(1)}, bf16[96,1536]{1,0:T(8,128)(2,1)S(1)}, u32[]{:S(2)}, u32[]{:S(2)}) collective-permute-start(bf16[96,1536]{1,0:T(8,128)(2,1)S(1)} %get-tuple-element.131), channel_id=1, source_target_pairs={{0,8},{1,13},{2,10},{3,15},{4,12},{5,9},{6,14},{7,11},{8,0},{9,5},... | collective-permute-start | bytes 884744 | tf_op jit(solution)/shard_map/ppermute | solution.py:17
  9.7 2.6 %collective-permute-start.5 = (bf16[96,1536]{1,0:T(8,128)(2,1)S(1)}, bf16[96,1536]{1,0:T(8,128)(2,1)S(1)}, u32[]{:S(2)}, u32[]{:S(2)}) collective-permute-start(bf16[96,1536]{1,0:T(8,128)(2,1)S(1)} %get-tuple-element.136), channel_id=1, source_target_pairs={{0,16},{1,21},{2,18},{3,23},{4,20},{5,17},{6,22},{7,19},{8,24},{9,... | collective-permute-start | bytes 884744 | tf_op jit(solution)/shard_map/ppermute | solution.py:17
  12.3 8.8 %collective-permute-done.3 = bf16[96,1536]{1,0:T(8,128)(2,1)S(1)} collective-permute-done((bf16[96,1536]{1,0:T(8,128)(2,1)S(1)}, bf16[96,1536]{1,0:T(8,128)(2,1)S(1)}, u32[]{:S(2)}, u32[]{:S(2)}) %collective-permute-start.3) | collective-permute-done | bytes 294944 | tf_op jit(solution)/shard_map/ppermute | solution.py:17
  21.2 2.7 %collective-permute-start.4 = (bf16[192,1536]{1,0:T(8,128)(2,1)S(1)}, bf16[192,1536]{1,0:T(8,128)(2,1)S(1)}, u32[]{:S(2)}, u32[]{:S(2)}) collective-permute-start(bf16[192,1536]{1,0:T(8,128)(2,1)S(1)} %constant_dynamic-update-slice_fusion.mine.refs_0_), channel_id=1, source_target_pairs={{0,2},{1,3},{2,0},{3,1},{4,6},{5,7},{6,4},{7,5},{8,10},{9,11},{10,... | collective-permute-start | bytes 1769480 | tf_op jit(solution)/shard_map/ppermute | solution.py:17
  23.9 3.8 %collective-permute-start.8 = (bf16[32,6144]{1,0:T(8,128)(2,1)S(1)}, bf16[32,6144]{1,0:T(8,128)(2,1)S(1)}, u32[]{:S(2)}, u32[]{:S(2)}) collective-permute-start(bf16[32,6144]{1,0:T(8,128)(2,1)S(1)} %copy-done.6), channel_id=1, source_target_pairs={{0,1},{1,0},{2,3},{3,2},{4,5},{5,4},{6,7},{7,6},{8,9},{9,8},{10,11... | collective-permute-start | bytes 1179656 | tf_op jit(solution)/shard_map/ppermute | solution.py:17
  27.8 2.5 %collective-permute-start.11 = (bf16[96,1536]{1,0:T(8,128)(2,1)S(1)}, bf16[96,1536]{1,0:T(8,128)(2,1)S(1)}, u32[]{:S(2)}, u32[]{:S(2)}) collective-permute-start(bf16[96,1536]{1,0:T(8,128)(2,1)S(1)} %get-tuple-element.152), channel_id=1, source_target_pairs={{0,24},{1,29},{2,26},{3,31},{4,28},{5,25},{6,30},{7,27},{8,16},{9,... | collective-permute-start | bytes 884744 | tf_op jit(solution)/shard_map/ppermute | solution.py:17
  32.8 3.3 %collective-permute-done.4.far.refs_1_ = bf16[192,1536]{1,0:T(8,128)(2,1)S(1)} collective-permute-done((bf16[192,1536]{1,0:T(8,128)(2,1)S(1)}, bf16[192,1536]{1,0:T(8,128)(2,1)S(1)}, u32[]{:S(2)}, u32[]{:S(2)}) %collective-permute-start.4) | collective-permute-done | bytes 589856 | tf_op jit(solution)/shard_map/ppermute | solution.py:17
  37.5 2.7 %shard_map.95 = (f32[384,512]{1,0:T(8,128)S(1)}, f32[384,512]{1,0:T(8,128)S(1)}, bf16[384,512]{1,0:T(8,128)(2,1)S(1)}, bf16[384,512]{1,0:T(8,128)(2,1)S(1)}, bf1...) custom-call(bf16[192,1536]{1,0:T(8,128)(2,1)S(1)} %constant_dynamic-update-slice_fusion.mine.refs_0_, ...), custom_call_target="tpu_custom_call" | custom-call | flops 1 | bytes 1 | tf_op jit(solution)/shard_map/pallas_call | solution.py:203
  40.2 2.5 %collective-permute-start.10 = (bf16[192,1536]{1,0:T(8,128)(2,1)S(1)}, bf16[192,1536]{1,0:T(8,128)(2,1)S(1)}, u32[]{:S(2)}, u32[]{:S(2)}) collective-permute-start(bf16[192,1536]{1,0:T(8,128)(2,1)S(1)} %get-tuple-element.150), channel_id=1, source_target_pairs={{0,2},{1,3},{2,0},{3,1},{4,6},{5,7},{6,4},{7,5},{8,10},{9,11},{10,... | collective-permute-start | bytes 1769480 | tf_op jit(solution)/shard_map/ppermute | solution.py:17
  42.8 3.3 %collective-permute-start.17 = (bf16[96,1536]{1,0:T(8,128)(2,1)S(1)}, bf16[96,1536]{1,0:T(8,128)(2,1)S(1)}, u32[]{:S(2)}, u32[]{:S(2)}) collective-permute-start(bf16[96,1536]{1,0:T(8,128)(2,1)S(1)} %get-tuple-element.168), channel_id=1, source_target_pairs={{0,24},{1,29},{2,26},{3,31},{4,28},{5,25},{6,30},{7,27},{8,16},{9,... | collective-permute-start | bytes 884744 | tf_op jit(solution)/shard_map/ppermute | solution.py:17
  49.2 11.6 %collective-permute-done.12.far.refs_5_ = bf16[96,1536]{1,0:T(8,128)(2,1)S(1)} collective-permute-done((bf16[96,1536]{1,0:T(8,128)(2,1)S(1)}, bf16[96,1536]{1,0:T(8,128)(2,1)S(1)}, u32[]{:S(2)}, u32[]{:S(2)}) %collective-permute-start.12) | collective-permute-done | bytes 294944 | tf_op jit(solution)/shard_map/ppermute | solution.py:17
  62.3 2.5 %collective-permute-start.14 = (bf16[96,1536]{1,0:T(8,128)(2,1)S(1)}, bf16[96,1536]{1,0:T(8,128)(2,1)S(1)}, u32[]{:S(2)}, u32[]{:S(2)}) collective-permute-start(bf16[96,1536]{1,0:T(8,128)(2,1)S(1)} %get-tuple-element.163), channel_id=1, source_target_pairs={{0,2},{1,3},{2,0},{3,1},{4,6},{5,7},{6,4},{7,5},{8,10},{9,11},{10,... | collective-permute-start | bytes 884744 | tf_op jit(solution)/shard_map/ppermute | solution.py:17
  65.0 2.1 %collective-permute-done.16.far = bf16[96,1536]{1,0:T(8,128)(2,1)S(1)} collective-permute-done((bf16[96,1536]{1,0:T(8,128)(2,1)S(1)}, bf16[96,1536]{1,0:T(8,128)(2,1)S(1)}, u32[]{:S(2)}, u32[]{:S(2)}) %collective-permute-start.16) | collective-permute-done | bytes 294944 | tf_op jit(solution)/shard_map/ppermute | solution.py:17
  69.2 2.4 %collective-permute-start.19 = (bf16[96,1536]{1,0:T(8,128)(2,1)S(1)}, bf16[96,1536]{1,0:T(8,128)(2,1)S(1)}, u32[]{:S(2)}, u32[]{:S(2)}) collective-permute-start(bf16[96,1536]{1,0:T(8,128)(2,1)S(1)} %collective-permute-done.17.mine.refs_7_), channel_id=1, source_target_pairs={{0,2},{1,3},{2,0},{3,1},{4,6},{5,7},{6,4},{7,5},{8,10},{9,11},{10,... | collective-permute-start | bytes 884744 | tf_op jit(solution)/shard_map/ppermute | solution.py:17
  73.4 4.3 %collective-permute-start.24 = (bf16[96,1536]{1,0:T(8,128)(2,1)S(1)}, bf16[96,1536]{1,0:T(8,128)(2,1)S(1)}, u32[]{:S(2)}, u32[]{:S(2)}) collective-permute-start(bf16[96,1536]{1,0:T(8,128)(2,1)S(1)} %shard_map.99), channel_id=1, source_target_pairs={{0,16},{1,21},{2,18},{3,23},{4,20},{5,17},{6,22},{7,19},{8,24},{9,... | collective-permute-start | bytes 884744 | tf_op jit(solution)/shard_map/ppermute | solution.py:17
  77.8 1.9 %collective-permute-done.19.far.refs_8_ = bf16[96,1536]{1,0:T(8,128)(2,1)S(1)} collective-permute-done((bf16[96,1536]{1,0:T(8,128)(2,1)S(1)}, bf16[96,1536]{1,0:T(8,128)(2,1)S(1)}, u32[]{:S(2)}, u32[]{:S(2)}) %collective-permute-start.19) | collective-permute-done | bytes 294944 | tf_op jit(solution)/shard_map/ppermute | solution.py:17
  79.7 2.2 %shard_map.101 = (bf16[192,512]{1,0:T(8,128)(2,1)S(1)}, bf16[192,512]{1,0:T(8,128)(2,1)S(1)}, bf16[96,1536]{1,0:T(8,128)(2,1)S(1)}, bf16[96,1536]{1,0:T(8,128)(2,1)S(1)}) custom-call(bf16[96,1536]{1,0:T(8,128)(2,1)S(1)} %collective-permute-done.17.mine.refs_7_, bf16[96,1536]{1,0:T(8,128)(2,1)S(1)} %collective-permute-done.19.far.refs_8_, ...), custom_call_target="tpu_custom_call" | custom-call | flops 1 | bytes 1 | tf_op jit(solution)/shard_map/pallas_call | solution.py:203
  82.0 2.5 %collective-permute-start.22 = (bf16[96,1536]{1,0:T(8,128)(2,1)S(1)}, bf16[96,1536]{1,0:T(8,128)(2,1)S(1)}, u32[]{:S(2)}, u32[]{:S(2)}) collective-permute-start(bf16[96,1536]{1,0:T(8,128)(2,1)S(1)} %get-tuple-element.184), channel_id=1, source_target_pairs={{0,2},{1,3},{2,0},{3,1},{4,6},{5,7},{6,4},{7,5},{8,10},{9,11},{10,... | collective-permute-start | bytes 884744 | tf_op jit(solution)/shard_map/ppermute | solution.py:17
  84.6 3.6 %collective-permute-start.18 = (bf16[96,1536]{1,0:T(8,128)(2,1)S(1)}, bf16[96,1536]{1,0:T(8,128)(2,1)S(1)}, u32[]{:S(2)}, u32[]{:S(2)}) collective-permute-start(bf16[96,1536]{1,0:T(8,128)(2,1)S(1)} %shard_map.100), channel_id=1, source_target_pairs={{0,24},{1,29},{2,26},{3,31},{4,28},{5,25},{6,30},{7,27},{8,16},{9,... | collective-permute-start | bytes 884744 | tf_op jit(solution)/shard_map/ppermute | solution.py:17
  88.2 8.6 %collective-permute-done.24.refs_3_ = bf16[96,1536]{1,0:T(8,128)(2,1)S(1)} collective-permute-done((bf16[96,1536]{1,0:T(8,128)(2,1)S(1)}, bf16[96,1536]{1,0:T(8,128)(2,1)S(1)}, u32[]{:S(2)}, u32[]{:S(2)}) %collective-permute-start.24) | collective-permute-done | bytes 294944 | tf_op jit(solution)/shard_map/ppermute | solution.py:17
  96.8 2.2 %shard_map.102 = (bf16[192,512]{1,0:T(8,128)(2,1)S(1)}, bf16[192,512]{1,0:T(8,128)(2,1)S(1)}, bf16[96,1536]{1,0:T(8,128)(2,1)S(1)}, bf16[96,1536]{1,0:T(8,128)(2,1)S(1)}) custom-call(bf16[96,1536]{1,0:T(8,128)(2,1)S(1)} %collective-permute-done.15.mine.refs_5_, bf16[96,1536]{1,0:T(8,128)(2,1)S(1)} %collective-permute-done.23.far.refs_6_, ...), custom_call_target="tpu_custom_call" | custom-call | flops 1 | bytes 1 | tf_op jit(solution)/shard_map/pallas_call | solution.py:203
  99.3 12.1 %collective-permute-done.27.far = bf16[96,1536]{1,0:T(8,128)(2,1)S(1)} collective-permute-done((bf16[96,1536]{1,0:T(8,128)(2,1)S(1)}, bf16[96,1536]{1,0:T(8,128)(2,1)S(1)}, u32[]{:S(2)}, u32[]{:S(2)}) %collective-permute-start.27) | collective-permute-done | bytes 294944 | tf_op jit(solution)/shard_map/ppermute | solution.py:17
  111.5 2.8 %shard_map.105 = (bf16[384,512]{1,0:T(8,128)(2,1)S(1)}, bf16[384,512]{1,0:T(8,128)(2,1)S(1)}, bf16[192,1536]{1,0:T(8,128)(2,1)S(1)}, bf16[192,1536]{1,0:T(8,128)(2,1)S(1)}) custom-call(bf16[192,1536]{1,0:T(8,128)(2,1)S(1)} %constant_dynamic-update-slice_fusion.2.mine.refs_3_, bf16[192,1536]{1,0:T(8,128)(2,1)S(1)} %collective-permute-done.30.far.refs_4_, ...), custom_call_target="tpu_custom_call" | custom-call | flops 1 | bytes 1 | tf_op jit(solution)/shard_map/pallas_call | solution.py:203
  114.3 2.4 %collective-permute-start.31 = (bf16[96,1536]{1,0:T(8,128)(2,1)S(1)}, bf16[96,1536]{1,0:T(8,128)(2,1)S(1)}, u32[]{:S(2)}, u32[]{:S(2)}) collective-permute-start(bf16[96,1536]{1,0:T(8,128)(2,1)S(1)} %pad_maximum_fusion.1), channel_id=1, source_target_pairs={{0,1},{1,0},{2,3},{3,2},{4,5},{5,4},{6,7},{7,6},{8,9},{9,8},{10,11... | collective-permute-start | bytes 884744 | tf_op jit(solution)/shard_map/ppermute | solution.py:17
  116.7 4.7 %collective-permute-start.28 = (bf16[96,1536]{1,0:T(8,128)(2,1)S(1)}, bf16[96,1536]{1,0:T(8,128)(2,1)S(1)}, u32[]{:S(2)}, u32[]{:S(2)}) collective-permute-start(bf16[96,1536]{1,0:T(8,128)(2,1)S(1)} %shard_map.104), channel_id=1, source_target_pairs={{0,16},{1,21},{2,18},{3,23},{4,20},{5,17},{6,22},{7,19},{8,24},{9,... | collective-permute-start | bytes 884744 | tf_op jit(solution)/shard_map/ppermute | solution.py:17
  129.4 2.8 %collective-permute-start.38 = (bf16[512,1536]{1,0:T(8,128)(2,1)S(1)}, bf16[512,1536]{1,0:T(8,128)(2,1)S(1)}, u32[]{:S(2)}, u32[]{:S(2)}) collective-permute-start(bf16[512,1536]{1,0:T(8,128)(2,1)S(1)} %shard_map.106), channel_id=1, source_target_pairs={{0,1},{1,0},{2,3},{3,2},{4,5},{5,4},{6,7},{7,6},{8,9},{9,8},{10,11... | collective-permute-start | bytes 4718600 | tf_op jit(solution)/shard_map/ppermute | solution.py:17
  132.2 3.3 %collective-permute-done.28.refs_2_ = bf16[96,1536]{1,0:T(8,128)(2,1)S(1)} collective-permute-done((bf16[96,1536]{1,0:T(8,128)(2,1)S(1)}, bf16[96,1536]{1,0:T(8,128)(2,1)S(1)}, u32[]{:S(2)}, u32[]{:S(2)}) %collective-permute-start.28) | collective-permute-done | bytes 294944 | tf_op jit(solution)/shard_map/ppermute | solution.py:17
  139.4 1.7 %shard_map.111 = bf16[32,6144]{1,0:T(8,128)(2,1)} custom-call(s32[1]{0:T(128)} %bitcast.index_ref, s32[2,128]{1,0:T(2,128)S(1)} %bitcast.24, f32[2,128]{1,0:T(2,128)S(1)} %bitcast.28, bf16[96,1536]{1,0:T(8,128)(2,1)S(1)} %collective-permute-done.25.refs_1_, bf16[96,1536]{1,0:T(8,128)(2,1)S(1)} %collective-permute-done.26.refs_2_, ...), custom_call_target="tpu_custom_call" | custom-call | flops 1 | bytes 1 | tf_op jit(solution)/shard_map/pallas_call | solution.py:187
  141.1 6.2 %collective-permute-done.35.refs_1_ = bf16[96,1536]{1,0:T(8,128)(2,1)S(1)} collective-permute-done((bf16[96,1536]{1,0:T(8,128)(2,1)S(1)}, bf16[96,1536]{1,0:T(8,128)(2,1)S(1)}, u32[]{:S(2)}, u32[]{:S(2)}) %collective-permute-start.35) | collective-permute-done | bytes 294944 | tf_op jit(solution)/shard_map/ppermute | solution.py:17
  147.4 2.6 %collective-permute-start.36 = (bf16[192,1536]{1,0:T(8,128)(2,1)S(1)}, bf16[192,1536]{1,0:T(8,128)(2,1)S(1)}, u32[]{:S(2)}, u32[]{:S(2)}) collective-permute-start(bf16[192,1536]{1,0:T(8,128)(2,1)S(1)} %pad_maximum_fusion), channel_id=1, source_target_pairs={{0,1},{1,0},{2,3},{3,2},{4,5},{5,4},{6,7},{7,6},{8,9},{9,8},{10,11... | collective-permute-start | bytes 1769480 | tf_op jit(solution)/shard_map/ppermute | solution.py:17
  150.0 1.9 %shard_map.112 = f32[512,1536]{1,0:T(8,128)} custom-call(f32[512,1536]{1,0:T(8,128)S(1)} %shard_map.108.own, bf16[512,1536]{1,0:T(8,128)(2,1)S(1)} %collective-permute-done.38.other), custom_call_target="tpu_custom_call" | custom-call | flops 1 | bytes 1 | tf_op jit(solution)/shard_map/pallas_call | solution.py:203
  151.9 1.9 %shard_map.113 = f32[1536,512]{1,0:T(8,128)} custom-call(f32[1536,512]{1,0:T(8,128)S(1)} %shard_map.109.own, bf16[1536,512]{1,0:T(8,128)(2,1)S(1)} %collective-permute-done.37.other), custom_call_target="tpu_custom_call" | custom-call | flops 1 | bytes 1 | tf_op jit(solution)/shard_map/pallas_call | solution.py:203
  (104 shorter events, 32.7 us)
Async XLA Ops:
  5.4 18.5 %collective-permute-start.6 = (bf16[1536,512]{1,0:T(8,128)(2,1)}, bf16[1536,512]{1,0:T(8,128)(2,1)S(1)}, u32[]{:S(2)}, u32[]{:S(2)}) collective-permute-start(bf16[1536,512]{1,0:T(8,128)(2,1)} %bitcast.7), channel_id=1, source_target_pairs={{0,1},{1,0},{2,3},{3,2},{4,5},{5,4},{6,7},{7,6},{8,9},{9,8},{10,11... | collective-permute-start | bytes 4718600 | tf_op jit(solution)/shard_map/ppermute | solution.py:17
  5.9 18.0 %collective-permute-start.7 = (bf16[512,1536]{1,0:T(8,128)(2,1)}, bf16[512,1536]{1,0:T(8,128)(2,1)S(1)}, u32[]{:S(2)}, u32[]{:S(2)}) collective-permute-start(bf16[512,1536]{1,0:T(8,128)(2,1)} %bitcast.14), channel_id=1, source_target_pairs={{0,1},{1,0},{2,3},{3,2},{4,5},{5,4},{6,7},{7,6},{8,9},{9,8},{10,11... | collective-permute-start | bytes 4718600 | tf_op jit(solution)/shard_map/ppermute | solution.py:17
  6.7 14.4 %collective-permute-start.3 = (bf16[96,1536]{1,0:T(8,128)(2,1)S(1)}, bf16[96,1536]{1,0:T(8,128)(2,1)S(1)}, u32[]{:S(2)}, u32[]{:S(2)}) collective-permute-start(bf16[96,1536]{1,0:T(8,128)(2,1)S(1)} %get-tuple-element.131), channel_id=1, source_target_pairs={{0,8},{1,13},{2,10},{3,15},{4,12},{5,9},{6,14},{7,11},{8,0},{9,5},... | collective-permute-start | bytes 884744 | tf_op jit(solution)/shard_map/ppermute | solution.py:17
  9.7 14.2 %collective-permute-start.5 = (bf16[96,1536]{1,0:T(8,128)(2,1)S(1)}, bf16[96,1536]{1,0:T(8,128)(2,1)S(1)}, u32[]{:S(2)}, u32[]{:S(2)}) collective-permute-start(bf16[96,1536]{1,0:T(8,128)(2,1)S(1)} %get-tuple-element.136), channel_id=1, source_target_pairs={{0,16},{1,21},{2,18},{3,23},{4,20},{5,17},{6,22},{7,19},{8,24},{9,... | collective-permute-start | bytes 884744 | tf_op jit(solution)/shard_map/ppermute | solution.py:17
  21.2 15.0 %collective-permute-start.4 = (bf16[192,1536]{1,0:T(8,128)(2,1)S(1)}, bf16[192,1536]{1,0:T(8,128)(2,1)S(1)}, u32[]{:S(2)}, u32[]{:S(2)}) collective-permute-start(bf16[192,1536]{1,0:T(8,128)(2,1)S(1)} %constant_dynamic-update-slice_fusion.mine.refs_0_), channel_id=1, source_target_pairs={{0,2},{1,3},{2,0},{3,1},{4,6},{5,7},{6,4},{7,5},{8,10},{9,11},{10,... | collective-permute-start | bytes 1769480 | tf_op jit(solution)/shard_map/ppermute | solution.py:17
  23.9 7.8 %collective-permute-start.8 = (bf16[32,6144]{1,0:T(8,128)(2,1)S(1)}, bf16[32,6144]{1,0:T(8,128)(2,1)S(1)}, u32[]{:S(2)}, u32[]{:S(2)}) collective-permute-start(bf16[32,6144]{1,0:T(8,128)(2,1)S(1)} %copy-done.6), channel_id=1, source_target_pairs={{0,1},{1,0},{2,3},{3,2},{4,5},{5,4},{6,7},{7,6},{8,9},{9,8},{10,11... | collective-permute-start | bytes 1179656 | tf_op jit(solution)/shard_map/ppermute | solution.py:17
  27.8 15.0 %collective-permute-start.11 = (bf16[96,1536]{1,0:T(8,128)(2,1)S(1)}, bf16[96,1536]{1,0:T(8,128)(2,1)S(1)}, u32[]{:S(2)}, u32[]{:S(2)}) collective-permute-start(bf16[96,1536]{1,0:T(8,128)(2,1)S(1)} %get-tuple-element.152), channel_id=1, source_target_pairs={{0,24},{1,29},{2,26},{3,31},{4,28},{5,25},{6,30},{7,27},{8,16},{9,... | collective-permute-start | bytes 884744 | tf_op jit(solution)/shard_map/ppermute | solution.py:17
  30.2 12.6 %collective-permute-start.13 = (bf16[96,1536]{1,0:T(8,128)(2,1)S(1)}, bf16[96,1536]{1,0:T(8,128)(2,1)S(1)}, u32[]{:S(2)}, u32[]{:S(2)}) collective-permute-start(bf16[96,1536]{1,0:T(8,128)(2,1)S(1)} %collective-permute-done.5.mine.refs_2_), channel_id=1, source_target_pairs={{0,2},{1,3},{2,0},{3,1},{4,6},{5,7},{6,4},{7,5},{8,10},{9,11},{10,... | collective-permute-start | bytes 884744 | tf_op jit(solution)/shard_map/ppermute | solution.py:17
  40.2 24.6 %collective-permute-start.10 = (bf16[192,1536]{1,0:T(8,128)(2,1)S(1)}, bf16[192,1536]{1,0:T(8,128)(2,1)S(1)}, u32[]{:S(2)}, u32[]{:S(2)}) collective-permute-start(bf16[192,1536]{1,0:T(8,128)(2,1)S(1)} %get-tuple-element.150), channel_id=1, source_target_pairs={{0,2},{1,3},{2,0},{3,1},{4,6},{5,7},{6,4},{7,5},{8,10},{9,11},{10,... | collective-permute-start | bytes 1769480 | tf_op jit(solution)/shard_map/ppermute | solution.py:17
  42.8 18.0 %collective-permute-start.12 = (bf16[96,1536]{1,0:T(8,128)(2,1)S(1)}, bf16[96,1536]{1,0:T(8,128)(2,1)S(1)}, u32[]{:S(2)}, u32[]{:S(2)}) collective-permute-start(bf16[96,1536]{1,0:T(8,128)(2,1)S(1)} %collective-permute-done.11.mine.refs_4_), channel_id=1, source_target_pairs={{0,2},{1,3},{2,0},{3,1},{4,6},{5,7},{6,4},{7,5},{8,10},{9,11},{10,... | collective-permute-start | bytes 884744 | tf_op jit(solution)/shard_map/ppermute | solution.py:17
  42.8 22.1 %collective-permute-start.17 = (bf16[96,1536]{1,0:T(8,128)(2,1)S(1)}, bf16[96,1536]{1,0:T(8,128)(2,1)S(1)}, u32[]{:S(2)}, u32[]{:S(2)}) collective-permute-start(bf16[96,1536]{1,0:T(8,128)(2,1)S(1)} %get-tuple-element.168), channel_id=1, source_target_pairs={{0,24},{1,29},{2,26},{3,31},{4,28},{5,25},{6,30},{7,27},{8,16},{9,... | collective-permute-start | bytes 884744 | tf_op jit(solution)/shard_map/ppermute | solution.py:17
  47.7 19.4 %collective-permute-start.16 = (bf16[96,1536]{1,0:T(8,128)(2,1)S(1)}, bf16[96,1536]{1,0:T(8,128)(2,1)S(1)}, u32[]{:S(2)}, u32[]{:S(2)}) collective-permute-start(bf16[96,1536]{1,0:T(8,128)(2,1)S(1)} %get-tuple-element.166), channel_id=1, source_target_pairs={{0,2},{1,3},{2,0},{3,1},{4,6},{5,7},{6,4},{7,5},{8,10},{9,11},{10,... | collective-permute-start | bytes 884744 | tf_op jit(solution)/shard_map/ppermute | solution.py:17
  49.2 23.8 %collective-permute-start.15 = (bf16[96,1536]{1,0:T(8,128)(2,1)S(1)}, bf16[96,1536]{1,0:T(8,128)(2,1)S(1)}, u32[]{:S(2)}, u32[]{:S(2)}) collective-permute-start(bf16[96,1536]{1,0:T(8,128)(2,1)S(1)} %get-tuple-element.165), channel_id=1, source_target_pairs={{0,16},{1,21},{2,18},{3,23},{4,20},{5,17},{6,22},{7,19},{8,24},{9,... | collective-permute-start | bytes 884744 | tf_op jit(solution)/shard_map/ppermute | solution.py:17
  62.3 11.1 %collective-permute-start.14 = (bf16[96,1536]{1,0:T(8,128)(2,1)S(1)}, bf16[96,1536]{1,0:T(8,128)(2,1)S(1)}, u32[]{:S(2)}, u32[]{:S(2)}) collective-permute-start(bf16[96,1536]{1,0:T(8,128)(2,1)S(1)} %get-tuple-element.163), channel_id=1, source_target_pairs={{0,2},{1,3},{2,0},{3,1},{4,6},{5,7},{6,4},{7,5},{8,10},{9,11},{10,... | collective-permute-start | bytes 884744 | tf_op jit(solution)/shard_map/ppermute | solution.py:17
  67.2 10.6 %collective-permute-start.20 = (bf16[96,1536]{1,0:T(8,128)(2,1)S(1)}, bf16[96,1536]{1,0:T(8,128)(2,1)S(1)}, u32[]{:S(2)}, u32[]{:S(2)}) collective-permute-start(bf16[96,1536]{1,0:T(8,128)(2,1)S(1)} %get-tuple-element.176), channel_id=1, source_target_pairs={{0,0},{1,5},{2,2},{3,7},{4,4},{5,1},{6,6},{7,3},{8,8},{9,13},{10,1... | collective-permute-start | bytes 884744 | tf_op jit(solution)/shard_map/ppermute | solution.py:17
  68.0 9.8 %collective-permute-start.21 = (bf16[96,1536]{1,0:T(8,128)(2,1)S(1)}, bf16[96,1536]{1,0:T(8,128)(2,1)S(1)}, u32[]{:S(2)}, u32[]{:S(2)}) collective-permute-start(bf16[96,1536]{1,0:T(8,128)(2,1)S(1)} %get-tuple-element.178), channel_id=1, source_target_pairs={{0,8},{1,13},{2,10},{3,15},{4,12},{5,9},{6,14},{7,11},{8,0},{9,5},... | collective-permute-start | bytes 884744 | tf_op jit(solution)/shard_map/ppermute | solution.py:17
  69.2 10.5 %collective-permute-start.19 = (bf16[96,1536]{1,0:T(8,128)(2,1)S(1)}, bf16[96,1536]{1,0:T(8,128)(2,1)S(1)}, u32[]{:S(2)}, u32[]{:S(2)}) collective-permute-start(bf16[96,1536]{1,0:T(8,128)(2,1)S(1)} %collective-permute-done.17.mine.refs_7_), channel_id=1, source_target_pairs={{0,2},{1,3},{2,0},{3,1},{4,6},{5,7},{6,4},{7,5},{8,10},{9,11},{10,... | collective-permute-start | bytes 884744 | tf_op jit(solution)/shard_map/ppermute | solution.py:17
  73.0 23.8 %collective-permute-start.23 = (bf16[96,1536]{1,0:T(8,128)(2,1)S(1)}, bf16[96,1536]{1,0:T(8,128)(2,1)S(1)}, u32[]{:S(2)}, u32[]{:S(2)}) collective-permute-start(bf16[96,1536]{1,0:T(8,128)(2,1)S(1)} %collective-permute-done.15.mine.refs_5_), channel_id=1, source_target_pairs={{0,2},{1,3},{2,0},{3,1},{4,6},{5,7},{6,4},{7,5},{8,10},{9,11},{10,... | collective-permute-start | bytes 884744 | tf_op jit(solution)/shard_map/ppermute | solution.py:17
  73.4 23.4 %collective-permute-start.24 = (bf16[96,1536]{1,0:T(8,128)(2,1)S(1)}, bf16[96,1536]{1,0:T(8,128)(2,1)S(1)}, u32[]{:S(2)}, u32[]{:S(2)}) collective-permute-start(bf16[96,1536]{1,0:T(8,128)(2,1)S(1)} %shard_map.99), channel_id=1, source_target_pairs={{0,16},{1,21},{2,18},{3,23},{4,20},{5,17},{6,22},{7,19},{8,24},{9,... | collective-permute-start | bytes 884744 | tf_op jit(solution)/shard_map/ppermute | solution.py:17
  82.0 17.2 %collective-permute-start.22 = (bf16[96,1536]{1,0:T(8,128)(2,1)S(1)}, bf16[96,1536]{1,0:T(8,128)(2,1)S(1)}, u32[]{:S(2)}, u32[]{:S(2)}) collective-permute-start(bf16[96,1536]{1,0:T(8,128)(2,1)S(1)} %get-tuple-element.184), channel_id=1, source_target_pairs={{0,2},{1,3},{2,0},{3,1},{4,6},{5,7},{6,4},{7,5},{8,10},{9,11},{10,... | collective-permute-start | bytes 884744 | tf_op jit(solution)/shard_map/ppermute | solution.py:17
  84.5 27.0 %collective-permute-start.30 = (bf16[192,1536]{1,0:T(8,128)(2,1)S(1)}, bf16[192,1536]{1,0:T(8,128)(2,1)S(1)}, u32[]{:S(2)}, u32[]{:S(2)}) collective-permute-start(bf16[192,1536]{1,0:T(8,128)(2,1)S(1)} %constant_dynamic-update-slice_fusion.2.mine.refs_3_), channel_id=1, source_target_pairs={{0,2},{1,3},{2,0},{3,1},{4,6},{5,7},{6,4},{7,5},{8,10},{9,11},{10,... | collective-permute-start | bytes 1769480 | tf_op jit(solution)/shard_map/ppermute | solution.py:17
  84.6 14.7 %collective-permute-start.18 = (bf16[96,1536]{1,0:T(8,128)(2,1)S(1)}, bf16[96,1536]{1,0:T(8,128)(2,1)S(1)}, u32[]{:S(2)}, u32[]{:S(2)}) collective-permute-start(bf16[96,1536]{1,0:T(8,128)(2,1)S(1)} %shard_map.100), channel_id=1, source_target_pairs={{0,24},{1,29},{2,26},{3,31},{4,28},{5,25},{6,30},{7,27},{8,16},{9,... | collective-permute-start | bytes 884744 | tf_op jit(solution)/shard_map/ppermute | solution.py:17
  99.1 12.4 %collective-permute-start.27 = (bf16[96,1536]{1,0:T(8,128)(2,1)S(1)}, bf16[96,1536]{1,0:T(8,128)(2,1)S(1)}, u32[]{:S(2)}, u32[]{:S(2)}) collective-permute-start(bf16[96,1536]{1,0:T(8,128)(2,1)S(1)} %get-tuple-element.199), channel_id=1, source_target_pairs={{0,2},{1,3},{2,0},{3,1},{4,6},{5,7},{6,4},{7,5},{8,10},{9,11},{10,... | collective-permute-start | bytes 884744 | tf_op jit(solution)/shard_map/ppermute | solution.py:17
  99.2 15.1 %collective-permute-start.29 = (bf16[96,1536]{1,0:T(8,128)(2,1)S(1)}, bf16[96,1536]{1,0:T(8,128)(2,1)S(1)}, u32[]{:S(2)}, u32[]{:S(2)}) collective-permute-start(bf16[96,1536]{1,0:T(8,128)(2,1)S(1)} %shard_map.103), channel_id=1, source_target_pairs={{0,24},{1,29},{2,26},{3,31},{4,28},{5,25},{6,30},{7,27},{8,16},{9,... | collective-permute-start | bytes 884744 | tf_op jit(solution)/shard_map/ppermute | solution.py:17
  114.3 9.4 %collective-permute-start.31 = (bf16[96,1536]{1,0:T(8,128)(2,1)S(1)}, bf16[96,1536]{1,0:T(8,128)(2,1)S(1)}, u32[]{:S(2)}, u32[]{:S(2)}) collective-permute-start(bf16[96,1536]{1,0:T(8,128)(2,1)S(1)} %pad_maximum_fusion.1), channel_id=1, source_target_pairs={{0,1},{1,0},{2,3},{3,2},{4,5},{5,4},{6,7},{7,6},{8,9},{9,8},{10,11... | collective-permute-start | bytes 884744 | tf_op jit(solution)/shard_map/ppermute | solution.py:17
  116.7 18.8 %collective-permute-start.28 = (bf16[96,1536]{1,0:T(8,128)(2,1)S(1)}, bf16[96,1536]{1,0:T(8,128)(2,1)S(1)}, u32[]{:S(2)}, u32[]{:S(2)}) collective-permute-start(bf16[96,1536]{1,0:T(8,128)(2,1)S(1)} %shard_map.104), channel_id=1, source_target_pairs={{0,16},{1,21},{2,18},{3,23},{4,20},{5,17},{6,22},{7,19},{8,24},{9,... | collective-permute-start | bytes 884744 | tf_op jit(solution)/shard_map/ppermute | solution.py:17
  121.5 16.6 %collective-permute-start.33 = (bf16[192,1536]{1,0:T(8,128)(2,1)S(1)}, bf16[192,1536]{1,0:T(8,128)(2,1)S(1)}, u32[]{:S(2)}, u32[]{:S(2)}) collective-permute-start(bf16[192,1536]{1,0:T(8,128)(2,1)S(1)} %get-tuple-element.232), channel_id=1, source_target_pairs={{0,2},{1,3},{2,0},{3,1},{4,6},{5,7},{6,4},{7,5},{8,10},{9,11},{10,... | collective-permute-start | bytes 1769480 | tf_op jit(solution)/shard_map/ppermute | solution.py:17
  122.9 12.6 %collective-permute-start.25 = (bf16[96,1536]{1,0:T(8,128)(2,1)S(1)}, bf16[96,1536]{1,0:T(8,128)(2,1)S(1)}, u32[]{:S(2)}, u32[]{:S(2)}) collective-permute-start(bf16[96,1536]{1,0:T(8,128)(2,1)S(1)} %get-tuple-element.195), channel_id=1, source_target_pairs={{0,0},{1,5},{2,2},{3,7},{4,4},{5,1},{6,6},{7,3},{8,8},{9,13},{10,1... | collective-permute-start | bytes 884744 | tf_op jit(solution)/shard_map/ppermute | solution.py:17
  123.6 13.3 %collective-permute-start.26 = (bf16[96,1536]{1,0:T(8,128)(2,1)S(1)}, bf16[96,1536]{1,0:T(8,128)(2,1)S(1)}, u32[]{:S(2)}, u32[]{:S(2)}) collective-permute-start(bf16[96,1536]{1,0:T(8,128)(2,1)S(1)} %get-tuple-element.197), channel_id=1, source_target_pairs={{0,8},{1,13},{2,10},{3,15},{4,12},{5,9},{6,14},{7,11},{8,0},{9,5},... | collective-permute-start | bytes 884744 | tf_op jit(solution)/shard_map/ppermute | solution.py:17
  129.4 20.6 %collective-permute-start.38 = (bf16[512,1536]{1,0:T(8,128)(2,1)S(1)}, bf16[512,1536]{1,0:T(8,128)(2,1)S(1)}, u32[]{:S(2)}, u32[]{:S(2)}) collective-permute-start(bf16[512,1536]{1,0:T(8,128)(2,1)S(1)} %shard_map.106), channel_id=1, source_target_pairs={{0,1},{1,0},{2,3},{3,2},{4,5},{5,4},{6,7},{7,6},{8,9},{9,8},{10,11... | collective-permute-start | bytes 4718600 | tf_op jit(solution)/shard_map/ppermute | solution.py:17
  135.5 16.4 %collective-permute-start.37 = (bf16[1536,512]{1,0:T(8,128)(2,1)S(1)}, bf16[1536,512]{1,0:T(8,128)(2,1)S(1)}, u32[]{:S(2)}, u32[]{:S(2)}) collective-permute-start(bf16[1536,512]{1,0:T(8,128)(2,1)S(1)} %shard_map.107), channel_id=1, source_target_pairs={{0,1},{1,0},{2,3},{3,2},{4,5},{5,4},{6,7},{7,6},{8,9},{9,8},{10,11... | collective-permute-start | bytes 4718600 | tf_op jit(solution)/shard_map/ppermute | solution.py:17
  138.9 8.4 %collective-permute-start.35 = (bf16[96,1536]{1,0:T(8,128)(2,1)S(1)}, bf16[96,1536]{1,0:T(8,128)(2,1)S(1)}, u32[]{:S(2)}, u32[]{:S(2)}) collective-permute-start(bf16[96,1536]{1,0:T(8,128)(2,1)S(1)} %get-tuple-element.239), channel_id=1, source_target_pairs={{0,8},{1,13},{2,10},{3,15},{4,12},{5,9},{6,14},{7,11},{8,0},{9,5},... | collective-permute-start | bytes 884744 | tf_op jit(solution)/shard_map/ppermute | solution.py:17
  (18 other events, 160.7 us)

commit v5 on v4

--- a/solution.py
+++ b/solution.py
@@ -96,7 +96,7 @@
     routes_refs, refs = refs[:2], refs[2:]
     if gated:
         gates_refs, refs = refs[:2], refs[2:]
-    tokens_refs, blocks = refs[:2], refs[2:]
+    tokens_refs, blocks = refs[:2], refs[-(experts_all // 2) :]
     rows = routes_refs[0].shape[1]
     me, core = index_ref[0] // SPLIT, index_ref[0] % 2
     slot = iota((experts_all * capacity, rows), 0)
@@ -166,18 +166,20 @@
         out_ref[:, h * feature : (h + 1) * feature] = total[h * per_head : (h + 1) * per_head]
 
 
-def place(index, routes, gates, tokens, experts_all, capacity):
+def place(index, routes, gates, tokens, experts_all, capacity, *ahead):
     feature = tokens[0].shape[1] // HEADS
     operands = [*routes, *gates, *tokens]
+    vmem = pl.BlockSpec(memory_space=pltpu.VMEM)
     block = jax.ShapeDtypeStruct((2 * capacity, feature), jnp.bfloat16)
     return pl.pallas_call(
         functools.partial(place_kernel, experts_all, capacity, bool(gates)),
         out_shape=[block] * (experts_all // 2),
-        in_specs=[pl.BlockSpec(memory_space=pltpu.SMEM)] + [pl.BlockSpec()] * len(operands),
-        out_specs=[pl.BlockSpec(memory_space=pltpu.VMEM)] * (experts_all // 2),
+        in_specs=[pl.BlockSpec(memory_space=pltpu.SMEM)] + [pl.BlockSpec()] * len(operands)
+        + [vmem] * len(ahead),
+        out_specs=[vmem] * (experts_all // 2),
         cost_estimate=FREE,
         compiler_params=pltpu.CompilerParams(vmem_limit_bytes=VMEM),
-    )(index, *operands)
+    )(index, *operands, *ahead)
 
 
 def collect(index, routes, gates, blocks, others, tok_local, experts_all, capacity):
@@ -369,6 +371,8 @@
         (cotangent, cotangent_other),
         experts_all,
         capacity,
+        up_own,
+        down_own,
     )
     order.done(g_blocks[0])
     pre0, hid0, part0, part0_far = forward(x0, order.wait(x0_far), weights)

time: 156 us -> 155 us (level)
  waiting for transfers between devices: 62.5 us -> 56 us
  starting transfers between devices: 60.2 us -> 65.6 us
    ppermute x39, waiting for transfers between devices: 62.5 us -> 56 us  [swap(): lax.ppermute(value, 'expert', [(i, i ^ bits ^ (odd_bits if i % 2 else 0))...]
    ppermute x39, starting transfers between devices: 60.2 us -> 65.6 us  [swap(): lax.ppermute(value, 'expert', [(i, i ^ bits ^ (odd_bits if i % 2 else 0))...]
  transfers between devices with their start and end apart: 39 -> 39, of which waited for: 14 -> 15; matrix products, arithmetic and copies ran while one was open for 0% -> 0% of each run, Pallas kernels for 17% -> 17%
where the time goes in v5:
time: 155 us; the launch traced here: 154 us
  starting transfers between devices  65.6 us (42%)
  waiting for transfers between devices  56 us (36%)
  Pallas kernels  28.3 us (18%)
  local copies, waits for them, and re-layouts  3.28 us (2%)
    ppermute x39, starting transfers between devices, swap(): lax.ppermute(value, 'expert', [(i, i ^ bits ^ (odd_bits if i % 2 else 0))...  65.6 us
    ppermute x39, waiting for transfers between devices, swap(): lax.ppermute(value, 'expert', [(i, i ^ bits ^ (odd_bits if i % 2 else 0))...  56 us
    pallas_call x18, Pallas kernels, call(): pl.pallas_call(kernel, out_shape=[jax.ShapeDtypeStruct(shape, dtype) for...  23 us
    pallas_call x2, Pallas kernels, collect(): pl.pallas_call(functools.partial(collect_kernel, experts_all, capacity, b...  3.34 us
    unnamed x22, local copies, waits for them, and re-layouts  3.15 us
  transfers between devices with their start and end apart: 39, of which 15 were waited for; matrix products, arithmetic and copies ran while one was open for 0% of the time, Pallas kernels for 17%

profile of v5, /device:TPU:0, one launch (start us, length us, event | category | flops | bytes accessed | tf_op | source)
XLA Modules:
  0.0 154.3 jit_solution(6494036009248923639)
XLA Ops:
  6.7 3.0 %collective-permute-start.3 = (bf16[96,1536]{1,0:T(8,128)(2,1)S(1)}, bf16[96,1536]{1,0:T(8,128)(2,1)S(1)}, u32[]{:S(2)}, u32[]{:S(2)}) collective-permute-start(bf16[96,1536]{1,0:T(8,128)(2,1)S(1)} %get-tuple-element.131), channel_id=1, source_target_pairs={{0,8},{1,13},{2,10},{3,15},{4,12},{5,9},{6,14},{7,11},{8,0},{9,5},... | collective-permute-start | bytes 884744 | tf_op jit(solution)/shard_map/ppermute | solution.py:17
  9.7 2.6 %collective-permute-start.5 = (bf16[96,1536]{1,0:T(8,128)(2,1)S(1)}, bf16[96,1536]{1,0:T(8,128)(2,1)S(1)}, u32[]{:S(2)}, u32[]{:S(2)}) collective-permute-start(bf16[96,1536]{1,0:T(8,128)(2,1)S(1)} %get-tuple-element.136), channel_id=1, source_target_pairs={{0,16},{1,21},{2,18},{3,23},{4,20},{5,17},{6,22},{7,19},{8,24},{9,... | collective-permute-start | bytes 884744 | tf_op jit(solution)/shard_map/ppermute | solution.py:17
  12.3 8.8 %collective-permute-done.3 = bf16[96,1536]{1,0:T(8,128)(2,1)S(1)} collective-permute-done((bf16[96,1536]{1,0:T(8,128)(2,1)S(1)}, bf16[96,1536]{1,0:T(8,128)(2,1)S(1)}, u32[]{:S(2)}, u32[]{:S(2)}) %collective-permute-start.3) | collective-permute-done | bytes 294944 | tf_op jit(solution)/shard_map/ppermute | solution.py:17
  21.2 2.7 %collective-permute-start.4 = (bf16[192,1536]{1,0:T(8,128)(2,1)S(1)}, bf16[192,1536]{1,0:T(8,128)(2,1)S(1)}, u32[]{:S(2)}, u32[]{:S(2)}) collective-permute-start(bf16[192,1536]{1,0:T(8,128)(2,1)S(1)} %constant_dynamic-update-slice_fusion.mine.refs_0_), channel_id=1, source_target_pairs={{0,2},{1,3},{2,0},{3,1},{4,6},{5,7},{6,4},{7,5},{8,10},{9,11},{10,... | collective-permute-start | bytes 1769480 | tf_op jit(solution)/shard_map/ppermute | solution.py:17
  23.9 3.8 %collective-permute-start.8 = (bf16[32,6144]{1,0:T(8,128)(2,1)S(1)}, bf16[32,6144]{1,0:T(8,128)(2,1)S(1)}, u32[]{:S(2)}, u32[]{:S(2)}) collective-permute-start(bf16[32,6144]{1,0:T(8,128)(2,1)S(1)} %copy-done.5), channel_id=1, source_target_pairs={{0,1},{1,0},{2,3},{3,2},{4,5},{5,4},{6,7},{7,6},{8,9},{9,8},{10,11... | collective-permute-start | bytes 1179656 | tf_op jit(solution)/shard_map/ppermute | solution.py:17
  27.8 2.5 %collective-permute-start.11 = (bf16[96,1536]{1,0:T(8,128)(2,1)S(1)}, bf16[96,1536]{1,0:T(8,128)(2,1)S(1)}, u32[]{:S(2)}, u32[]{:S(2)}) collective-permute-start(bf16[96,1536]{1,0:T(8,128)(2,1)S(1)} %get-tuple-element.152), channel_id=1, source_target_pairs={{0,24},{1,29},{2,26},{3,31},{4,28},{5,25},{6,30},{7,27},{8,16},{9,... | collective-permute-start | bytes 884744 | tf_op jit(solution)/shard_map/ppermute | solution.py:17
  34.2 1.9 %collective-permute-done.4.far.refs_1_ = bf16[192,1536]{1,0:T(8,128)(2,1)S(1)} collective-permute-done((bf16[192,1536]{1,0:T(8,128)(2,1)S(1)}, bf16[192,1536]{1,0:T(8,128)(2,1)S(1)}, u32[]{:S(2)}, u32[]{:S(2)}) %collective-permute-start.4) | collective-permute-done | bytes 589856 | tf_op jit(solution)/shard_map/ppermute | solution.py:17
  36.1 2.7 %shard_map.95 = (f32[384,512]{1,0:T(8,128)S(1)}, f32[384,512]{1,0:T(8,128)S(1)}, bf16[384,512]{1,0:T(8,128)(2,1)S(1)}, bf16[384,512]{1,0:T(8,128)(2,1)S(1)}, bf1...) custom-call(bf16[192,1536]{1,0:T(8,128)(2,1)S(1)} %constant_dynamic-update-slice_fusion.mine.refs_0_, ...), custom_call_target="tpu_custom_call" | custom-call | flops 1 | bytes 1 | tf_op jit(solution)/shard_map/pallas_call | solution.py:205
  38.8 2.5 %collective-permute-start.10 = (bf16[192,1536]{1,0:T(8,128)(2,1)S(1)}, bf16[192,1536]{1,0:T(8,128)(2,1)S(1)}, u32[]{:S(2)}, u32[]{:S(2)}) collective-permute-start(bf16[192,1536]{1,0:T(8,128)(2,1)S(1)} %get-tuple-element.150), channel_id=1, source_target_pairs={{0,2},{1,3},{2,0},{3,1},{4,6},{5,7},{6,4},{7,5},{8,10},{9,11},{10,... | collective-permute-start | bytes 1769480 | tf_op jit(solution)/shard_map/ppermute | solution.py:17
  42.4 3.7 %collective-permute-start.17 = (bf16[96,1536]{1,0:T(8,128)(2,1)S(1)}, bf16[96,1536]{1,0:T(8,128)(2,1)S(1)}, u32[]{:S(2)}, u32[]{:S(2)}) collective-permute-start(bf16[96,1536]{1,0:T(8,128)(2,1)S(1)} %get-tuple-element.168), channel_id=1, source_target_pairs={{0,24},{1,29},{2,26},{3,31},{4,28},{5,25},{6,30},{7,27},{8,16},{9,... | collective-permute-start | bytes 884744 | tf_op jit(solution)/shard_map/ppermute | solution.py:17
  49.2 12.7 %collective-permute-done.12.far.refs_5_ = bf16[96,1536]{1,0:T(8,128)(2,1)S(1)} collective-permute-done((bf16[96,1536]{1,0:T(8,128)(2,1)S(1)}, bf16[96,1536]{1,0:T(8,128)(2,1)S(1)}, u32[]{:S(2)}, u32[]{:S(2)}) %collective-permute-start.12) | collective-permute-done | bytes 294944 | tf_op jit(solution)/shard_map/ppermute | solution.py:17
  63.4 2.0 %collective-permute-start.14 = (bf16[96,1536]{1,0:T(8,128)(2,1)S(1)}, bf16[96,1536]{1,0:T(8,128)(2,1)S(1)}, u32[]{:S(2)}, u32[]{:S(2)}) collective-permute-start(bf16[96,1536]{1,0:T(8,128)(2,1)S(1)} %get-tuple-element.163), channel_id=1, source_target_pairs={{0,2},{1,3},{2,0},{3,1},{4,6},{5,7},{6,4},{7,5},{8,10},{9,11},{10,... | collective-permute-start | bytes 884744 | tf_op jit(solution)/shard_map/ppermute | solution.py:17
  65.6 2.6 %collective-permute-done.16.far = bf16[96,1536]{1,0:T(8,128)(2,1)S(1)} collective-permute-done((bf16[96,1536]{1,0:T(8,128)(2,1)S(1)}, bf16[96,1536]{1,0:T(8,128)(2,1)S(1)}, u32[]{:S(2)}, u32[]{:S(2)}) %collective-permute-start.16) | collective-permute-done | bytes 294944 | tf_op jit(solution)/shard_map/ppermute | solution.py:17
  69.2 2.0 %collective-permute-start.19 = (bf16[96,1536]{1,0:T(8,128)(2,1)S(1)}, bf16[96,1536]{1,0:T(8,128)(2,1)S(1)}, u32[]{:S(2)}, u32[]{:S(2)}) collective-permute-start(bf16[96,1536]{1,0:T(8,128)(2,1)S(1)} %collective-permute-done.17.mine.refs_7_), channel_id=1, source_target_pairs={{0,2},{1,3},{2,0},{3,1},{4,6},{5,7},{6,4},{7,5},{8,10},{9,11},{10,... | collective-permute-start | bytes 884744 | tf_op jit(solution)/shard_map/ppermute | solution.py:17
  71.3 1.8 %collective-permute-done.15.mine.refs_5_ = bf16[96,1536]{1,0:T(8,128)(2,1)S(1)} collective-permute-done((bf16[96,1536]{1,0:T(8,128)(2,1)S(1)}, bf16[96,1536]{1,0:T(8,128)(2,1)S(1)}, u32[]{:S(2)}, u32[]{:S(2)}) %collective-permute-start.15) | collective-permute-done | bytes 294944 | tf_op jit(solution)/shard_map/ppermute | solution.py:17
  74.5 2.1 %collective-permute-start.24 = (bf16[96,1536]{1,0:T(8,128)(2,1)S(1)}, bf16[96,1536]{1,0:T(8,128)(2,1)S(1)}, u32[]{:S(2)}, u32[]{:S(2)}) collective-permute-start(bf16[96,1536]{1,0:T(8,128)(2,1)S(1)} %shard_map.99), channel_id=1, source_target_pairs={{0,16},{1,21},{2,18},{3,23},{4,20},{5,17},{6,22},{7,19},{8,24},{9,... | collective-permute-start | bytes 884744 | tf_op jit(solution)/shard_map/ppermute | solution.py:17
  76.7 4.1 %collective-permute-done.19.far.refs_8_ = bf16[96,1536]{1,0:T(8,128)(2,1)S(1)} collective-permute-done((bf16[96,1536]{1,0:T(8,128)(2,1)S(1)}, bf16[96,1536]{1,0:T(8,128)(2,1)S(1)}, u32[]{:S(2)}, u32[]{:S(2)}) %collective-permute-start.19) | collective-permute-done | bytes 294944 | tf_op jit(solution)/shard_map/ppermute | solution.py:17
  80.9 2.2 %shard_map.101 = (bf16[192,512]{1,0:T(8,128)(2,1)S(1)}, bf16[192,512]{1,0:T(8,128)(2,1)S(1)}, bf16[96,1536]{1,0:T(8,128)(2,1)S(1)}, bf16[96,1536]{1,0:T(8,128)(2,1)S(1)}) custom-call(bf16[96,1536]{1,0:T(8,128)(2,1)S(1)} %collective-permute-done.17.mine.refs_7_, bf16[96,1536]{1,0:T(8,128)(2,1)S(1)} %collective-permute-done.19.far.refs_8_, ...), custom_call_target="tpu_custom_call" | custom-call | flops 1 | bytes 1 | tf_op jit(solution)/shard_map/pallas_call | solution.py:205
  83.1 2.0 %collective-permute-start.22 = (bf16[96,1536]{1,0:T(8,128)(2,1)S(1)}, bf16[96,1536]{1,0:T(8,128)(2,1)S(1)}, u32[]{:S(2)}, u32[]{:S(2)}) collective-permute-start(bf16[96,1536]{1,0:T(8,128)(2,1)S(1)} %get-tuple-element.184), channel_id=1, source_target_pairs={{0,2},{1,3},{2,0},{3,1},{4,6},{5,7},{6,4},{7,5},{8,10},{9,11},{10,... | collective-permute-start | bytes 884744 | tf_op jit(solution)/shard_map/ppermute | solution.py:17
  85.3 3.2 %collective-permute-start.18 = (bf16[96,1536]{1,0:T(8,128)(2,1)S(1)}, bf16[96,1536]{1,0:T(8,128)(2,1)S(1)}, u32[]{:S(2)}, u32[]{:S(2)}) collective-permute-start(bf16[96,1536]{1,0:T(8,128)(2,1)S(1)} %shard_map.100), channel_id=1, source_target_pairs={{0,24},{1,29},{2,26},{3,31},{4,28},{5,25},{6,30},{7,27},{8,16},{9,... | collective-permute-start | bytes 884744 | tf_op jit(solution)/shard_map/ppermute | solution.py:17
  90.3 2.2 %shard_map.102 = (bf16[192,512]{1,0:T(8,128)(2,1)S(1)}, bf16[192,512]{1,0:T(8,128)(2,1)S(1)}, bf16[96,1536]{1,0:T(8,128)(2,1)S(1)}, bf16[96,1536]{1,0:T(8,128)(2,1)S(1)}) custom-call(bf16[96,1536]{1,0:T(8,128)(2,1)S(1)} %collective-permute-done.15.mine.refs_5_, bf16[96,1536]{1,0:T(8,128)(2,1)S(1)} %collective-permute-done.23.far.refs_6_, ...), custom_call_target="tpu_custom_call" | custom-call | flops 1 | bytes 1 | tf_op jit(solution)/shard_map/pallas_call | solution.py:205
  92.5 2.3 %collective-permute-start.27 = (bf16[96,1536]{1,0:T(8,128)(2,1)S(1)}, bf16[96,1536]{1,0:T(8,128)(2,1)S(1)}, u32[]{:S(2)}, u32[]{:S(2)}) collective-permute-start(bf16[96,1536]{1,0:T(8,128)(2,1)S(1)} %get-tuple-element.199), channel_id=1, source_target_pairs={{0,2},{1,3},{2,0},{3,1},{4,6},{5,7},{6,4},{7,5},{8,10},{9,11},{10,... | collective-permute-start | bytes 884744 | tf_op jit(solution)/shard_map/ppermute | solution.py:17
  94.9 9.9 %collective-permute-start.29 = (bf16[96,1536]{1,0:T(8,128)(2,1)S(1)}, bf16[96,1536]{1,0:T(8,128)(2,1)S(1)}, u32[]{:S(2)}, u32[]{:S(2)}) collective-permute-start(bf16[96,1536]{1,0:T(8,128)(2,1)S(1)} %shard_map.103), channel_id=1, source_target_pairs={{0,24},{1,29},{2,26},{3,31},{4,28},{5,25},{6,30},{7,27},{8,16},{9,... | collective-permute-start | bytes 884744 | tf_op jit(solution)/shard_map/ppermute | solution.py:17
  104.9 7.6 %collective-permute-done.27.far = bf16[96,1536]{1,0:T(8,128)(2,1)S(1)} collective-permute-done((bf16[96,1536]{1,0:T(8,128)(2,1)S(1)}, bf16[96,1536]{1,0:T(8,128)(2,1)S(1)}, u32[]{:S(2)}, u32[]{:S(2)}) %collective-permute-start.27) | collective-permute-done | bytes 294944 | tf_op jit(solution)/shard_map/ppermute | solution.py:17
  112.6 2.8 %shard_map.105 = (bf16[384,512]{1,0:T(8,128)(2,1)S(1)}, bf16[384,512]{1,0:T(8,128)(2,1)S(1)}, bf16[192,1536]{1,0:T(8,128)(2,1)S(1)}, bf16[192,1536]{1,0:T(8,128)(2,1)S(1)}) custom-call(bf16[192,1536]{1,0:T(8,128)(2,1)S(1)} %constant_dynamic-update-slice_fusion.2.mine.refs_3_, bf16[192,1536]{1,0:T(8,128)(2,1)S(1)} %collective-permute-done.30.far.refs_4_, ...), custom_call_target="tpu_custom_call" | custom-call | flops 1 | bytes 1 | tf_op jit(solution)/shard_map/pallas_call | solution.py:205
  116.7 3.6 %collective-permute-start.28 = (bf16[96,1536]{1,0:T(8,128)(2,1)S(1)}, bf16[96,1536]{1,0:T(8,128)(2,1)S(1)}, u32[]{:S(2)}, u32[]{:S(2)}) collective-permute-start(bf16[96,1536]{1,0:T(8,128)(2,1)S(1)} %shard_map.104), channel_id=1, source_target_pairs={{0,16},{1,21},{2,18},{3,23},{4,20},{5,17},{6,22},{7,19},{8,24},{9,... | collective-permute-start | bytes 884744 | tf_op jit(solution)/shard_map/ppermute | solution.py:17
  128.4 2.7 %collective-permute-start.38 = (bf16[512,1536]{1,0:T(8,128)(2,1)S(1)}, bf16[512,1536]{1,0:T(8,128)(2,1)S(1)}, u32[]{:S(2)}, u32[]{:S(2)}) collective-permute-start(bf16[512,1536]{1,0:T(8,128)(2,1)S(1)} %shard_map.106), channel_id=1, source_target_pairs={{0,1},{1,0},{2,3},{3,2},{4,5},{5,4},{6,7},{7,6},{8,9},{9,8},{10,11... | collective-permute-start | bytes 4718600 | tf_op jit(solution)/shard_map/ppermute | solution.py:17
  131.1 3.2 %collective-permute-done.28.refs_2_ = bf16[96,1536]{1,0:T(8,128)(2,1)S(1)} collective-permute-done((bf16[96,1536]{1,0:T(8,128)(2,1)S(1)}, bf16[96,1536]{1,0:T(8,128)(2,1)S(1)}, u32[]{:S(2)}, u32[]{:S(2)}) %collective-permute-start.28) | collective-permute-done | bytes 294944 | tf_op jit(solution)/shard_map/ppermute | solution.py:17
  139.9 5.9 %collective-permute-done.35.refs_1_ = bf16[96,1536]{1,0:T(8,128)(2,1)S(1)} collective-permute-done((bf16[96,1536]{1,0:T(8,128)(2,1)S(1)}, bf16[96,1536]{1,0:T(8,128)(2,1)S(1)}, u32[]{:S(2)}, u32[]{:S(2)}) %collective-permute-start.35) | collective-permute-done | bytes 294944 | tf_op jit(solution)/shard_map/ppermute | solution.py:17
  145.8 3.0 %collective-permute-start.36 = (bf16[192,1536]{1,0:T(8,128)(2,1)S(1)}, bf16[192,1536]{1,0:T(8,128)(2,1)S(1)}, u32[]{:S(2)}, u32[]{:S(2)}) collective-permute-start(bf16[192,1536]{1,0:T(8,128)(2,1)S(1)} %pad_maximum_fusion), channel_id=1, source_target_pairs={{0,1},{1,0},{2,3},{3,2},{4,5},{5,4},{6,7},{7,6},{8,9},{9,8},{10,11... | collective-permute-start | bytes 1769480 | tf_op jit(solution)/shard_map/ppermute | solution.py:17
  148.9 1.9 %shard_map.112 = f32[512,1536]{1,0:T(8,128)} custom-call(f32[512,1536]{1,0:T(8,128)S(1)} %shard_map.108.own, bf16[512,1536]{1,0:T(8,128)(2,1)S(1)} %collective-permute-done.38.other), custom_call_target="tpu_custom_call" | custom-call | flops 1 | bytes 1 | tf_op jit(solution)/shard_map/pallas_call | solution.py:205
  150.8 1.9 %shard_map.113 = f32[1536,512]{1,0:T(8,128)} custom-call(f32[1536,512]{1,0:T(8,128)S(1)} %shard_map.109.own, bf16[1536,512]{1,0:T(8,128)(2,1)S(1)} %collective-permute-done.37.other), custom_call_target="tpu_custom_call" | custom-call | flops 1 | bytes 1 | tf_op jit(solution)/shard_map/pallas_call | solution.py:205
  (104 shorter events, 37.1 us)
Async XLA Ops:
  5.4 18.5 %collective-permute-start.6 = (bf16[1536,512]{1,0:T(8,128)(2,1)}, bf16[1536,512]{1,0:T(8,128)(2,1)S(1)}, u32[]{:S(2)}, u32[]{:S(2)}) collective-permute-start(bf16[1536,512]{1,0:T(8,128)(2,1)} %bitcast.7), channel_id=1, source_target_pairs={{0,1},{1,0},{2,3},{3,2},{4,5},{5,4},{6,7},{7,6},{8,9},{9,8},{10,11... | collective-permute-start | bytes 4718600 | tf_op jit(solution)/shard_map/ppermute | solution.py:17
  5.9 18.0 %collective-permute-start.7 = (bf16[512,1536]{1,0:T(8,128)(2,1)}, bf16[512,1536]{1,0:T(8,128)(2,1)S(1)}, u32[]{:S(2)}, u32[]{:S(2)}) collective-permute-start(bf16[512,1536]{1,0:T(8,128)(2,1)} %bitcast.15), channel_id=1, source_target_pairs={{0,1},{1,0},{2,3},{3,2},{4,5},{5,4},{6,7},{7,6},{8,9},{9,8},{10,11... | collective-permute-start | bytes 4718600 | tf_op jit(solution)/shard_map/ppermute | solution.py:17
  6.7 14.4 %collective-permute-start.3 = (bf16[96,1536]{1,0:T(8,128)(2,1)S(1)}, bf16[96,1536]{1,0:T(8,128)(2,1)S(1)}, u32[]{:S(2)}, u32[]{:S(2)}) collective-permute-start(bf16[96,1536]{1,0:T(8,128)(2,1)S(1)} %get-tuple-element.131), channel_id=1, source_target_pairs={{0,8},{1,13},{2,10},{3,15},{4,12},{5,9},{6,14},{7,11},{8,0},{9,5},... | collective-permute-start | bytes 884744 | tf_op jit(solution)/shard_map/ppermute | solution.py:17
  9.7 14.2 %collective-permute-start.5 = (bf16[96,1536]{1,0:T(8,128)(2,1)S(1)}, bf16[96,1536]{1,0:T(8,128)(2,1)S(1)}, u32[]{:S(2)}, u32[]{:S(2)}) collective-permute-start(bf16[96,1536]{1,0:T(8,128)(2,1)S(1)} %get-tuple-element.136), channel_id=1, source_target_pairs={{0,16},{1,21},{2,18},{3,23},{4,20},{5,17},{6,22},{7,19},{8,24},{9,... | collective-permute-start | bytes 884744 | tf_op jit(solution)/shard_map/ppermute | solution.py:17
  21.2 15.0 %collective-permute-start.4 = (bf16[192,1536]{1,0:T(8,128)(2,1)S(1)}, bf16[192,1536]{1,0:T(8,128)(2,1)S(1)}, u32[]{:S(2)}, u32[]{:S(2)}) collective-permute-start(bf16[192,1536]{1,0:T(8,128)(2,1)S(1)} %constant_dynamic-update-slice_fusion.mine.refs_0_), channel_id=1, source_target_pairs={{0,2},{1,3},{2,0},{3,1},{4,6},{5,7},{6,4},{7,5},{8,10},{9,11},{10,... | collective-permute-start | bytes 1769480 | tf_op jit(solution)/shard_map/ppermute | solution.py:17
  23.9 7.8 %collective-permute-start.8 = (bf16[32,6144]{1,0:T(8,128)(2,1)S(1)}, bf16[32,6144]{1,0:T(8,128)(2,1)S(1)}, u32[]{:S(2)}, u32[]{:S(2)}) collective-permute-start(bf16[32,6144]{1,0:T(8,128)(2,1)S(1)} %copy-done.5), channel_id=1, source_target_pairs={{0,1},{1,0},{2,3},{3,2},{4,5},{5,4},{6,7},{7,6},{8,9},{9,8},{10,11... | collective-permute-start | bytes 1179656 | tf_op jit(solution)/shard_map/ppermute | solution.py:17
  27.8 13.6 %collective-permute-start.11 = (bf16[96,1536]{1,0:T(8,128)(2,1)S(1)}, bf16[96,1536]{1,0:T(8,128)(2,1)S(1)}, u32[]{:S(2)}, u32[]{:S(2)}) collective-permute-start(bf16[96,1536]{1,0:T(8,128)(2,1)S(1)} %get-tuple-element.152), channel_id=1, source_target_pairs={{0,24},{1,29},{2,26},{3,31},{4,28},{5,25},{6,30},{7,27},{8,16},{9,... | collective-permute-start | bytes 884744 | tf_op jit(solution)/shard_map/ppermute | solution.py:17
  30.3 12.2 %collective-permute-start.13 = (bf16[96,1536]{1,0:T(8,128)(2,1)S(1)}, bf16[96,1536]{1,0:T(8,128)(2,1)S(1)}, u32[]{:S(2)}, u32[]{:S(2)}) collective-permute-start(bf16[96,1536]{1,0:T(8,128)(2,1)S(1)} %collective-permute-done.5.mine.refs_2_), channel_id=1, source_target_pairs={{0,2},{1,3},{2,0},{3,1},{4,6},{5,7},{6,4},{7,5},{8,10},{9,11},{10,... | collective-permute-start | bytes 884744 | tf_op jit(solution)/shard_map/ppermute | solution.py:17
  38.8 26.7 %collective-permute-start.10 = (bf16[192,1536]{1,0:T(8,128)(2,1)S(1)}, bf16[192,1536]{1,0:T(8,128)(2,1)S(1)}, u32[]{:S(2)}, u32[]{:S(2)}) collective-permute-start(bf16[192,1536]{1,0:T(8,128)(2,1)S(1)} %get-tuple-element.150), channel_id=1, source_target_pairs={{0,2},{1,3},{2,0},{3,1},{4,6},{5,7},{6,4},{7,5},{8,10},{9,11},{10,... | collective-permute-start | bytes 1769480 | tf_op jit(solution)/shard_map/ppermute | solution.py:17
  41.3 20.6 %collective-permute-start.12 = (bf16[96,1536]{1,0:T(8,128)(2,1)S(1)}, bf16[96,1536]{1,0:T(8,128)(2,1)S(1)}, u32[]{:S(2)}, u32[]{:S(2)}) collective-permute-start(bf16[96,1536]{1,0:T(8,128)(2,1)S(1)} %collective-permute-done.11.mine.refs_4_), channel_id=1, source_target_pairs={{0,2},{1,3},{2,0},{3,1},{4,6},{5,7},{6,4},{7,5},{8,10},{9,11},{10,... | collective-permute-start | bytes 884744 | tf_op jit(solution)/shard_map/ppermute | solution.py:17
  42.4 23.2 %collective-permute-start.17 = (bf16[96,1536]{1,0:T(8,128)(2,1)S(1)}, bf16[96,1536]{1,0:T(8,128)(2,1)S(1)}, u32[]{:S(2)}, u32[]{:S(2)}) collective-permute-start(bf16[96,1536]{1,0:T(8,128)(2,1)S(1)} %get-tuple-element.168), channel_id=1, source_target_pairs={{0,24},{1,29},{2,26},{3,31},{4,28},{5,25},{6,30},{7,27},{8,16},{9,... | collective-permute-start | bytes 884744 | tf_op jit(solution)/shard_map/ppermute | solution.py:17
  47.7 20.6 %collective-permute-start.16 = (bf16[96,1536]{1,0:T(8,128)(2,1)S(1)}, bf16[96,1536]{1,0:T(8,128)(2,1)S(1)}, u32[]{:S(2)}, u32[]{:S(2)}) collective-permute-start(bf16[96,1536]{1,0:T(8,128)(2,1)S(1)} %get-tuple-element.166), channel_id=1, source_target_pairs={{0,2},{1,3},{2,0},{3,1},{4,6},{5,7},{6,4},{7,5},{8,10},{9,11},{10,... | collective-permute-start | bytes 884744 | tf_op jit(solution)/shard_map/ppermute | solution.py:17
  49.2 23.9 %collective-permute-start.15 = (bf16[96,1536]{1,0:T(8,128)(2,1)S(1)}, bf16[96,1536]{1,0:T(8,128)(2,1)S(1)}, u32[]{:S(2)}, u32[]{:S(2)}) collective-permute-start(bf16[96,1536]{1,0:T(8,128)(2,1)S(1)} %get-tuple-element.165), channel_id=1, source_target_pairs={{0,16},{1,21},{2,18},{3,23},{4,20},{5,17},{6,22},{7,19},{8,24},{9,... | collective-permute-start | bytes 884744 | tf_op jit(solution)/shard_map/ppermute | solution.py:17
  63.4 11.1 %collective-permute-start.14 = (bf16[96,1536]{1,0:T(8,128)(2,1)S(1)}, bf16[96,1536]{1,0:T(8,128)(2,1)S(1)}, u32[]{:S(2)}, u32[]{:S(2)}) collective-permute-start(bf16[96,1536]{1,0:T(8,128)(2,1)S(1)} %get-tuple-element.163), channel_id=1, source_target_pairs={{0,2},{1,3},{2,0},{3,1},{4,6},{5,7},{6,4},{7,5},{8,10},{9,11},{10,... | collective-permute-start | bytes 884744 | tf_op jit(solution)/shard_map/ppermute | solution.py:17
  68.3 8.4 %collective-permute-start.20 = (bf16[96,1536]{1,0:T(8,128)(2,1)S(1)}, bf16[96,1536]{1,0:T(8,128)(2,1)S(1)}, u32[]{:S(2)}, u32[]{:S(2)}) collective-permute-start(bf16[96,1536]{1,0:T(8,128)(2,1)S(1)} %get-tuple-element.176), channel_id=1, source_target_pairs={{0,0},{1,5},{2,2},{3,7},{4,4},{5,1},{6,6},{7,3},{8,8},{9,13},{10,1... | collective-permute-start | bytes 884744 | tf_op jit(solution)/shard_map/ppermute | solution.py:17
  69.2 7.5 %collective-permute-start.21 = (bf16[96,1536]{1,0:T(8,128)(2,1)S(1)}, bf16[96,1536]{1,0:T(8,128)(2,1)S(1)}, u32[]{:S(2)}, u32[]{:S(2)}) collective-permute-start(bf16[96,1536]{1,0:T(8,128)(2,1)S(1)} %get-tuple-element.178), channel_id=1, source_target_pairs={{0,8},{1,13},{2,10},{3,15},{4,12},{5,9},{6,14},{7,11},{8,0},{9,5},... | collective-permute-start | bytes 884744 | tf_op jit(solution)/shard_map/ppermute | solution.py:17
  69.2 11.6 %collective-permute-start.19 = (bf16[96,1536]{1,0:T(8,128)(2,1)S(1)}, bf16[96,1536]{1,0:T(8,128)(2,1)S(1)}, u32[]{:S(2)}, u32[]{:S(2)}) collective-permute-start(bf16[96,1536]{1,0:T(8,128)(2,1)S(1)} %collective-permute-done.17.mine.refs_7_), channel_id=1, source_target_pairs={{0,2},{1,3},{2,0},{3,1},{4,6},{5,7},{6,4},{7,5},{8,10},{9,11},{10,... | collective-permute-start | bytes 884744 | tf_op jit(solution)/shard_map/ppermute | solution.py:17
  73.1 17.2 %collective-permute-start.23 = (bf16[96,1536]{1,0:T(8,128)(2,1)S(1)}, bf16[96,1536]{1,0:T(8,128)(2,1)S(1)}, u32[]{:S(2)}, u32[]{:S(2)}) collective-permute-start(bf16[96,1536]{1,0:T(8,128)(2,1)S(1)} %collective-permute-done.15.mine.refs_5_), channel_id=1, source_target_pairs={{0,2},{1,3},{2,0},{3,1},{4,6},{5,7},{6,4},{7,5},{8,10},{9,11},{10,... | collective-permute-start | bytes 884744 | tf_op jit(solution)/shard_map/ppermute | solution.py:17
  74.5 15.7 %collective-permute-start.24 = (bf16[96,1536]{1,0:T(8,128)(2,1)S(1)}, bf16[96,1536]{1,0:T(8,128)(2,1)S(1)}, u32[]{:S(2)}, u32[]{:S(2)}) collective-permute-start(bf16[96,1536]{1,0:T(8,128)(2,1)S(1)} %shard_map.99), channel_id=1, source_target_pairs={{0,16},{1,21},{2,18},{3,23},{4,20},{5,17},{6,22},{7,19},{8,24},{9,... | collective-permute-start | bytes 884744 | tf_op jit(solution)/shard_map/ppermute | solution.py:17
  83.1 11.7 %collective-permute-start.22 = (bf16[96,1536]{1,0:T(8,128)(2,1)S(1)}, bf16[96,1536]{1,0:T(8,128)(2,1)S(1)}, u32[]{:S(2)}, u32[]{:S(2)}) collective-permute-start(bf16[96,1536]{1,0:T(8,128)(2,1)S(1)} %get-tuple-element.184), channel_id=1, source_target_pairs={{0,2},{1,3},{2,0},{3,1},{4,6},{5,7},{6,4},{7,5},{8,10},{9,11},{10,... | collective-permute-start | bytes 884744 | tf_op jit(solution)/shard_map/ppermute | solution.py:17
  85.2 27.4 %collective-permute-start.30 = (bf16[192,1536]{1,0:T(8,128)(2,1)S(1)}, bf16[192,1536]{1,0:T(8,128)(2,1)S(1)}, u32[]{:S(2)}, u32[]{:S(2)}) collective-permute-start(bf16[192,1536]{1,0:T(8,128)(2,1)S(1)} %constant_dynamic-update-slice_fusion.2.mine.refs_3_), channel_id=1, source_target_pairs={{0,2},{1,3},{2,0},{3,1},{4,6},{5,7},{6,4},{7,5},{8,10},{9,11},{10,... | collective-permute-start | bytes 1769480 | tf_op jit(solution)/shard_map/ppermute | solution.py:17
  85.3 19.6 %collective-permute-start.18 = (bf16[96,1536]{1,0:T(8,128)(2,1)S(1)}, bf16[96,1536]{1,0:T(8,128)(2,1)S(1)}, u32[]{:S(2)}, u32[]{:S(2)}) collective-permute-start(bf16[96,1536]{1,0:T(8,128)(2,1)S(1)} %shard_map.100), channel_id=1, source_target_pairs={{0,24},{1,29},{2,26},{3,31},{4,28},{5,25},{6,30},{7,27},{8,16},{9,... | collective-permute-start | bytes 884744 | tf_op jit(solution)/shard_map/ppermute | solution.py:17
  92.5 19.9 %collective-permute-start.27 = (bf16[96,1536]{1,0:T(8,128)(2,1)S(1)}, bf16[96,1536]{1,0:T(8,128)(2,1)S(1)}, u32[]{:S(2)}, u32[]{:S(2)}) collective-permute-start(bf16[96,1536]{1,0:T(8,128)(2,1)S(1)} %get-tuple-element.199), channel_id=1, source_target_pairs={{0,2},{1,3},{2,0},{3,1},{4,6},{5,7},{6,4},{7,5},{8,10},{9,11},{10,... | collective-permute-start | bytes 884744 | tf_op jit(solution)/shard_map/ppermute | solution.py:17
  94.9 20.5 %collective-permute-start.29 = (bf16[96,1536]{1,0:T(8,128)(2,1)S(1)}, bf16[96,1536]{1,0:T(8,128)(2,1)S(1)}, u32[]{:S(2)}, u32[]{:S(2)}) collective-permute-start(bf16[96,1536]{1,0:T(8,128)(2,1)S(1)} %shard_map.103), channel_id=1, source_target_pairs={{0,24},{1,29},{2,26},{3,31},{4,28},{5,25},{6,30},{7,27},{8,16},{9,... | collective-permute-start | bytes 884744 | tf_op jit(solution)/shard_map/ppermute | solution.py:17
  115.4 7.3 %collective-permute-start.31 = (bf16[96,1536]{1,0:T(8,128)(2,1)S(1)}, bf16[96,1536]{1,0:T(8,128)(2,1)S(1)}, u32[]{:S(2)}, u32[]{:S(2)}) collective-permute-start(bf16[96,1536]{1,0:T(8,128)(2,1)S(1)} %pad_maximum_fusion.1), channel_id=1, source_target_pairs={{0,1},{1,0},{2,3},{3,2},{4,5},{5,4},{6,7},{7,6},{8,9},{9,8},{10,11... | collective-permute-start | bytes 884744 | tf_op jit(solution)/shard_map/ppermute | solution.py:17
  116.7 17.6 %collective-permute-start.28 = (bf16[96,1536]{1,0:T(8,128)(2,1)S(1)}, bf16[96,1536]{1,0:T(8,128)(2,1)S(1)}, u32[]{:S(2)}, u32[]{:S(2)}) collective-permute-start(bf16[96,1536]{1,0:T(8,128)(2,1)S(1)} %shard_map.104), channel_id=1, source_target_pairs={{0,16},{1,21},{2,18},{3,23},{4,20},{5,17},{6,22},{7,19},{8,24},{9,... | collective-permute-start | bytes 884744 | tf_op jit(solution)/shard_map/ppermute | solution.py:17
  120.3 16.4 %collective-permute-start.33 = (bf16[192,1536]{1,0:T(8,128)(2,1)S(1)}, bf16[192,1536]{1,0:T(8,128)(2,1)S(1)}, u32[]{:S(2)}, u32[]{:S(2)}) collective-permute-start(bf16[192,1536]{1,0:T(8,128)(2,1)S(1)} %get-tuple-element.232), channel_id=1, source_target_pairs={{0,2},{1,3},{2,0},{3,1},{4,6},{5,7},{6,4},{7,5},{8,10},{9,11},{10,... | collective-permute-start | bytes 1769480 | tf_op jit(solution)/shard_map/ppermute | solution.py:17
  121.8 12.5 %collective-permute-start.25 = (bf16[96,1536]{1,0:T(8,128)(2,1)S(1)}, bf16[96,1536]{1,0:T(8,128)(2,1)S(1)}, u32[]{:S(2)}, u32[]{:S(2)}) collective-permute-start(bf16[96,1536]{1,0:T(8,128)(2,1)S(1)} %get-tuple-element.195), channel_id=1, source_target_pairs={{0,0},{1,5},{2,2},{3,7},{4,4},{5,1},{6,6},{7,3},{8,8},{9,13},{10,1... | collective-permute-start | bytes 884744 | tf_op jit(solution)/shard_map/ppermute | solution.py:17
  122.5 13.2 %collective-permute-start.26 = (bf16[96,1536]{1,0:T(8,128)(2,1)S(1)}, bf16[96,1536]{1,0:T(8,128)(2,1)S(1)}, u32[]{:S(2)}, u32[]{:S(2)}) collective-permute-start(bf16[96,1536]{1,0:T(8,128)(2,1)S(1)} %get-tuple-element.197), channel_id=1, source_target_pairs={{0,8},{1,13},{2,10},{3,15},{4,12},{5,9},{6,14},{7,11},{8,0},{9,5},... | collective-permute-start | bytes 884744 | tf_op jit(solution)/shard_map/ppermute | solution.py:17
  128.4 20.5 %collective-permute-start.38 = (bf16[512,1536]{1,0:T(8,128)(2,1)S(1)}, bf16[512,1536]{1,0:T(8,128)(2,1)S(1)}, u32[]{:S(2)}, u32[]{:S(2)}) collective-permute-start(bf16[512,1536]{1,0:T(8,128)(2,1)S(1)} %shard_map.106), channel_id=1, source_target_pairs={{0,1},{1,0},{2,3},{3,2},{4,5},{5,4},{6,7},{7,6},{8,9},{9,8},{10,11... | collective-permute-start | bytes 4718600 | tf_op jit(solution)/shard_map/ppermute | solution.py:17
  134.3 16.5 %collective-permute-start.37 = (bf16[1536,512]{1,0:T(8,128)(2,1)S(1)}, bf16[1536,512]{1,0:T(8,128)(2,1)S(1)}, u32[]{:S(2)}, u32[]{:S(2)}) collective-permute-start(bf16[1536,512]{1,0:T(8,128)(2,1)S(1)} %shard_map.107), channel_id=1, source_target_pairs={{0,1},{1,0},{2,3},{3,2},{4,5},{5,4},{6,7},{7,6},{8,9},{9,8},{10,11... | collective-permute-start | bytes 4718600 | tf_op jit(solution)/shard_map/ppermute | solution.py:17
  137.6 8.2 %collective-permute-start.35 = (bf16[96,1536]{1,0:T(8,128)(2,1)S(1)}, bf16[96,1536]{1,0:T(8,128)(2,1)S(1)}, u32[]{:S(2)}, u32[]{:S(2)}) collective-permute-start(bf16[96,1536]{1,0:T(8,128)(2,1)S(1)} %get-tuple-element.239), channel_id=1, source_target_pairs={{0,8},{1,13},{2,10},{3,15},{4,12},{5,9},{6,14},{7,11},{8,0},{9,5},... | collective-permute-start | bytes 884744 | tf_op jit(solution)/shard_map/ppermute | solution.py:17
  (18 other events, 152.1 us)

commit v6 on v5

--- a/solution.py
+++ b/solution.py
@@ -8,7 +8,7 @@
 
 HEADS = 4
 SPLIT = 4
-VMEM = 20 * 1024 * 1024
+VMEM = 30 * 1024 * 1024
 FREE = pl.CostEstimate(flops=1, bytes_accessed=1, transcendentals=0)
 
 
@@ -299,12 +299,16 @@
     return call(kernel, [(shape, dtype)] * cuts, *left, *right)
 
 
-def joined_kernel(own, other, out):
-    out[...] = own[...] + other[...].astype(jnp.float32)
-
-
-def joined_weights(own, other):
-    return call(joined_kernel, [(own.shape, jnp.float32)], own, other)[0]
+def joined_kernel(own, *refs):
+    out = refs[-1]
+    rows = refs[0].shape[0]
+    for i, ref in enumerate(refs[:-1]):
+        part = slice(i * rows, (i + 1) * rows)
+        out[part] = own[part] + ref[...].astype(jnp.float32)
+
+
+def joined_weights(own, pieces):
+    return call(joined_kernel, [(own.shape, jnp.float32)], own, *pieces)[0]
 
 
 def hop(value, line):
@@ -427,15 +431,15 @@
     g_all = (g0, g0_far, g1, g1_far, g2, g2_far)
     hid_own, hid_other = zip(hid0, hid1, hid2)
     dpre_own, dpre_other = zip(dpre0, dpre1, dpre2)
-    (down_part,) = weight_grad(jnp.bfloat16, 1, (order.now(hid0[1]), *hid_other[1:]), g_all)
-    (up_part,) = weight_grad(jnp.bfloat16, 1, x_all, (order.now(dpre0[1]), *dpre_other[1:]))
-    order.done(down_part)
-    order.done(up_part)
+    down_part = weight_grad(jnp.bfloat16, 2, (order.now(hid0[1]), *hid_other[1:]), g_all)
+    up_part = weight_grad(jnp.bfloat16, 2, x_all, (order.now(dpre0[1]), *dpre_other[1:]))
+    order.done(down_part[0])
+    order.done(up_part[0])
     (down_own_part,) = weight_grad(jnp.float32, 1, (order.now(hid0[0]), *hid_own[1:]), g_all)
     order.done(down_own_part)
     (up_own_part,) = weight_grad(jnp.float32, 1, x_all, (order.now(dpre0[0]), *dpre_own[1:]))
     order.done(up_own_part)
-    down_sent, up_sent = core(down_part), core(up_part)
+    down_sent, up_sent = [core(part) for part in down_part], [core(part) for part in up_part]
     b_home |= come(b_mid)
     m_near = come(m_near)
     m_near_other = core(halves(m_near))
@@ -451,11 +455,11 @@
         *sizes,
     )
     order.done(mixed)
+    grad_down = joined_weights(down_own_part, order.wait(*down_sent))
+    order.done(grad_down)
     b_home |= come(b_near)
     b_other = core(halves(b_home))
-    grad_down = joined_weights(down_own_part, order.wait(down_sent))
-    order.done(grad_down)
-    grad_up = joined_weights(up_own_part, order.wait(up_sent))
+    grad_up = joined_weights(up_own_part, order.wait(*up_sent))
     order.done(grad_up)
     b_other = order.wait(b_other)
     token_grad = collect(index, routes, (), ordered(b_home), [b_other], *sizes)

time: 155 us -> 153 us (0.987)
  waiting for transfers between devices: 56 us -> 51.2 us
  starting transfers between devices: 65.6 us -> 68.4 us
    ppermute x39 -> x41, waiting for transfers between devices: 56 us -> 51.2 us  [swap(): lax.ppermute(value, 'expert', [(i, i ^ bits ^ (odd_bits if i % 2 else 0))...]
    ppermute x39 -> x41, starting transfers between devices: 65.6 us -> 68.4 us  [swap(): lax.ppermute(value, 'expert', [(i, i ^ bits ^ (odd_bits if i % 2 else 0))...]
    unnamed x22 -> x26, local copies, waits for them, and re-layouts: 3.15 us -> 3.16 us
  transfers between devices with their start and end apart: 39 -> 41, of which waited for: 15 -> 14; matrix products, arithmetic and copies ran while one was open for 0% -> 0% of each run, Pallas kernels for 17% -> 17%
where the time goes in v6:
time: 153 us; the launch traced here: 152 us
  starting transfers between devices  68.4 us (45%)
  waiting for transfers between devices  51.2 us (33%)
  Pallas kernels  28.4 us (19%)
  local copies, waits for them, and re-layouts  3.28 us (2%)
    ppermute x41, starting transfers between devices, swap(): lax.ppermute(value, 'expert', [(i, i ^ bits ^ (odd_bits if i % 2 else 0))...  68.4 us
    ppermute x41, waiting for transfers between devices, swap(): lax.ppermute(value, 'expert', [(i, i ^ bits ^ (odd_bits if i % 2 else 0))...  51.2 us
    pallas_call x18, Pallas kernels, call(): pl.pallas_call(kernel, out_shape=[jax.ShapeDtypeStruct(shape, dtype) for...  23.1 us
    pallas_call x2, Pallas kernels, collect(): pl.pallas_call(functools.partial(collect_kernel, experts_all, capacity, b...  3.34 us
    unnamed x26, local copies, waits for them, and re-layouts  3.16 us
  transfers between devices with their start and end apart: 41, of which 14 were waited for; matrix products, arithmetic and copies ran while one was open for 0% of the time, Pallas kernels for 17%

profile of v6, /device:TPU:0, one launch (start us, length us, event | category | flops | bytes accessed | tf_op | source)
XLA Modules:
  0.0 152.4 jit_solution(16087915365053064162)
XLA Ops:
  6.7 3.0 %collective-permute-start.3 = (bf16[96,1536]{1,0:T(8,128)(2,1)S(1)}, bf16[96,1536]{1,0:T(8,128)(2,1)S(1)}, u32[]{:S(2)}, u32[]{:S(2)}) collective-permute-start(bf16[96,1536]{1,0:T(8,128)(2,1)S(1)} %get-tuple-element.139), channel_id=1, source_target_pairs={{0,8},{1,13},{2,10},{3,15},{4,12},{5,9},{6,14},{7,11},{8,0},{9,5},... | collective-permute-start | bytes 884744 | tf_op jit(solution)/shard_map/ppermute | solution.py:17
  9.7 2.6 %collective-permute-start.5 = (bf16[96,1536]{1,0:T(8,128)(2,1)S(1)}, bf16[96,1536]{1,0:T(8,128)(2,1)S(1)}, u32[]{:S(2)}, u32[]{:S(2)}) collective-permute-start(bf16[96,1536]{1,0:T(8,128)(2,1)S(1)} %get-tuple-element.144), channel_id=1, source_target_pairs={{0,16},{1,21},{2,18},{3,23},{4,20},{5,17},{6,22},{7,19},{8,24},{9,... | collective-permute-start | bytes 884744 | tf_op jit(solution)/shard_map/ppermute | solution.py:17
  12.3 8.8 %collective-permute-done.3 = bf16[96,1536]{1,0:T(8,128)(2,1)S(1)} collective-permute-done((bf16[96,1536]{1,0:T(8,128)(2,1)S(1)}, bf16[96,1536]{1,0:T(8,128)(2,1)S(1)}, u32[]{:S(2)}, u32[]{:S(2)}) %collective-permute-start.3) | collective-permute-done | bytes 294944 | tf_op jit(solution)/shard_map/ppermute | solution.py:17
  21.2 2.7 %collective-permute-start.4 = (bf16[192,1536]{1,0:T(8,128)(2,1)S(1)}, bf16[192,1536]{1,0:T(8,128)(2,1)S(1)}, u32[]{:S(2)}, u32[]{:S(2)}) collective-permute-start(bf16[192,1536]{1,0:T(8,128)(2,1)S(1)} %constant_dynamic-update-slice_fusion.mine.refs_0_), channel_id=1, source_target_pairs={{0,2},{1,3},{2,0},{3,1},{4,6},{5,7},{6,4},{7,5},{8,10},{9,11},{10,... | collective-permute-start | bytes 1769480 | tf_op jit(solution)/shard_map/ppermute | solution.py:17
  23.9 3.8 %collective-permute-start.8 = (bf16[32,6144]{1,0:T(8,128)(2,1)S(1)}, bf16[32,6144]{1,0:T(8,128)(2,1)S(1)}, u32[]{:S(2)}, u32[]{:S(2)}) collective-permute-start(bf16[32,6144]{1,0:T(8,128)(2,1)S(1)} %copy-done.7), channel_id=1, source_target_pairs={{0,1},{1,0},{2,3},{3,2},{4,5},{5,4},{6,7},{7,6},{8,9},{9,8},{10,11... | collective-permute-start | bytes 1179656 | tf_op jit(solution)/shard_map/ppermute | solution.py:17
  27.8 2.5 %collective-permute-start.11 = (bf16[96,1536]{1,0:T(8,128)(2,1)S(1)}, bf16[96,1536]{1,0:T(8,128)(2,1)S(1)}, u32[]{:S(2)}, u32[]{:S(2)}) collective-permute-start(bf16[96,1536]{1,0:T(8,128)(2,1)S(1)} %get-tuple-element.160), channel_id=1, source_target_pairs={{0,24},{1,29},{2,26},{3,31},{4,28},{5,25},{6,30},{7,27},{8,16},{9,... | collective-permute-start | bytes 884744 | tf_op jit(solution)/shard_map/ppermute | solution.py:17
  34.2 1.9 %collective-permute-done.4.far.refs_1_ = bf16[192,1536]{1,0:T(8,128)(2,1)S(1)} collective-permute-done((bf16[192,1536]{1,0:T(8,128)(2,1)S(1)}, bf16[192,1536]{1,0:T(8,128)(2,1)S(1)}, u32[]{:S(2)}, u32[]{:S(2)}) %collective-permute-start.4) | collective-permute-done | bytes 589856 | tf_op jit(solution)/shard_map/ppermute | solution.py:17
  36.1 2.7 %shard_map.95 = (f32[384,512]{1,0:T(8,128)S(1)}, f32[384,512]{1,0:T(8,128)S(1)}, bf16[384,512]{1,0:T(8,128)(2,1)S(1)}, bf16[384,512]{1,0:T(8,128)(2,1)S(1)}, bf1...) custom-call(bf16[192,1536]{1,0:T(8,128)(2,1)S(1)} %constant_dynamic-update-slice_fusion.mine.refs_0_, ...), custom_call_target="tpu_custom_call" | custom-call | flops 1 | bytes 1 | tf_op jit(solution)/shard_map/pallas_call | solution.py:205
  38.8 2.5 %collective-permute-start.10 = (bf16[192,1536]{1,0:T(8,128)(2,1)S(1)}, bf16[192,1536]{1,0:T(8,128)(2,1)S(1)}, u32[]{:S(2)}, u32[]{:S(2)}) collective-permute-start(bf16[192,1536]{1,0:T(8,128)(2,1)S(1)} %get-tuple-element.158), channel_id=1, source_target_pairs={{0,2},{1,3},{2,0},{3,1},{4,6},{5,7},{6,4},{7,5},{8,10},{9,11},{10,... | collective-permute-start | bytes 1769480 | tf_op jit(solution)/shard_map/ppermute | solution.py:17
  42.4 3.7 %collective-permute-start.17 = (bf16[96,1536]{1,0:T(8,128)(2,1)S(1)}, bf16[96,1536]{1,0:T(8,128)(2,1)S(1)}, u32[]{:S(2)}, u32[]{:S(2)}) collective-permute-start(bf16[96,1536]{1,0:T(8,128)(2,1)S(1)} %get-tuple-element.176), channel_id=1, source_target_pairs={{0,24},{1,29},{2,26},{3,31},{4,28},{5,25},{6,30},{7,27},{8,16},{9,... | collective-permute-start | bytes 884744 | tf_op jit(solution)/shard_map/ppermute | solution.py:17
  49.2 12.7 %collective-permute-done.12.far.refs_5_ = bf16[96,1536]{1,0:T(8,128)(2,1)S(1)} collective-permute-done((bf16[96,1536]{1,0:T(8,128)(2,1)S(1)}, bf16[96,1536]{1,0:T(8,128)(2,1)S(1)}, u32[]{:S(2)}, u32[]{:S(2)}) %collective-permute-start.12) | collective-permute-done | bytes 294944 | tf_op jit(solution)/shard_map/ppermute | solution.py:17
  63.4 2.0 %collective-permute-start.14 = (bf16[96,1536]{1,0:T(8,128)(2,1)S(1)}, bf16[96,1536]{1,0:T(8,128)(2,1)S(1)}, u32[]{:S(2)}, u32[]{:S(2)}) collective-permute-start(bf16[96,1536]{1,0:T(8,128)(2,1)S(1)} %get-tuple-element.171), channel_id=1, source_target_pairs={{0,2},{1,3},{2,0},{3,1},{4,6},{5,7},{6,4},{7,5},{8,10},{9,11},{10,... | collective-permute-start | bytes 884744 | tf_op jit(solution)/shard_map/ppermute | solution.py:17
  65.6 2.6 %collective-permute-done.16.far = bf16[96,1536]{1,0:T(8,128)(2,1)S(1)} collective-permute-done((bf16[96,1536]{1,0:T(8,128)(2,1)S(1)}, bf16[96,1536]{1,0:T(8,128)(2,1)S(1)}, u32[]{:S(2)}, u32[]{:S(2)}) %collective-permute-start.16) | collective-permute-done | bytes 294944 | tf_op jit(solution)/shard_map/ppermute | solution.py:17
  69.2 2.0 %collective-permute-start.19 = (bf16[96,1536]{1,0:T(8,128)(2,1)S(1)}, bf16[96,1536]{1,0:T(8,128)(2,1)S(1)}, u32[]{:S(2)}, u32[]{:S(2)}) collective-permute-start(bf16[96,1536]{1,0:T(8,128)(2,1)S(1)} %collective-permute-done.17.mine.refs_7_), channel_id=1, source_target_pairs={{0,2},{1,3},{2,0},{3,1},{4,6},{5,7},{6,4},{7,5},{8,10},{9,11},{10,... | collective-permute-start | bytes 884744 | tf_op jit(solution)/shard_map/ppermute | solution.py:17
  71.3 1.8 %collective-permute-done.15.mine.refs_5_ = bf16[96,1536]{1,0:T(8,128)(2,1)S(1)} collective-permute-done((bf16[96,1536]{1,0:T(8,128)(2,1)S(1)}, bf16[96,1536]{1,0:T(8,128)(2,1)S(1)}, u32[]{:S(2)}, u32[]{:S(2)}) %collective-permute-start.15) | collective-permute-done | bytes 294944 | tf_op jit(solution)/shard_map/ppermute | solution.py:17
  74.5 2.1 %collective-permute-start.24 = (bf16[96,1536]{1,0:T(8,128)(2,1)S(1)}, bf16[96,1536]{1,0:T(8,128)(2,1)S(1)}, u32[]{:S(2)}, u32[]{:S(2)}) collective-permute-start(bf16[96,1536]{1,0:T(8,128)(2,1)S(1)} %shard_map.99), channel_id=1, source_target_pairs={{0,16},{1,21},{2,18},{3,23},{4,20},{5,17},{6,22},{7,19},{8,24},{9,... | collective-permute-start | bytes 884744 | tf_op jit(solution)/shard_map/ppermute | solution.py:17
  76.7 4.1 %collective-permute-done.19.far.refs_8_ = bf16[96,1536]{1,0:T(8,128)(2,1)S(1)} collective-permute-done((bf16[96,1536]{1,0:T(8,128)(2,1)S(1)}, bf16[96,1536]{1,0:T(8,128)(2,1)S(1)}, u32[]{:S(2)}, u32[]{:S(2)}) %collective-permute-start.19) | collective-permute-done | bytes 294944 | tf_op jit(solution)/shard_map/ppermute | solution.py:17
  80.9 2.2 %shard_map.101 = (bf16[192,512]{1,0:T(8,128)(2,1)S(1)}, bf16[192,512]{1,0:T(8,128)(2,1)S(1)}, bf16[96,1536]{1,0:T(8,128)(2,1)S(1)}, bf16[96,1536]{1,0:T(8,128)(2,1)S(1)}) custom-call(bf16[96,1536]{1,0:T(8,128)(2,1)S(1)} %collective-permute-done.17.mine.refs_7_, bf16[96,1536]{1,0:T(8,128)(2,1)S(1)} %collective-permute-done.19.far.refs_8_, ...), custom_call_target="tpu_custom_call" | custom-call | flops 1 | bytes 1 | tf_op jit(solution)/shard_map/pallas_call | solution.py:205
  83.1 2.0 %collective-permute-start.22 = (bf16[96,1536]{1,0:T(8,128)(2,1)S(1)}, bf16[96,1536]{1,0:T(8,128)(2,1)S(1)}, u32[]{:S(2)}, u32[]{:S(2)}) collective-permute-start(bf16[96,1536]{1,0:T(8,128)(2,1)S(1)} %get-tuple-element.192), channel_id=1, source_target_pairs={{0,2},{1,3},{2,0},{3,1},{4,6},{5,7},{6,4},{7,5},{8,10},{9,11},{10,... | collective-permute-start | bytes 884744 | tf_op jit(solution)/shard_map/ppermute | solution.py:17
  85.3 3.2 %collective-permute-start.18 = (bf16[96,1536]{1,0:T(8,128)(2,1)S(1)}, bf16[96,1536]{1,0:T(8,128)(2,1)S(1)}, u32[]{:S(2)}, u32[]{:S(2)}) collective-permute-start(bf16[96,1536]{1,0:T(8,128)(2,1)S(1)} %shard_map.100), channel_id=1, source_target_pairs={{0,24},{1,29},{2,26},{3,31},{4,28},{5,25},{6,30},{7,27},{8,16},{9,... | collective-permute-start | bytes 884744 | tf_op jit(solution)/shard_map/ppermute | solution.py:17
  90.3 2.2 %shard_map.102 = (bf16[192,512]{1,0:T(8,128)(2,1)S(1)}, bf16[192,512]{1,0:T(8,128)(2,1)S(1)}, bf16[96,1536]{1,0:T(8,128)(2,1)S(1)}, bf16[96,1536]{1,0:T(8,128)(2,1)S(1)}) custom-call(bf16[96,1536]{1,0:T(8,128)(2,1)S(1)} %collective-permute-done.15.mine.refs_5_, bf16[96,1536]{1,0:T(8,128)(2,1)S(1)} %collective-permute-done.23.far.refs_6_, ...), custom_call_target="tpu_custom_call" | custom-call | flops 1 | bytes 1 | tf_op jit(solution)/shard_map/pallas_call | solution.py:205
  92.5 2.3 %collective-permute-start.27 = (bf16[96,1536]{1,0:T(8,128)(2,1)S(1)}, bf16[96,1536]{1,0:T(8,128)(2,1)S(1)}, u32[]{:S(2)}, u32[]{:S(2)}) collective-permute-start(bf16[96,1536]{1,0:T(8,128)(2,1)S(1)} %get-tuple-element.207), channel_id=1, source_target_pairs={{0,2},{1,3},{2,0},{3,1},{4,6},{5,7},{6,4},{7,5},{8,10},{9,11},{10,... | collective-permute-start | bytes 884744 | tf_op jit(solution)/shard_map/ppermute | solution.py:17
  94.9 9.9 %collective-permute-start.29 = (bf16[96,1536]{1,0:T(8,128)(2,1)S(1)}, bf16[96,1536]{1,0:T(8,128)(2,1)S(1)}, u32[]{:S(2)}, u32[]{:S(2)}) collective-permute-start(bf16[96,1536]{1,0:T(8,128)(2,1)S(1)} %shard_map.103), channel_id=1, source_target_pairs={{0,24},{1,29},{2,26},{3,31},{4,28},{5,25},{6,30},{7,27},{8,16},{9,... | collective-permute-start | bytes 884744 | tf_op jit(solution)/shard_map/ppermute | solution.py:17
  104.9 7.6 %collective-permute-done.27.far = bf16[96,1536]{1,0:T(8,128)(2,1)S(1)} collective-permute-done((bf16[96,1536]{1,0:T(8,128)(2,1)S(1)}, bf16[96,1536]{1,0:T(8,128)(2,1)S(1)}, u32[]{:S(2)}, u32[]{:S(2)}) %collective-permute-start.27) | collective-permute-done | bytes 294944 | tf_op jit(solution)/shard_map/ppermute | solution.py:17
  112.6 2.8 %shard_map.105 = (bf16[384,512]{1,0:T(8,128)(2,1)S(1)}, bf16[384,512]{1,0:T(8,128)(2,1)S(1)}, bf16[192,1536]{1,0:T(8,128)(2,1)S(1)}, bf16[192,1536]{1,0:T(8,128)(2,1)S(1)}) custom-call(bf16[192,1536]{1,0:T(8,128)(2,1)S(1)} %constant_dynamic-update-slice_fusion.2.mine.refs_3_, bf16[192,1536]{1,0:T(8,128)(2,1)S(1)} %collective-permute-done.30.far.refs_4_, ...), custom_call_target="tpu_custom_call" | custom-call | flops 1 | bytes 1 | tf_op jit(solution)/shard_map/pallas_call | solution.py:205
  116.7 3.6 %collective-permute-start.28 = (bf16[96,1536]{1,0:T(8,128)(2,1)S(1)}, bf16[96,1536]{1,0:T(8,128)(2,1)S(1)}, u32[]{:S(2)}, u32[]{:S(2)}) collective-permute-start(bf16[96,1536]{1,0:T(8,128)(2,1)S(1)} %shard_map.104), channel_id=1, source_target_pairs={{0,16},{1,21},{2,18},{3,23},{4,20},{5,17},{6,22},{7,19},{8,24},{9,... | collective-permute-start | bytes 884744 | tf_op jit(solution)/shard_map/ppermute | solution.py:17
  128.4 2.7 %collective-permute-start.36 = (bf16[256,1536]{1,0:T(8,128)(2,1)S(1)}, bf16[256,1536]{1,0:T(8,128)(2,1)S(1)}, u32[]{:S(2)}, u32[]{:S(2)}) collective-permute-start(bf16[256,1536]{1,0:T(8,128)(2,1)S(1)} %get-tuple-element.250), channel_id=1, source_target_pairs={{0,1},{1,0},{2,3},{3,2},{4,5},{5,4},{6,7},{7,6},{8,9},{9,8},{10,11... | collective-permute-start | bytes 2359304 | tf_op jit(solution)/shard_map/ppermute | solution.py:17
  131.1 3.2 %collective-permute-done.28.refs_2_ = bf16[96,1536]{1,0:T(8,128)(2,1)S(1)} collective-permute-done((bf16[96,1536]{1,0:T(8,128)(2,1)S(1)}, bf16[96,1536]{1,0:T(8,128)(2,1)S(1)}, u32[]{:S(2)}, u32[]{:S(2)}) %collective-permute-start.28) | collective-permute-done | bytes 294944 | tf_op jit(solution)/shard_map/ppermute | solution.py:17
  138.0 2.7 %collective-permute-start.39 = (bf16[768,512]{1,0:T(8,128)(2,1)S(1)}, bf16[768,512]{1,0:T(8,128)(2,1)S(1)}, u32[]{:S(2)}, u32[]{:S(2)}) collective-permute-start(bf16[768,512]{1,0:T(8,128)(2,1)S(1)} %get-tuple-element.258), channel_id=1, source_target_pairs={{0,1},{1,0},{2,3},{3,2},{4,5},{5,4},{6,7},{7,6},{8,9},{9,8},{10,11... | collective-permute-start | bytes 2359304 | tf_op jit(solution)/shard_map/ppermute | solution.py:17
  142.5 2.0 %shard_map.112 = f32[512,1536]{1,0:T(8,128)} custom-call(f32[512,1536]{1,0:T(8,128)S(1)} %shard_map.108.own, bf16[256,1536]{1,0:T(8,128)(2,1)S(1)} %collective-permute-done.36.refs_0_, bf16[256,1536]{1,0:T(8,128)(2,1)S(1)} %collective-permute-done.37.refs_1_), custom_call_target="tpu_custom_call" | custom-call | flops 1 | bytes 1 | tf_op jit(solution)/shard_map/pallas_call | solution.py:205
  145.9 3.0 %collective-permute-start.38 = (bf16[192,1536]{1,0:T(8,128)(2,1)S(1)}, bf16[192,1536]{1,0:T(8,128)(2,1)S(1)}, u32[]{:S(2)}, u32[]{:S(2)}) collective-permute-start(bf16[192,1536]{1,0:T(8,128)(2,1)S(1)} %pad_maximum_fusion), channel_id=1, source_target_pairs={{0,1},{1,0},{2,3},{3,2},{4,5},{5,4},{6,7},{7,6},{8,9},{9,8},{10,11... | collective-permute-start | bytes 1769480 | tf_op jit(solution)/shard_map/ppermute | solution.py:17
  148.9 1.9 %shard_map.113 = f32[1536,512]{1,0:T(8,128)} custom-call(f32[1536,512]{1,0:T(8,128)S(1)} %shard_map.109.own, bf16[768,512]{1,0:T(8,128)(2,1)S(1)} %collective-permute-done.39.refs_0_, bf16[768,512]{1,0:T(8,128)(2,1)S(1)} %collective-permute-done.40.refs_1_), custom_call_target="tpu_custom_call" | custom-call | flops 1 | bytes 1 | tf_op jit(solution)/shard_map/pallas_call | solution.py:205
  (113 shorter events, 38.2 us)
Async XLA Ops:
  5.4 18.5 %collective-permute-start.6 = (bf16[1536,512]{1,0:T(8,128)(2,1)}, bf16[1536,512]{1,0:T(8,128)(2,1)S(1)}, u32[]{:S(2)}, u32[]{:S(2)}) collective-permute-start(bf16[1536,512]{1,0:T(8,128)(2,1)} %bitcast.7), channel_id=1, source_target_pairs={{0,1},{1,0},{2,3},{3,2},{4,5},{5,4},{6,7},{7,6},{8,9},{9,8},{10,11... | collective-permute-start | bytes 4718600 | tf_op jit(solution)/shard_map/ppermute | solution.py:17
  5.9 18.0 %collective-permute-start.7 = (bf16[512,1536]{1,0:T(8,128)(2,1)}, bf16[512,1536]{1,0:T(8,128)(2,1)S(1)}, u32[]{:S(2)}, u32[]{:S(2)}) collective-permute-start(bf16[512,1536]{1,0:T(8,128)(2,1)} %bitcast.15), channel_id=1, source_target_pairs={{0,1},{1,0},{2,3},{3,2},{4,5},{5,4},{6,7},{7,6},{8,9},{9,8},{10,11... | collective-permute-start | bytes 4718600 | tf_op jit(solution)/shard_map/ppermute | solution.py:17
  6.7 14.4 %collective-permute-start.3 = (bf16[96,1536]{1,0:T(8,128)(2,1)S(1)}, bf16[96,1536]{1,0:T(8,128)(2,1)S(1)}, u32[]{:S(2)}, u32[]{:S(2)}) collective-permute-start(bf16[96,1536]{1,0:T(8,128)(2,1)S(1)} %get-tuple-element.139), channel_id=1, source_target_pairs={{0,8},{1,13},{2,10},{3,15},{4,12},{5,9},{6,14},{7,11},{8,0},{9,5},... | collective-permute-start | bytes 884744 | tf_op jit(solution)/shard_map/ppermute | solution.py:17
  9.7 14.2 %collective-permute-start.5 = (bf16[96,1536]{1,0:T(8,128)(2,1)S(1)}, bf16[96,1536]{1,0:T(8,128)(2,1)S(1)}, u32[]{:S(2)}, u32[]{:S(2)}) collective-permute-start(bf16[96,1536]{1,0:T(8,128)(2,1)S(1)} %get-tuple-element.144), channel_id=1, source_target_pairs={{0,16},{1,21},{2,18},{3,23},{4,20},{5,17},{6,22},{7,19},{8,24},{9,... | collective-permute-start | bytes 884744 | tf_op jit(solution)/shard_map/ppermute | solution.py:17
  21.2 15.0 %collective-permute-start.4 = (bf16[192,1536]{1,0:T(8,128)(2,1)S(1)}, bf16[192,1536]{1,0:T(8,128)(2,1)S(1)}, u32[]{:S(2)}, u32[]{:S(2)}) collective-permute-start(bf16[192,1536]{1,0:T(8,128)(2,1)S(1)} %constant_dynamic-update-slice_fusion.mine.refs_0_), channel_id=1, source_target_pairs={{0,2},{1,3},{2,0},{3,1},{4,6},{5,7},{6,4},{7,5},{8,10},{9,11},{10,... | collective-permute-start | bytes 1769480 | tf_op jit(solution)/shard_map/ppermute | solution.py:17
  23.9 7.8 %collective-permute-start.8 = (bf16[32,6144]{1,0:T(8,128)(2,1)S(1)}, bf16[32,6144]{1,0:T(8,128)(2,1)S(1)}, u32[]{:S(2)}, u32[]{:S(2)}) collective-permute-start(bf16[32,6144]{1,0:T(8,128)(2,1)S(1)} %copy-done.7), channel_id=1, source_target_pairs={{0,1},{1,0},{2,3},{3,2},{4,5},{5,4},{6,7},{7,6},{8,9},{9,8},{10,11... | collective-permute-start | bytes 1179656 | tf_op jit(solution)/shard_map/ppermute | solution.py:17
  27.8 13.6 %collective-permute-start.11 = (bf16[96,1536]{1,0:T(8,128)(2,1)S(1)}, bf16[96,1536]{1,0:T(8,128)(2,1)S(1)}, u32[]{:S(2)}, u32[]{:S(2)}) collective-permute-start(bf16[96,1536]{1,0:T(8,128)(2,1)S(1)} %get-tuple-element.160), channel_id=1, source_target_pairs={{0,24},{1,29},{2,26},{3,31},{4,28},{5,25},{6,30},{7,27},{8,16},{9,... | collective-permute-start | bytes 884744 | tf_op jit(solution)/shard_map/ppermute | solution.py:17
  30.3 12.2 %collective-permute-start.13 = (bf16[96,1536]{1,0:T(8,128)(2,1)S(1)}, bf16[96,1536]{1,0:T(8,128)(2,1)S(1)}, u32[]{:S(2)}, u32[]{:S(2)}) collective-permute-start(bf16[96,1536]{1,0:T(8,128)(2,1)S(1)} %collective-permute-done.5.mine.refs_2_), channel_id=1, source_target_pairs={{0,2},{1,3},{2,0},{3,1},{4,6},{5,7},{6,4},{7,5},{8,10},{9,11},{10,... | collective-permute-start | bytes 884744 | tf_op jit(solution)/shard_map/ppermute | solution.py:17
  38.8 26.7 %collective-permute-start.10 = (bf16[192,1536]{1,0:T(8,128)(2,1)S(1)}, bf16[192,1536]{1,0:T(8,128)(2,1)S(1)}, u32[]{:S(2)}, u32[]{:S(2)}) collective-permute-start(bf16[192,1536]{1,0:T(8,128)(2,1)S(1)} %get-tuple-element.158), channel_id=1, source_target_pairs={{0,2},{1,3},{2,0},{3,1},{4,6},{5,7},{6,4},{7,5},{8,10},{9,11},{10,... | collective-permute-start | bytes 1769480 | tf_op jit(solution)/shard_map/ppermute | solution.py:17
  41.3 20.6 %collective-permute-start.12 = (bf16[96,1536]{1,0:T(8,128)(2,1)S(1)}, bf16[96,1536]{1,0:T(8,128)(2,1)S(1)}, u32[]{:S(2)}, u32[]{:S(2)}) collective-permute-start(bf16[96,1536]{1,0:T(8,128)(2,1)S(1)} %collective-permute-done.11.mine.refs_4_), channel_id=1, source_target_pairs={{0,2},{1,3},{2,0},{3,1},{4,6},{5,7},{6,4},{7,5},{8,10},{9,11},{10,... | collective-permute-start | bytes 884744 | tf_op jit(solution)/shard_map/ppermute | solution.py:17
  42.4 23.2 %collective-permute-start.17 = (bf16[96,1536]{1,0:T(8,128)(2,1)S(1)}, bf16[96,1536]{1,0:T(8,128)(2,1)S(1)}, u32[]{:S(2)}, u32[]{:S(2)}) collective-permute-start(bf16[96,1536]{1,0:T(8,128)(2,1)S(1)} %get-tuple-element.176), channel_id=1, source_target_pairs={{0,24},{1,29},{2,26},{3,31},{4,28},{5,25},{6,30},{7,27},{8,16},{9,... | collective-permute-start | bytes 884744 | tf_op jit(solution)/shard_map/ppermute | solution.py:17
  47.7 20.6 %collective-permute-start.16 = (bf16[96,1536]{1,0:T(8,128)(2,1)S(1)}, bf16[96,1536]{1,0:T(8,128)(2,1)S(1)}, u32[]{:S(2)}, u32[]{:S(2)}) collective-permute-start(bf16[96,1536]{1,0:T(8,128)(2,1)S(1)} %get-tuple-element.174), channel_id=1, source_target_pairs={{0,2},{1,3},{2,0},{3,1},{4,6},{5,7},{6,4},{7,5},{8,10},{9,11},{10,... | collective-permute-start | bytes 884744 | tf_op jit(solution)/shard_map/ppermute | solution.py:17
  49.2 23.9 %collective-permute-start.15 = (bf16[96,1536]{1,0:T(8,128)(2,1)S(1)}, bf16[96,1536]{1,0:T(8,128)(2,1)S(1)}, u32[]{:S(2)}, u32[]{:S(2)}) collective-permute-start(bf16[96,1536]{1,0:T(8,128)(2,1)S(1)} %get-tuple-element.173), channel_id=1, source_target_pairs={{0,16},{1,21},{2,18},{3,23},{4,20},{5,17},{6,22},{7,19},{8,24},{9,... | collective-permute-start | bytes 884744 | tf_op jit(solution)/shard_map/ppermute | solution.py:17
  63.4 11.1 %collective-permute-start.14 = (bf16[96,1536]{1,0:T(8,128)(2,1)S(1)}, bf16[96,1536]{1,0:T(8,128)(2,1)S(1)}, u32[]{:S(2)}, u32[]{:S(2)}) collective-permute-start(bf16[96,1536]{1,0:T(8,128)(2,1)S(1)} %get-tuple-element.171), channel_id=1, source_target_pairs={{0,2},{1,3},{2,0},{3,1},{4,6},{5,7},{6,4},{7,5},{8,10},{9,11},{10,... | collective-permute-start | bytes 884744 | tf_op jit(solution)/shard_map/ppermute | solution.py:17
  68.3 8.4 %collective-permute-start.20 = (bf16[96,1536]{1,0:T(8,128)(2,1)S(1)}, bf16[96,1536]{1,0:T(8,128)(2,1)S(1)}, u32[]{:S(2)}, u32[]{:S(2)}) collective-permute-start(bf16[96,1536]{1,0:T(8,128)(2,1)S(1)} %get-tuple-element.184), channel_id=1, source_target_pairs={{0,0},{1,5},{2,2},{3,7},{4,4},{5,1},{6,6},{7,3},{8,8},{9,13},{10,1... | collective-permute-start | bytes 884744 | tf_op jit(solution)/shard_map/ppermute | solution.py:17
  69.2 11.6 %collective-permute-start.19 = (bf16[96,1536]{1,0:T(8,128)(2,1)S(1)}, bf16[96,1536]{1,0:T(8,128)(2,1)S(1)}, u32[]{:S(2)}, u32[]{:S(2)}) collective-permute-start(bf16[96,1536]{1,0:T(8,128)(2,1)S(1)} %collective-permute-done.17.mine.refs_7_), channel_id=1, source_target_pairs={{0,2},{1,3},{2,0},{3,1},{4,6},{5,7},{6,4},{7,5},{8,10},{9,11},{10,... | collective-permute-start | bytes 884744 | tf_op jit(solution)/shard_map/ppermute | solution.py:17
  73.1 17.2 %collective-permute-start.23 = (bf16[96,1536]{1,0:T(8,128)(2,1)S(1)}, bf16[96,1536]{1,0:T(8,128)(2,1)S(1)}, u32[]{:S(2)}, u32[]{:S(2)}) collective-permute-start(bf16[96,1536]{1,0:T(8,128)(2,1)S(1)} %collective-permute-done.15.mine.refs_5_), channel_id=1, source_target_pairs={{0,2},{1,3},{2,0},{3,1},{4,6},{5,7},{6,4},{7,5},{8,10},{9,11},{10,... | collective-permute-start | bytes 884744 | tf_op jit(solution)/shard_map/ppermute | solution.py:17
  74.5 15.7 %collective-permute-start.24 = (bf16[96,1536]{1,0:T(8,128)(2,1)S(1)}, bf16[96,1536]{1,0:T(8,128)(2,1)S(1)}, u32[]{:S(2)}, u32[]{:S(2)}) collective-permute-start(bf16[96,1536]{1,0:T(8,128)(2,1)S(1)} %shard_map.99), channel_id=1, source_target_pairs={{0,16},{1,21},{2,18},{3,23},{4,20},{5,17},{6,22},{7,19},{8,24},{9,... | collective-permute-start | bytes 884744 | tf_op jit(solution)/shard_map/ppermute | solution.py:17
  83.1 11.7 %collective-permute-start.22 = (bf16[96,1536]{1,0:T(8,128)(2,1)S(1)}, bf16[96,1536]{1,0:T(8,128)(2,1)S(1)}, u32[]{:S(2)}, u32[]{:S(2)}) collective-permute-start(bf16[96,1536]{1,0:T(8,128)(2,1)S(1)} %get-tuple-element.192), channel_id=1, source_target_pairs={{0,2},{1,3},{2,0},{3,1},{4,6},{5,7},{6,4},{7,5},{8,10},{9,11},{10,... | collective-permute-start | bytes 884744 | tf_op jit(solution)/shard_map/ppermute | solution.py:17
  85.2 27.4 %collective-permute-start.30 = (bf16[192,1536]{1,0:T(8,128)(2,1)S(1)}, bf16[192,1536]{1,0:T(8,128)(2,1)S(1)}, u32[]{:S(2)}, u32[]{:S(2)}) collective-permute-start(bf16[192,1536]{1,0:T(8,128)(2,1)S(1)} %constant_dynamic-update-slice_fusion.2.mine.refs_3_), channel_id=1, source_target_pairs={{0,2},{1,3},{2,0},{3,1},{4,6},{5,7},{6,4},{7,5},{8,10},{9,11},{10,... | collective-permute-start | bytes 1769480 | tf_op jit(solution)/shard_map/ppermute | solution.py:17
  85.3 19.6 %collective-permute-start.18 = (bf16[96,1536]{1,0:T(8,128)(2,1)S(1)}, bf16[96,1536]{1,0:T(8,128)(2,1)S(1)}, u32[]{:S(2)}, u32[]{:S(2)}) collective-permute-start(bf16[96,1536]{1,0:T(8,128)(2,1)S(1)} %shard_map.100), channel_id=1, source_target_pairs={{0,24},{1,29},{2,26},{3,31},{4,28},{5,25},{6,30},{7,27},{8,16},{9,... | collective-permute-start | bytes 884744 | tf_op jit(solution)/shard_map/ppermute | solution.py:17
  92.5 19.9 %collective-permute-start.27 = (bf16[96,1536]{1,0:T(8,128)(2,1)S(1)}, bf16[96,1536]{1,0:T(8,128)(2,1)S(1)}, u32[]{:S(2)}, u32[]{:S(2)}) collective-permute-start(bf16[96,1536]{1,0:T(8,128)(2,1)S(1)} %get-tuple-element.207), channel_id=1, source_target_pairs={{0,2},{1,3},{2,0},{3,1},{4,6},{5,7},{6,4},{7,5},{8,10},{9,11},{10,... | collective-permute-start | bytes 884744 | tf_op jit(solution)/shard_map/ppermute | solution.py:17
  94.9 20.5 %collective-permute-start.29 = (bf16[96,1536]{1,0:T(8,128)(2,1)S(1)}, bf16[96,1536]{1,0:T(8,128)(2,1)S(1)}, u32[]{:S(2)}, u32[]{:S(2)}) collective-permute-start(bf16[96,1536]{1,0:T(8,128)(2,1)S(1)} %shard_map.103), channel_id=1, source_target_pairs={{0,24},{1,29},{2,26},{3,31},{4,28},{5,25},{6,30},{7,27},{8,16},{9,... | collective-permute-start | bytes 884744 | tf_op jit(solution)/shard_map/ppermute | solution.py:17
  116.7 17.6 %collective-permute-start.28 = (bf16[96,1536]{1,0:T(8,128)(2,1)S(1)}, bf16[96,1536]{1,0:T(8,128)(2,1)S(1)}, u32[]{:S(2)}, u32[]{:S(2)}) collective-permute-start(bf16[96,1536]{1,0:T(8,128)(2,1)S(1)} %shard_map.104), channel_id=1, source_target_pairs={{0,16},{1,21},{2,18},{3,23},{4,20},{5,17},{6,22},{7,19},{8,24},{9,... | collective-permute-start | bytes 884744 | tf_op jit(solution)/shard_map/ppermute | solution.py:17
  120.3 16.4 %collective-permute-start.33 = (bf16[192,1536]{1,0:T(8,128)(2,1)S(1)}, bf16[192,1536]{1,0:T(8,128)(2,1)S(1)}, u32[]{:S(2)}, u32[]{:S(2)}) collective-permute-start(bf16[192,1536]{1,0:T(8,128)(2,1)S(1)} %get-tuple-element.242), channel_id=1, source_target_pairs={{0,2},{1,3},{2,0},{3,1},{4,6},{5,7},{6,4},{7,5},{8,10},{9,11},{10,... | collective-permute-start | bytes 1769480 | tf_op jit(solution)/shard_map/ppermute | solution.py:17
  121.8 12.5 %collective-permute-start.25 = (bf16[96,1536]{1,0:T(8,128)(2,1)S(1)}, bf16[96,1536]{1,0:T(8,128)(2,1)S(1)}, u32[]{:S(2)}, u32[]{:S(2)}) collective-permute-start(bf16[96,1536]{1,0:T(8,128)(2,1)S(1)} %get-tuple-element.203), channel_id=1, source_target_pairs={{0,0},{1,5},{2,2},{3,7},{4,4},{5,1},{6,6},{7,3},{8,8},{9,13},{10,1... | collective-permute-start | bytes 884744 | tf_op jit(solution)/shard_map/ppermute | solution.py:17
  122.5 13.2 %collective-permute-start.26 = (bf16[96,1536]{1,0:T(8,128)(2,1)S(1)}, bf16[96,1536]{1,0:T(8,128)(2,1)S(1)}, u32[]{:S(2)}, u32[]{:S(2)}) collective-permute-start(bf16[96,1536]{1,0:T(8,128)(2,1)S(1)} %get-tuple-element.205), channel_id=1, source_target_pairs={{0,8},{1,13},{2,10},{3,15},{4,12},{5,9},{6,14},{7,11},{8,0},{9,5},... | collective-permute-start | bytes 884744 | tf_op jit(solution)/shard_map/ppermute | solution.py:17
  128.4 14.1 %collective-permute-start.36 = (bf16[256,1536]{1,0:T(8,128)(2,1)S(1)}, bf16[256,1536]{1,0:T(8,128)(2,1)S(1)}, u32[]{:S(2)}, u32[]{:S(2)}) collective-permute-start(bf16[256,1536]{1,0:T(8,128)(2,1)S(1)} %get-tuple-element.250), channel_id=1, source_target_pairs={{0,1},{1,0},{2,3},{3,2},{4,5},{5,4},{6,7},{7,6},{8,9},{9,8},{10,11... | collective-permute-start | bytes 2359304 | tf_op jit(solution)/shard_map/ppermute | solution.py:17
  134.3 8.2 %collective-permute-start.37 = (bf16[256,1536]{1,0:T(8,128)(2,1)S(1)}, bf16[256,1536]{1,0:T(8,128)(2,1)S(1)}, u32[]{:S(2)}, u32[]{:S(2)}) collective-permute-start(bf16[256,1536]{1,0:T(8,128)(2,1)S(1)} %get-tuple-element.252), channel_id=1, source_target_pairs={{0,1},{1,0},{2,3},{3,2},{4,5},{5,4},{6,7},{7,6},{8,9},{9,8},{10,11... | collective-permute-start | bytes 2359304 | tf_op jit(solution)/shard_map/ppermute | solution.py:17
  136.9 7.7 %collective-permute-start.34 = (bf16[96,1536]{1,0:T(8,128)(2,1)S(1)}, bf16[96,1536]{1,0:T(8,128)(2,1)S(1)}, u32[]{:S(2)}, u32[]{:S(2)}) collective-permute-start(bf16[96,1536]{1,0:T(8,128)(2,1)S(1)} %get-tuple-element.247), channel_id=1, source_target_pairs={{0,0},{1,5},{2,2},{3,7},{4,4},{5,1},{6,6},{7,3},{8,8},{9,13},{10,1... | collective-permute-start | bytes 884744 | tf_op jit(solution)/shard_map/ppermute | solution.py:17
  137.6 8.2 %collective-permute-start.35 = (bf16[96,1536]{1,0:T(8,128)(2,1)S(1)}, bf16[96,1536]{1,0:T(8,128)(2,1)S(1)}, u32[]{:S(2)}, u32[]{:S(2)}) collective-permute-start(bf16[96,1536]{1,0:T(8,128)(2,1)S(1)} %get-tuple-element.249), channel_id=1, source_target_pairs={{0,8},{1,13},{2,10},{3,15},{4,12},{5,9},{6,14},{7,11},{8,0},{9,5},... | collective-permute-start | bytes 884744 | tf_op jit(solution)/shard_map/ppermute | solution.py:17
  138.0 10.9 %collective-permute-start.39 = (bf16[768,512]{1,0:T(8,128)(2,1)S(1)}, bf16[768,512]{1,0:T(8,128)(2,1)S(1)}, u32[]{:S(2)}, u32[]{:S(2)}) collective-permute-start(bf16[768,512]{1,0:T(8,128)(2,1)S(1)} %get-tuple-element.258), channel_id=1, source_target_pairs={{0,1},{1,0},{2,3},{3,2},{4,5},{5,4},{6,7},{7,6},{8,9},{9,8},{10,11... | collective-permute-start | bytes 2359304 | tf_op jit(solution)/shard_map/ppermute | solution.py:17
  (23 other events, 185.9 us)

commit v7 on v6

--- a/solution.py
+++ b/solution.py
@@ -446,6 +446,8 @@
     b_sum |= added(back0, order.wait(b0_far), near)
     order.done(b_sum[near[0]])
     b_near = hops(b_sum, near)
+    grad_down = joined_weights(down_own_part, order.wait(*down_sent))
+    order.done(grad_down)
     mixed = collect(
         index,
         routes,
@@ -455,8 +457,6 @@
         *sizes,
     )
     order.done(mixed)
-    grad_down = joined_weights(down_own_part, order.wait(*down_sent))
-    order.done(grad_down)
     b_home |= come(b_near)
     b_other = core(halves(b_home))
     grad_up = joined_weights(up_own_part, order.wait(*up_sent))

time: 153 us -> 153 us (level)
  no operation moved by 1% of the time
where the time goes in v7:
time: 153 us; the launch traced here: 152 us
  starting transfers between devices  68.4 us (45%)
  waiting for transfers between devices  51.3 us (34%)
  Pallas kernels  28.3 us (18%)
  local copies, waits for them, and re-layouts  3.28 us (2%)
    ppermute x41, starting transfers between devices, swap(): lax.ppermute(value, 'expert', [(i, i ^ bits ^ (odd_bits if i % 2 else 0))...  68.4 us
    ppermute x41, waiting for transfers between devices, swap(): lax.ppermute(value, 'expert', [(i, i ^ bits ^ (odd_bits if i % 2 else 0))...  51.3 us
    pallas_call x18, Pallas kernels, call(): pl.pallas_call(kernel, out_shape=[jax.ShapeDtypeStruct(shape, dtype) for...  23 us
    pallas_call x2, Pallas kernels, collect(): pl.pallas_call(functools.partial(collect_kernel, experts_all, capacity, b...  3.34 us
    unnamed x26, local copies, waits for them, and re-layouts  3.16 us
  transfers between devices with their start and end apart: 41, of which 14 were waited for; matrix products, arithmetic and copies ran while one was open for 0% of the time, Pallas kernels for 17%

profile of v7, /device:TPU:0, one launch (start us, length us, event | category | flops | bytes accessed | tf_op | source)
XLA Modules:
  0.0 152.4 jit_solution(16658378034172939580)
XLA Ops:
  6.7 3.0 %collective-permute-start.3 = (bf16[96,1536]{1,0:T(8,128)(2,1)S(1)}, bf16[96,1536]{1,0:T(8,128)(2,1)S(1)}, u32[]{:S(2)}, u32[]{:S(2)}) collective-permute-start(bf16[96,1536]{1,0:T(8,128)(2,1)S(1)} %get-tuple-element.139), channel_id=1, source_target_pairs={{0,8},{1,13},{2,10},{3,15},{4,12},{5,9},{6,14},{7,11},{8,0},{9,5},... | collective-permute-start | bytes 884744 | tf_op jit(solution)/shard_map/ppermute | solution.py:17
  9.7 2.6 %collective-permute-start.5 = (bf16[96,1536]{1,0:T(8,128)(2,1)S(1)}, bf16[96,1536]{1,0:T(8,128)(2,1)S(1)}, u32[]{:S(2)}, u32[]{:S(2)}) collective-permute-start(bf16[96,1536]{1,0:T(8,128)(2,1)S(1)} %get-tuple-element.144), channel_id=1, source_target_pairs={{0,16},{1,21},{2,18},{3,23},{4,20},{5,17},{6,22},{7,19},{8,24},{9,... | collective-permute-start | bytes 884744 | tf_op jit(solution)/shard_map/ppermute | solution.py:17
  12.3 8.8 %collective-permute-done.3 = bf16[96,1536]{1,0:T(8,128)(2,1)S(1)} collective-permute-done((bf16[96,1536]{1,0:T(8,128)(2,1)S(1)}, bf16[96,1536]{1,0:T(8,128)(2,1)S(1)}, u32[]{:S(2)}, u32[]{:S(2)}) %collective-permute-start.3) | collective-permute-done | bytes 294944 | tf_op jit(solution)/shard_map/ppermute | solution.py:17
  21.2 2.7 %collective-permute-start.4 = (bf16[192,1536]{1,0:T(8,128)(2,1)S(1)}, bf16[192,1536]{1,0:T(8,128)(2,1)S(1)}, u32[]{:S(2)}, u32[]{:S(2)}) collective-permute-start(bf16[192,1536]{1,0:T(8,128)(2,1)S(1)} %constant_dynamic-update-slice_fusion.mine.refs_0_), channel_id=1, source_target_pairs={{0,2},{1,3},{2,0},{3,1},{4,6},{5,7},{6,4},{7,5},{8,10},{9,11},{10,... | collective-permute-start | bytes 1769480 | tf_op jit(solution)/shard_map/ppermute | solution.py:17
  23.9 3.8 %collective-permute-start.8 = (bf16[32,6144]{1,0:T(8,128)(2,1)S(1)}, bf16[32,6144]{1,0:T(8,128)(2,1)S(1)}, u32[]{:S(2)}, u32[]{:S(2)}) collective-permute-start(bf16[32,6144]{1,0:T(8,128)(2,1)S(1)} %copy-done.7), channel_id=1, source_target_pairs={{0,1},{1,0},{2,3},{3,2},{4,5},{5,4},{6,7},{7,6},{8,9},{9,8},{10,11... | collective-permute-start | bytes 1179656 | tf_op jit(solution)/shard_map/ppermute | solution.py:17
  27.8 2.5 %collective-permute-start.11 = (bf16[96,1536]{1,0:T(8,128)(2,1)S(1)}, bf16[96,1536]{1,0:T(8,128)(2,1)S(1)}, u32[]{:S(2)}, u32[]{:S(2)}) collective-permute-start(bf16[96,1536]{1,0:T(8,128)(2,1)S(1)} %get-tuple-element.160), channel_id=1, source_target_pairs={{0,24},{1,29},{2,26},{3,31},{4,28},{5,25},{6,30},{7,27},{8,16},{9,... | collective-permute-start | bytes 884744 | tf_op jit(solution)/shard_map/ppermute | solution.py:17
  34.2 1.9 %collective-permute-done.4.far.refs_1_ = bf16[192,1536]{1,0:T(8,128)(2,1)S(1)} collective-permute-done((bf16[192,1536]{1,0:T(8,128)(2,1)S(1)}, bf16[192,1536]{1,0:T(8,128)(2,1)S(1)}, u32[]{:S(2)}, u32[]{:S(2)}) %collective-permute-start.4) | collective-permute-done | bytes 589856 | tf_op jit(solution)/shard_map/ppermute | solution.py:17
  36.1 2.7 %shard_map.95 = (f32[384,512]{1,0:T(8,128)S(1)}, f32[384,512]{1,0:T(8,128)S(1)}, bf16[384,512]{1,0:T(8,128)(2,1)S(1)}, bf16[384,512]{1,0:T(8,128)(2,1)S(1)}, bf1...) custom-call(bf16[192,1536]{1,0:T(8,128)(2,1)S(1)} %constant_dynamic-update-slice_fusion.mine.refs_0_, ...), custom_call_target="tpu_custom_call" | custom-call | flops 1 | bytes 1 | tf_op jit(solution)/shard_map/pallas_call | solution.py:205
  38.8 2.5 %collective-permute-start.10 = (bf16[192,1536]{1,0:T(8,128)(2,1)S(1)}, bf16[192,1536]{1,0:T(8,128)(2,1)S(1)}, u32[]{:S(2)}, u32[]{:S(2)}) collective-permute-start(bf16[192,1536]{1,0:T(8,128)(2,1)S(1)} %get-tuple-element.158), channel_id=1, source_target_pairs={{0,2},{1,3},{2,0},{3,1},{4,6},{5,7},{6,4},{7,5},{8,10},{9,11},{10,... | collective-permute-start | bytes 1769480 | tf_op jit(solution)/shard_map/ppermute | solution.py:17
  42.4 3.7 %collective-permute-start.17 = (bf16[96,1536]{1,0:T(8,128)(2,1)S(1)}, bf16[96,1536]{1,0:T(8,128)(2,1)S(1)}, u32[]{:S(2)}, u32[]{:S(2)}) collective-permute-start(bf16[96,1536]{1,0:T(8,128)(2,1)S(1)} %get-tuple-element.176), channel_id=1, source_target_pairs={{0,24},{1,29},{2,26},{3,31},{4,28},{5,25},{6,30},{7,27},{8,16},{9,... | collective-permute-start | bytes 884744 | tf_op jit(solution)/shard_map/ppermute | solution.py:17
  49.2 12.7 %collective-permute-done.12.far.refs_5_ = bf16[96,1536]{1,0:T(8,128)(2,1)S(1)} collective-permute-done((bf16[96,1536]{1,0:T(8,128)(2,1)S(1)}, bf16[96,1536]{1,0:T(8,128)(2,1)S(1)}, u32[]{:S(2)}, u32[]{:S(2)}) %collective-permute-start.12) | collective-permute-done | bytes 294944 | tf_op jit(solution)/shard_map/ppermute | solution.py:17
  63.4 2.0 %collective-permute-start.14 = (bf16[96,1536]{1,0:T(8,128)(2,1)S(1)}, bf16[96,1536]{1,0:T(8,128)(2,1)S(1)}, u32[]{:S(2)}, u32[]{:S(2)}) collective-permute-start(bf16[96,1536]{1,0:T(8,128)(2,1)S(1)} %get-tuple-element.171), channel_id=1, source_target_pairs={{0,2},{1,3},{2,0},{3,1},{4,6},{5,7},{6,4},{7,5},{8,10},{9,11},{10,... | collective-permute-start | bytes 884744 | tf_op jit(solution)/shard_map/ppermute | solution.py:17
  65.6 2.6 %collective-permute-done.16.far = bf16[96,1536]{1,0:T(8,128)(2,1)S(1)} collective-permute-done((bf16[96,1536]{1,0:T(8,128)(2,1)S(1)}, bf16[96,1536]{1,0:T(8,128)(2,1)S(1)}, u32[]{:S(2)}, u32[]{:S(2)}) %collective-permute-start.16) | collective-permute-done | bytes 294944 | tf_op jit(solution)/shard_map/ppermute | solution.py:17
  69.2 2.0 %collective-permute-start.19 = (bf16[96,1536]{1,0:T(8,128)(2,1)S(1)}, bf16[96,1536]{1,0:T(8,128)(2,1)S(1)}, u32[]{:S(2)}, u32[]{:S(2)}) collective-permute-start(bf16[96,1536]{1,0:T(8,128)(2,1)S(1)} %collective-permute-done.17.mine.refs_7_), channel_id=1, source_target_pairs={{0,2},{1,3},{2,0},{3,1},{4,6},{5,7},{6,4},{7,5},{8,10},{9,11},{10,... | collective-permute-start | bytes 884744 | tf_op jit(solution)/shard_map/ppermute | solution.py:17
  71.3 1.8 %collective-permute-done.15.mine.refs_5_ = bf16[96,1536]{1,0:T(8,128)(2,1)S(1)} collective-permute-done((bf16[96,1536]{1,0:T(8,128)(2,1)S(1)}, bf16[96,1536]{1,0:T(8,128)(2,1)S(1)}, u32[]{:S(2)}, u32[]{:S(2)}) %collective-permute-start.15) | collective-permute-done | bytes 294944 | tf_op jit(solution)/shard_map/ppermute | solution.py:17
  74.5 2.1 %collective-permute-start.24 = (bf16[96,1536]{1,0:T(8,128)(2,1)S(1)}, bf16[96,1536]{1,0:T(8,128)(2,1)S(1)}, u32[]{:S(2)}, u32[]{:S(2)}) collective-permute-start(bf16[96,1536]{1,0:T(8,128)(2,1)S(1)} %shard_map.99), channel_id=1, source_target_pairs={{0,16},{1,21},{2,18},{3,23},{4,20},{5,17},{6,22},{7,19},{8,24},{9,... | collective-permute-start | bytes 884744 | tf_op jit(solution)/shard_map/ppermute | solution.py:17
  76.7 4.1 %collective-permute-done.19.far.refs_8_ = bf16[96,1536]{1,0:T(8,128)(2,1)S(1)} collective-permute-done((bf16[96,1536]{1,0:T(8,128)(2,1)S(1)}, bf16[96,1536]{1,0:T(8,128)(2,1)S(1)}, u32[]{:S(2)}, u32[]{:S(2)}) %collective-permute-start.19) | collective-permute-done | bytes 294944 | tf_op jit(solution)/shard_map/ppermute | solution.py:17
  80.9 2.2 %shard_map.101 = (bf16[192,512]{1,0:T(8,128)(2,1)S(1)}, bf16[192,512]{1,0:T(8,128)(2,1)S(1)}, bf16[96,1536]{1,0:T(8,128)(2,1)S(1)}, bf16[96,1536]{1,0:T(8,128)(2,1)S(1)}) custom-call(bf16[96,1536]{1,0:T(8,128)(2,1)S(1)} %collective-permute-done.17.mine.refs_7_, bf16[96,1536]{1,0:T(8,128)(2,1)S(1)} %collective-permute-done.19.far.refs_8_, ...), custom_call_target="tpu_custom_call" | custom-call | flops 1 | bytes 1 | tf_op jit(solution)/shard_map/pallas_call | solution.py:205
  83.1 2.0 %collective-permute-start.22 = (bf16[96,1536]{1,0:T(8,128)(2,1)S(1)}, bf16[96,1536]{1,0:T(8,128)(2,1)S(1)}, u32[]{:S(2)}, u32[]{:S(2)}) collective-permute-start(bf16[96,1536]{1,0:T(8,128)(2,1)S(1)} %get-tuple-element.192), channel_id=1, source_target_pairs={{0,2},{1,3},{2,0},{3,1},{4,6},{5,7},{6,4},{7,5},{8,10},{9,11},{10,... | collective-permute-start | bytes 884744 | tf_op jit(solution)/shard_map/ppermute | solution.py:17
  85.3 3.2 %collective-permute-start.18 = (bf16[96,1536]{1,0:T(8,128)(2,1)S(1)}, bf16[96,1536]{1,0:T(8,128)(2,1)S(1)}, u32[]{:S(2)}, u32[]{:S(2)}) collective-permute-start(bf16[96,1536]{1,0:T(8,128)(2,1)S(1)} %shard_map.100), channel_id=1, source_target_pairs={{0,24},{1,29},{2,26},{3,31},{4,28},{5,25},{6,30},{7,27},{8,16},{9,... | collective-permute-start | bytes 884744 | tf_op jit(solution)/shard_map/ppermute | solution.py:17
  90.3 2.2 %shard_map.102 = (bf16[192,512]{1,0:T(8,128)(2,1)S(1)}, bf16[192,512]{1,0:T(8,128)(2,1)S(1)}, bf16[96,1536]{1,0:T(8,128)(2,1)S(1)}, bf16[96,1536]{1,0:T(8,128)(2,1)S(1)}) custom-call(bf16[96,1536]{1,0:T(8,128)(2,1)S(1)} %collective-permute-done.15.mine.refs_5_, bf16[96,1536]{1,0:T(8,128)(2,1)S(1)} %collective-permute-done.23.far.refs_6_, ...), custom_call_target="tpu_custom_call" | custom-call | flops 1 | bytes 1 | tf_op jit(solution)/shard_map/pallas_call | solution.py:205
  92.5 2.3 %collective-permute-start.27 = (bf16[96,1536]{1,0:T(8,128)(2,1)S(1)}, bf16[96,1536]{1,0:T(8,128)(2,1)S(1)}, u32[]{:S(2)}, u32[]{:S(2)}) collective-permute-start(bf16[96,1536]{1,0:T(8,128)(2,1)S(1)} %get-tuple-element.207), channel_id=1, source_target_pairs={{0,2},{1,3},{2,0},{3,1},{4,6},{5,7},{6,4},{7,5},{8,10},{9,11},{10,... | collective-permute-start | bytes 884744 | tf_op jit(solution)/shard_map/ppermute | solution.py:17
  94.9 9.9 %collective-permute-start.29 = (bf16[96,1536]{1,0:T(8,128)(2,1)S(1)}, bf16[96,1536]{1,0:T(8,128)(2,1)S(1)}, u32[]{:S(2)}, u32[]{:S(2)}) collective-permute-start(bf16[96,1536]{1,0:T(8,128)(2,1)S(1)} %shard_map.103), channel_id=1, source_target_pairs={{0,24},{1,29},{2,26},{3,31},{4,28},{5,25},{6,30},{7,27},{8,16},{9,... | collective-permute-start | bytes 884744 | tf_op jit(solution)/shard_map/ppermute | solution.py:17
  104.9 7.6 %collective-permute-done.27.far = bf16[96,1536]{1,0:T(8,128)(2,1)S(1)} collective-permute-done((bf16[96,1536]{1,0:T(8,128)(2,1)S(1)}, bf16[96,1536]{1,0:T(8,128)(2,1)S(1)}, u32[]{:S(2)}, u32[]{:S(2)}) %collective-permute-start.27) | collective-permute-done | bytes 294944 | tf_op jit(solution)/shard_map/ppermute | solution.py:17
  112.6 2.8 %shard_map.105 = (bf16[384,512]{1,0:T(8,128)(2,1)S(1)}, bf16[384,512]{1,0:T(8,128)(2,1)S(1)}, bf16[192,1536]{1,0:T(8,128)(2,1)S(1)}, bf16[192,1536]{1,0:T(8,128)(2,1)S(1)}) custom-call(bf16[192,1536]{1,0:T(8,128)(2,1)S(1)} %constant_dynamic-update-slice_fusion.2.mine.refs_3_, bf16[192,1536]{1,0:T(8,128)(2,1)S(1)} %collective-permute-done.30.far.refs_4_, ...), custom_call_target="tpu_custom_call" | custom-call | flops 1 | bytes 1 | tf_op jit(solution)/shard_map/pallas_call | solution.py:205
  116.7 3.6 %collective-permute-start.28 = (bf16[96,1536]{1,0:T(8,128)(2,1)S(1)}, bf16[96,1536]{1,0:T(8,128)(2,1)S(1)}, u32[]{:S(2)}, u32[]{:S(2)}) collective-permute-start(bf16[96,1536]{1,0:T(8,128)(2,1)S(1)} %shard_map.104), channel_id=1, source_target_pairs={{0,16},{1,21},{2,18},{3,23},{4,20},{5,17},{6,22},{7,19},{8,24},{9,... | collective-permute-start | bytes 884744 | tf_op jit(solution)/shard_map/ppermute | solution.py:17
  128.3 2.7 %collective-permute-start.33 = (bf16[256,1536]{1,0:T(8,128)(2,1)S(1)}, bf16[256,1536]{1,0:T(8,128)(2,1)S(1)}, u32[]{:S(2)}, u32[]{:S(2)}) collective-permute-start(bf16[256,1536]{1,0:T(8,128)(2,1)S(1)} %get-tuple-element.242), channel_id=1, source_target_pairs={{0,1},{1,0},{2,3},{3,2},{4,5},{5,4},{6,7},{7,6},{8,9},{9,8},{10,11... | collective-permute-start | bytes 2359304 | tf_op jit(solution)/shard_map/ppermute | solution.py:17
  131.1 3.2 %collective-permute-done.28.refs_2_ = bf16[96,1536]{1,0:T(8,128)(2,1)S(1)} collective-permute-done((bf16[96,1536]{1,0:T(8,128)(2,1)S(1)}, bf16[96,1536]{1,0:T(8,128)(2,1)S(1)}, u32[]{:S(2)}, u32[]{:S(2)}) %collective-permute-start.28) | collective-permute-done | bytes 294944 | tf_op jit(solution)/shard_map/ppermute | solution.py:17
  138.0 2.7 %collective-permute-start.39 = (bf16[768,512]{1,0:T(8,128)(2,1)S(1)}, bf16[768,512]{1,0:T(8,128)(2,1)S(1)}, u32[]{:S(2)}, u32[]{:S(2)}) collective-permute-start(bf16[768,512]{1,0:T(8,128)(2,1)S(1)} %get-tuple-element.258), channel_id=1, source_target_pairs={{0,1},{1,0},{2,3},{3,2},{4,5},{5,4},{6,7},{7,6},{8,9},{9,8},{10,11... | collective-permute-start | bytes 2359304 | tf_op jit(solution)/shard_map/ppermute | solution.py:17
  140.8 1.9 %shard_map.111 = f32[512,1536]{1,0:T(8,128)} custom-call(f32[512,1536]{1,0:T(8,128)S(1)} %shard_map.108.own, bf16[256,1536]{1,0:T(8,128)(2,1)S(1)} %collective-permute-done.33.refs_0_, bf16[256,1536]{1,0:T(8,128)(2,1)S(1)} %collective-permute-done.34.refs_1_), custom_call_target="tpu_custom_call" | custom-call | flops 1 | bytes 1 | tf_op jit(solution)/shard_map/pallas_call | solution.py:205
  145.9 3.0 %collective-permute-start.38 = (bf16[192,1536]{1,0:T(8,128)(2,1)S(1)}, bf16[192,1536]{1,0:T(8,128)(2,1)S(1)}, u32[]{:S(2)}, u32[]{:S(2)}) collective-permute-start(bf16[192,1536]{1,0:T(8,128)(2,1)S(1)} %pad_maximum_fusion), channel_id=1, source_target_pairs={{0,1},{1,0},{2,3},{3,2},{4,5},{5,4},{6,7},{7,6},{8,9},{9,8},{10,11... | collective-permute-start | bytes 1769480 | tf_op jit(solution)/shard_map/ppermute | solution.py:17
  148.9 1.9 %shard_map.113 = f32[1536,512]{1,0:T(8,128)} custom-call(f32[1536,512]{1,0:T(8,128)S(1)} %shard_map.109.own, bf16[768,512]{1,0:T(8,128)(2,1)S(1)} %collective-permute-done.39.refs_0_, bf16[768,512]{1,0:T(8,128)(2,1)S(1)} %collective-permute-done.40.refs_1_), custom_call_target="tpu_custom_call" | custom-call | flops 1 | bytes 1 | tf_op jit(solution)/shard_map/pallas_call | solution.py:205
  (113 shorter events, 38.3 us)
Async XLA Ops:
  5.4 18.5 %collective-permute-start.6 = (bf16[1536,512]{1,0:T(8,128)(2,1)}, bf16[1536,512]{1,0:T(8,128)(2,1)S(1)}, u32[]{:S(2)}, u32[]{:S(2)}) collective-permute-start(bf16[1536,512]{1,0:T(8,128)(2,1)} %bitcast.7), channel_id=1, source_target_pairs={{0,1},{1,0},{2,3},{3,2},{4,5},{5,4},{6,7},{7,6},{8,9},{9,8},{10,11... | collective-permute-start | bytes 4718600 | tf_op jit(solution)/shard_map/ppermute | solution.py:17
  5.9 18.0 %collective-permute-start.7 = (bf16[512,1536]{1,0:T(8,128)(2,1)}, bf16[512,1536]{1,0:T(8,128)(2,1)S(1)}, u32[]{:S(2)}, u32[]{:S(2)}) collective-permute-start(bf16[512,1536]{1,0:T(8,128)(2,1)} %bitcast.15), channel_id=1, source_target_pairs={{0,1},{1,0},{2,3},{3,2},{4,5},{5,4},{6,7},{7,6},{8,9},{9,8},{10,11... | collective-permute-start | bytes 4718600 | tf_op jit(solution)/shard_map/ppermute | solution.py:17
  6.7 14.4 %collective-permute-start.3 = (bf16[96,1536]{1,0:T(8,128)(2,1)S(1)}, bf16[96,1536]{1,0:T(8,128)(2,1)S(1)}, u32[]{:S(2)}, u32[]{:S(2)}) collective-permute-start(bf16[96,1536]{1,0:T(8,128)(2,1)S(1)} %get-tuple-element.139), channel_id=1, source_target_pairs={{0,8},{1,13},{2,10},{3,15},{4,12},{5,9},{6,14},{7,11},{8,0},{9,5},... | collective-permute-start | bytes 884744 | tf_op jit(solution)/shard_map/ppermute | solution.py:17
  9.7 14.2 %collective-permute-start.5 = (bf16[96,1536]{1,0:T(8,128)(2,1)S(1)}, bf16[96,1536]{1,0:T(8,128)(2,1)S(1)}, u32[]{:S(2)}, u32[]{:S(2)}) collective-permute-start(bf16[96,1536]{1,0:T(8,128)(2,1)S(1)} %get-tuple-element.144), channel_id=1, source_target_pairs={{0,16},{1,21},{2,18},{3,23},{4,20},{5,17},{6,22},{7,19},{8,24},{9,... | collective-permute-start | bytes 884744 | tf_op jit(solution)/shard_map/ppermute | solution.py:17
  21.2 15.0 %collective-permute-start.4 = (bf16[192,1536]{1,0:T(8,128)(2,1)S(1)}, bf16[192,1536]{1,0:T(8,128)(2,1)S(1)}, u32[]{:S(2)}, u32[]{:S(2)}) collective-permute-start(bf16[192,1536]{1,0:T(8,128)(2,1)S(1)} %constant_dynamic-update-slice_fusion.mine.refs_0_), channel_id=1, source_target_pairs={{0,2},{1,3},{2,0},{3,1},{4,6},{5,7},{6,4},{7,5},{8,10},{9,11},{10,... | collective-permute-start | bytes 1769480 | tf_op jit(solution)/shard_map/ppermute | solution.py:17
  23.9 7.8 %collective-permute-start.8 = (bf16[32,6144]{1,0:T(8,128)(2,1)S(1)}, bf16[32,6144]{1,0:T(8,128)(2,1)S(1)}, u32[]{:S(2)}, u32[]{:S(2)}) collective-permute-start(bf16[32,6144]{1,0:T(8,128)(2,1)S(1)} %copy-done.7), channel_id=1, source_target_pairs={{0,1},{1,0},{2,3},{3,2},{4,5},{5,4},{6,7},{7,6},{8,9},{9,8},{10,11... | collective-permute-start | bytes 1179656 | tf_op jit(solution)/shard_map/ppermute | solution.py:17
  27.8 13.6 %collective-permute-start.11 = (bf16[96,1536]{1,0:T(8,128)(2,1)S(1)}, bf16[96,1536]{1,0:T(8,128)(2,1)S(1)}, u32[]{:S(2)}, u32[]{:S(2)}) collective-permute-start(bf16[96,1536]{1,0:T(8,128)(2,1)S(1)} %get-tuple-element.160), channel_id=1, source_target_pairs={{0,24},{1,29},{2,26},{3,31},{4,28},{5,25},{6,30},{7,27},{8,16},{9,... | collective-permute-start | bytes 884744 | tf_op jit(solution)/shard_map/ppermute | solution.py:17
  30.3 12.2 %collective-permute-start.13 = (bf16[96,1536]{1,0:T(8,128)(2,1)S(1)}, bf16[96,1536]{1,0:T(8,128)(2,1)S(1)}, u32[]{:S(2)}, u32[]{:S(2)}) collective-permute-start(bf16[96,1536]{1,0:T(8,128)(2,1)S(1)} %collective-permute-done.5.mine.refs_2_), channel_id=1, source_target_pairs={{0,2},{1,3},{2,0},{3,1},{4,6},{5,7},{6,4},{7,5},{8,10},{9,11},{10,... | collective-permute-start | bytes 884744 | tf_op jit(solution)/shard_map/ppermute | solution.py:17
  38.8 26.7 %collective-permute-start.10 = (bf16[192,1536]{1,0:T(8,128)(2,1)S(1)}, bf16[192,1536]{1,0:T(8,128)(2,1)S(1)}, u32[]{:S(2)}, u32[]{:S(2)}) collective-permute-start(bf16[192,1536]{1,0:T(8,128)(2,1)S(1)} %get-tuple-element.158), channel_id=1, source_target_pairs={{0,2},{1,3},{2,0},{3,1},{4,6},{5,7},{6,4},{7,5},{8,10},{9,11},{10,... | collective-permute-start | bytes 1769480 | tf_op jit(solution)/shard_map/ppermute | solution.py:17
  41.3 20.6 %collective-permute-start.12 = (bf16[96,1536]{1,0:T(8,128)(2,1)S(1)}, bf16[96,1536]{1,0:T(8,128)(2,1)S(1)}, u32[]{:S(2)}, u32[]{:S(2)}) collective-permute-start(bf16[96,1536]{1,0:T(8,128)(2,1)S(1)} %collective-permute-done.11.mine.refs_4_), channel_id=1, source_target_pairs={{0,2},{1,3},{2,0},{3,1},{4,6},{5,7},{6,4},{7,5},{8,10},{9,11},{10,... | collective-permute-start | bytes 884744 | tf_op jit(solution)/shard_map/ppermute | solution.py:17
  42.4 23.2 %collective-permute-start.17 = (bf16[96,1536]{1,0:T(8,128)(2,1)S(1)}, bf16[96,1536]{1,0:T(8,128)(2,1)S(1)}, u32[]{:S(2)}, u32[]{:S(2)}) collective-permute-start(bf16[96,1536]{1,0:T(8,128)(2,1)S(1)} %get-tuple-element.176), channel_id=1, source_target_pairs={{0,24},{1,29},{2,26},{3,31},{4,28},{5,25},{6,30},{7,27},{8,16},{9,... | collective-permute-start | bytes 884744 | tf_op jit(solution)/shard_map/ppermute | solution.py:17
  47.7 20.6 %collective-permute-start.16 = (bf16[96,1536]{1,0:T(8,128)(2,1)S(1)}, bf16[96,1536]{1,0:T(8,128)(2,1)S(1)}, u32[]{:S(2)}, u32[]{:S(2)}) collective-permute-start(bf16[96,1536]{1,0:T(8,128)(2,1)S(1)} %get-tuple-element.174), channel_id=1, source_target_pairs={{0,2},{1,3},{2,0},{3,1},{4,6},{5,7},{6,4},{7,5},{8,10},{9,11},{10,... | collective-permute-start | bytes 884744 | tf_op jit(solution)/shard_map/ppermute | solution.py:17
  49.2 23.9 %collective-permute-start.15 = (bf16[96,1536]{1,0:T(8,128)(2,1)S(1)}, bf16[96,1536]{1,0:T(8,128)(2,1)S(1)}, u32[]{:S(2)}, u32[]{:S(2)}) collective-permute-start(bf16[96,1536]{1,0:T(8,128)(2,1)S(1)} %get-tuple-element.173), channel_id=1, source_target_pairs={{0,16},{1,21},{2,18},{3,23},{4,20},{5,17},{6,22},{7,19},{8,24},{9,... | collective-permute-start | bytes 884744 | tf_op jit(solution)/shard_map/ppermute | solution.py:17
  63.4 11.1 %collective-permute-start.14 = (bf16[96,1536]{1,0:T(8,128)(2,1)S(1)}, bf16[96,1536]{1,0:T(8,128)(2,1)S(1)}, u32[]{:S(2)}, u32[]{:S(2)}) collective-permute-start(bf16[96,1536]{1,0:T(8,128)(2,1)S(1)} %get-tuple-element.171), channel_id=1, source_target_pairs={{0,2},{1,3},{2,0},{3,1},{4,6},{5,7},{6,4},{7,5},{8,10},{9,11},{10,... | collective-permute-start | bytes 884744 | tf_op jit(solution)/shard_map/ppermute | solution.py:17
  68.3 8.4 %collective-permute-start.20 = (bf16[96,1536]{1,0:T(8,128)(2,1)S(1)}, bf16[96,1536]{1,0:T(8,128)(2,1)S(1)}, u32[]{:S(2)}, u32[]{:S(2)}) collective-permute-start(bf16[96,1536]{1,0:T(8,128)(2,1)S(1)} %get-tuple-element.184), channel_id=1, source_target_pairs={{0,0},{1,5},{2,2},{3,7},{4,4},{5,1},{6,6},{7,3},{8,8},{9,13},{10,1... | collective-permute-start | bytes 884744 | tf_op jit(solution)/shard_map/ppermute | solution.py:17
  69.2 11.6 %collective-permute-start.19 = (bf16[96,1536]{1,0:T(8,128)(2,1)S(1)}, bf16[96,1536]{1,0:T(8,128)(2,1)S(1)}, u32[]{:S(2)}, u32[]{:S(2)}) collective-permute-start(bf16[96,1536]{1,0:T(8,128)(2,1)S(1)} %collective-permute-done.17.mine.refs_7_), channel_id=1, source_target_pairs={{0,2},{1,3},{2,0},{3,1},{4,6},{5,7},{6,4},{7,5},{8,10},{9,11},{10,... | collective-permute-start | bytes 884744 | tf_op jit(solution)/shard_map/ppermute | solution.py:17
  73.1 17.2 %collective-permute-start.23 = (bf16[96,1536]{1,0:T(8,128)(2,1)S(1)}, bf16[96,1536]{1,0:T(8,128)(2,1)S(1)}, u32[]{:S(2)}, u32[]{:S(2)}) collective-permute-start(bf16[96,1536]{1,0:T(8,128)(2,1)S(1)} %collective-permute-done.15.mine.refs_5_), channel_id=1, source_target_pairs={{0,2},{1,3},{2,0},{3,1},{4,6},{5,7},{6,4},{7,5},{8,10},{9,11},{10,... | collective-permute-start | bytes 884744 | tf_op jit(solution)/shard_map/ppermute | solution.py:17
  74.5 15.7 %collective-permute-start.24 = (bf16[96,1536]{1,0:T(8,128)(2,1)S(1)}, bf16[96,1536]{1,0:T(8,128)(2,1)S(1)}, u32[]{:S(2)}, u32[]{:S(2)}) collective-permute-start(bf16[96,1536]{1,0:T(8,128)(2,1)S(1)} %shard_map.99), channel_id=1, source_target_pairs={{0,16},{1,21},{2,18},{3,23},{4,20},{5,17},{6,22},{7,19},{8,24},{9,... | collective-permute-start | bytes 884744 | tf_op jit(solution)/shard_map/ppermute | solution.py:17
  83.1 11.7 %collective-permute-start.22 = (bf16[96,1536]{1,0:T(8,128)(2,1)S(1)}, bf16[96,1536]{1,0:T(8,128)(2,1)S(1)}, u32[]{:S(2)}, u32[]{:S(2)}) collective-permute-start(bf16[96,1536]{1,0:T(8,128)(2,1)S(1)} %get-tuple-element.192), channel_id=1, source_target_pairs={{0,2},{1,3},{2,0},{3,1},{4,6},{5,7},{6,4},{7,5},{8,10},{9,11},{10,... | collective-permute-start | bytes 884744 | tf_op jit(solution)/shard_map/ppermute | solution.py:17
  85.2 27.4 %collective-permute-start.30 = (bf16[192,1536]{1,0:T(8,128)(2,1)S(1)}, bf16[192,1536]{1,0:T(8,128)(2,1)S(1)}, u32[]{:S(2)}, u32[]{:S(2)}) collective-permute-start(bf16[192,1536]{1,0:T(8,128)(2,1)S(1)} %constant_dynamic-update-slice_fusion.2.mine.refs_3_), channel_id=1, source_target_pairs={{0,2},{1,3},{2,0},{3,1},{4,6},{5,7},{6,4},{7,5},{8,10},{9,11},{10,... | collective-permute-start | bytes 1769480 | tf_op jit(solution)/shard_map/ppermute | solution.py:17
  85.3 19.6 %collective-permute-start.18 = (bf16[96,1536]{1,0:T(8,128)(2,1)S(1)}, bf16[96,1536]{1,0:T(8,128)(2,1)S(1)}, u32[]{:S(2)}, u32[]{:S(2)}) collective-permute-start(bf16[96,1536]{1,0:T(8,128)(2,1)S(1)} %shard_map.100), channel_id=1, source_target_pairs={{0,24},{1,29},{2,26},{3,31},{4,28},{5,25},{6,30},{7,27},{8,16},{9,... | collective-permute-start | bytes 884744 | tf_op jit(solution)/shard_map/ppermute | solution.py:17
  92.5 19.9 %collective-permute-start.27 = (bf16[96,1536]{1,0:T(8,128)(2,1)S(1)}, bf16[96,1536]{1,0:T(8,128)(2,1)S(1)}, u32[]{:S(2)}, u32[]{:S(2)}) collective-permute-start(bf16[96,1536]{1,0:T(8,128)(2,1)S(1)} %get-tuple-element.207), channel_id=1, source_target_pairs={{0,2},{1,3},{2,0},{3,1},{4,6},{5,7},{6,4},{7,5},{8,10},{9,11},{10,... | collective-permute-start | bytes 884744 | tf_op jit(solution)/shard_map/ppermute | solution.py:17
  94.9 20.5 %collective-permute-start.29 = (bf16[96,1536]{1,0:T(8,128)(2,1)S(1)}, bf16[96,1536]{1,0:T(8,128)(2,1)S(1)}, u32[]{:S(2)}, u32[]{:S(2)}) collective-permute-start(bf16[96,1536]{1,0:T(8,128)(2,1)S(1)} %shard_map.103), channel_id=1, source_target_pairs={{0,24},{1,29},{2,26},{3,31},{4,28},{5,25},{6,30},{7,27},{8,16},{9,... | collective-permute-start | bytes 884744 | tf_op jit(solution)/shard_map/ppermute | solution.py:17
  116.7 17.6 %collective-permute-start.28 = (bf16[96,1536]{1,0:T(8,128)(2,1)S(1)}, bf16[96,1536]{1,0:T(8,128)(2,1)S(1)}, u32[]{:S(2)}, u32[]{:S(2)}) collective-permute-start(bf16[96,1536]{1,0:T(8,128)(2,1)S(1)} %shard_map.104), channel_id=1, source_target_pairs={{0,16},{1,21},{2,18},{3,23},{4,20},{5,17},{6,22},{7,19},{8,24},{9,... | collective-permute-start | bytes 884744 | tf_op jit(solution)/shard_map/ppermute | solution.py:17
  120.3 16.4 %collective-permute-start.35 = (bf16[192,1536]{1,0:T(8,128)(2,1)S(1)}, bf16[192,1536]{1,0:T(8,128)(2,1)S(1)}, u32[]{:S(2)}, u32[]{:S(2)}) collective-permute-start(bf16[192,1536]{1,0:T(8,128)(2,1)S(1)} %get-tuple-element.245), channel_id=1, source_target_pairs={{0,2},{1,3},{2,0},{3,1},{4,6},{5,7},{6,4},{7,5},{8,10},{9,11},{10,... | collective-permute-start | bytes 1769480 | tf_op jit(solution)/shard_map/ppermute | solution.py:17
  121.8 12.5 %collective-permute-start.25 = (bf16[96,1536]{1,0:T(8,128)(2,1)S(1)}, bf16[96,1536]{1,0:T(8,128)(2,1)S(1)}, u32[]{:S(2)}, u32[]{:S(2)}) collective-permute-start(bf16[96,1536]{1,0:T(8,128)(2,1)S(1)} %get-tuple-element.203), channel_id=1, source_target_pairs={{0,0},{1,5},{2,2},{3,7},{4,4},{5,1},{6,6},{7,3},{8,8},{9,13},{10,1... | collective-permute-start | bytes 884744 | tf_op jit(solution)/shard_map/ppermute | solution.py:17
  122.5 13.2 %collective-permute-start.26 = (bf16[96,1536]{1,0:T(8,128)(2,1)S(1)}, bf16[96,1536]{1,0:T(8,128)(2,1)S(1)}, u32[]{:S(2)}, u32[]{:S(2)}) collective-permute-start(bf16[96,1536]{1,0:T(8,128)(2,1)S(1)} %get-tuple-element.205), channel_id=1, source_target_pairs={{0,8},{1,13},{2,10},{3,15},{4,12},{5,9},{6,14},{7,11},{8,0},{9,5},... | collective-permute-start | bytes 884744 | tf_op jit(solution)/shard_map/ppermute | solution.py:17
  128.3 9.6 %collective-permute-start.33 = (bf16[256,1536]{1,0:T(8,128)(2,1)S(1)}, bf16[256,1536]{1,0:T(8,128)(2,1)S(1)}, u32[]{:S(2)}, u32[]{:S(2)}) collective-permute-start(bf16[256,1536]{1,0:T(8,128)(2,1)S(1)} %get-tuple-element.242), channel_id=1, source_target_pairs={{0,1},{1,0},{2,3},{3,2},{4,5},{5,4},{6,7},{7,6},{8,9},{9,8},{10,11... | collective-permute-start | bytes 2359304 | tf_op jit(solution)/shard_map/ppermute | solution.py:17
  136.9 7.6 %collective-permute-start.36 = (bf16[96,1536]{1,0:T(8,128)(2,1)S(1)}, bf16[96,1536]{1,0:T(8,128)(2,1)S(1)}, u32[]{:S(2)}, u32[]{:S(2)}) collective-permute-start(bf16[96,1536]{1,0:T(8,128)(2,1)S(1)} %get-tuple-element.252), channel_id=1, source_target_pairs={{0,0},{1,5},{2,2},{3,7},{4,4},{5,1},{6,6},{7,3},{8,8},{9,13},{10,1... | collective-permute-start | bytes 884744 | tf_op jit(solution)/shard_map/ppermute | solution.py:17
  137.6 8.2 %collective-permute-start.37 = (bf16[96,1536]{1,0:T(8,128)(2,1)S(1)}, bf16[96,1536]{1,0:T(8,128)(2,1)S(1)}, u32[]{:S(2)}, u32[]{:S(2)}) collective-permute-start(bf16[96,1536]{1,0:T(8,128)(2,1)S(1)} %get-tuple-element.254), channel_id=1, source_target_pairs={{0,8},{1,13},{2,10},{3,15},{4,12},{5,9},{6,14},{7,11},{8,0},{9,5},... | collective-permute-start | bytes 884744 | tf_op jit(solution)/shard_map/ppermute | solution.py:17
  138.0 10.9 %collective-permute-start.39 = (bf16[768,512]{1,0:T(8,128)(2,1)S(1)}, bf16[768,512]{1,0:T(8,128)(2,1)S(1)}, u32[]{:S(2)}, u32[]{:S(2)}) collective-permute-start(bf16[768,512]{1,0:T(8,128)(2,1)S(1)} %get-tuple-element.258), channel_id=1, source_target_pairs={{0,1},{1,0},{2,3},{3,2},{4,5},{5,4},{6,7},{7,6},{8,9},{9,8},{10,11... | collective-permute-start | bytes 2359304 | tf_op jit(solution)/shard_map/ppermute | solution.py:17
  140.7 8.2 %collective-permute-start.40 = (bf16[768,512]{1,0:T(8,128)(2,1)S(1)}, bf16[768,512]{1,0:T(8,128)(2,1)S(1)}, u32[]{:S(2)}, u32[]{:S(2)}) collective-permute-start(bf16[768,512]{1,0:T(8,128)(2,1)S(1)} %get-tuple-element.260), channel_id=1, source_target_pairs={{0,1},{1,0},{2,3},{3,2},{4,5},{5,4},{6,7},{7,6},{8,9},{9,8},{10,11... | collective-permute-start | bytes 2359304 | tf_op jit(solution)/shard_map/ppermute | solution.py:17
  (23 other events, 182.6 us)
